TPU v7x, 32 devices: a whole 2x2x4 slice. The times are simulated.
32 devices in a mesh: groups: 2 (over x), branch: 16 (over z, y, core).
Axes of the slice: x: 2, y: 2, z: 4, core: 2. Of those that a mesh axis runs over, the one named last changes fastest.
Arguments:
- prompt_k: bfloat16 [32, 1024, 1024], P(('groups', 'branch')), parts along dimension 0, may hold values from -6 to 6
- prompt_v: bfloat16 [32, 1024, 1024], P(('groups', 'branch')), parts along dimension 0, may hold values from -6 to 6
- prompt_mask: int32 [32, 8], P(('groups', 'branch')), parts along dimension 0, may hold values from 0 to 1, as said below
- shared_kv: bfloat16 [64, 24, 2048], P(('groups', 'branch')), parts along dimension 0, may hold values from -6 to 6
- shared_len: int32 [64], P(('groups', 'branch')), parts along dimension 0, may hold values from 1 to 24, 400 in all
- send_pick: int32 [32, 16], P(('groups', 'branch')), parts along dimension 0, may hold values from -1 to 1, as said below
- unique_q: bfloat16 [512, 8192], P(('groups', 'branch')), parts along dimension 0, may hold values from -132 to 132
- unique_kv: bfloat16 [512, 2048], P(('groups', 'branch')), parts along dimension 0, may hold values from -6.5 to 6.5
- unique_owner: int32 [512, 1], P(('groups', 'branch')), parts along dimension 0, may hold values from 0 to 15; in each aligned block of 16 rows (0 to 15, 16 to 31, ...) at most 2 rows name the same one
Outputs:
- attended: bfloat16 [512, 8192], P(('groups', 'branch')), parts along dimension 0
There are 2 independent parts, one for each index of `groups`. A program takes and returns all parts, laid end to end along the dimension named above; each array names one. Nothing has to cross between parts.
Inputs may be any that keep to these rules, and one draw needn't show every extreme that they name: `prompt_mask`: block 0 of every branch's prompt is visible. `send_pick`: entry [s, b] names which of owner s's 2 results branch b subscribes to, or -1 for none; every branch subscribes to exactly 12 results, at most one of each owner. `unique_owner`: among the rows of one source, no branch is named by more than 2 rows.
All inputs are finite; a program needn't handle non-finite values. No bound on the sum of `shared_len` on one device may be relied on, other than what follows from the above.
Results may differ from a plain program's by a relative error of at most 0.0027.
Values may be sent and summed in bfloat16 or wider, within the bound.
No kernel may reach another device: no remote copies, remote signals or barrier semaphores. Data moves between devices by JAX's collectives and lax.ppermute only.
A program may use at most 128 MiB of HBM per device.

v0:
```python
import math

import jax
import jax.numpy as jnp
from jax import lax
from jax.sharding import PartitionSpec as P

QH = 64
KVH = 8
HD = 128
GRP = 8


def attend(queries, key_rows, value_rows, allowed):
    count = queries.shape[0]
    keys_total = key_rows.shape[0]
    grouped = queries.reshape(count, KVH, GRP, HD).transpose(1, 2, 0, 3)
    key_heads = key_rows.reshape(keys_total, KVH, HD).transpose(1, 0, 2)
    value_heads = value_rows.reshape(keys_total, KVH, HD).transpose(1, 0, 2)
    scale = 1.0 / math.sqrt(HD)

    def one_head(operands):
        query_group, key_group, value_group = operands
        scores = (
            jnp.einsum("gsd,kd->gsk", query_group, key_group, preferred_element_type=jnp.float32)
            * scale
        )
        scores = jnp.where(allowed[None], scores, -1e30)
        largest = jnp.max(scores, axis=-1, keepdims=True)
        weights = jnp.exp(scores - largest)
        total = jnp.sum(weights, axis=-1, keepdims=True)
        probs = weights.astype(jnp.bfloat16)
        mixed = jnp.einsum("gsk,kd->gsd", probs, value_group, preferred_element_type=jnp.float32)
        return (mixed / total).astype(jnp.bfloat16)

    heads = lax.map(one_head, (grouped, key_heads, value_heads))
    return heads.transpose(2, 0, 1, 3).reshape(count, QH * HD)


def select(stack, lengths, picked):
    chosen = jnp.zeros((picked.shape[0],) + stack.shape[2:], jnp.bfloat16)
    live_len = jnp.zeros(picked.shape, jnp.int32)
    for which in range(stack.shape[1]):
        match = picked == which
        chosen = jnp.where(match[:, None, None], stack[:, which], chosen)
        live_len = jnp.where(match, lengths[:, which], live_len)
    return (chosen, live_len)


def body(
    prompt_k,
    prompt_v,
    prompt_mask,
    shared_kv,
    shared_len,
    send_pick,
    unique_q,
    unique_kv,
    unique_owner,
):
    branches = lax.axis_size("branch")
    row_count = unique_q.shape[0]
    capacity = 2 * row_count // branches
    width = branches * capacity
    kv_width = unique_kv.shape[1] // 2
    result_rows = shared_kv.shape[1]
    owner_of = unique_owner[:, 0]
    in_device = jnp.arange(row_count, dtype=jnp.int32)
    earlier = (owner_of[:, None] == owner_of[None, :]) & (in_device[None, :] < in_device[:, None])
    slot_index = owner_of * capacity + jnp.sum(earlier.astype(jnp.int32), axis=1)
    matches = jnp.arange(width, dtype=jnp.int32)[:, None] == slot_index[None, :]
    placing = matches.astype(jnp.bfloat16)
    send_q = (
        jnp.dot(placing, unique_q, preferred_element_type=jnp.float32)
        .astype(jnp.bfloat16)
        .reshape(branches, capacity, -1)
    )
    send_pairs = (
        jnp.dot(placing, unique_kv, preferred_element_type=jnp.float32)
        .astype(jnp.bfloat16)
        .reshape(branches, capacity, -1)
    )
    send_live = jnp.any(matches, axis=1).astype(jnp.int32).reshape(branches, capacity)
    recv_q, recv_pairs, recv_live = (
        lax.all_to_all(send_q, "branch", split_axis=0, concat_axis=0, tiled=True),
        lax.all_to_all(send_pairs, "branch", split_axis=0, concat_axis=0, tiled=True),
        lax.all_to_all(send_live, "branch", split_axis=0, concat_axis=0, tiled=True),
    )
    outgoing, outgoing_len = select(shared_kv[None], shared_len[None], send_pick[0])
    fetched, live_len = (
        lax.all_to_all(outgoing, "branch", split_axis=0, concat_axis=0, tiled=True),
        lax.all_to_all(outgoing_len, "branch", split_axis=0, concat_axis=0, tiled=True),
    )
    queries = recv_q.reshape(width, -1)
    pairs = recv_pairs.reshape(width, -1)
    slot_live = recv_live.reshape(width) > 0
    fetched_rows = fetched.reshape(branches * result_rows, 2 * kv_width)
    shared_ok = (jnp.arange(result_rows, dtype=jnp.int32)[None, :] < live_len[:, None]).reshape(
        branches * result_rows
    )
    block_size = prompt_k.shape[1] // prompt_mask.shape[1]
    block_ok = jnp.repeat(prompt_mask[0] > 0, block_size)
    slot_range = jnp.arange(width, dtype=jnp.int32)
    unique_ok = (slot_range[None, :] <= slot_range[:, None]) & slot_live[None, :]
    allowed = jnp.concatenate(
        [
            jnp.broadcast_to(block_ok[None], (width, block_ok.shape[0])),
            jnp.broadcast_to(shared_ok[None], (width, shared_ok.shape[0])),
            unique_ok,
        ],
        axis=1,
    )
    key_rows = jnp.concatenate(
        [prompt_k[0], fetched_rows[:, :kv_width], pairs[:, :kv_width]], axis=0
    )
    value_rows = jnp.concatenate(
        [prompt_v[0], fetched_rows[:, kv_width:], pairs[:, kv_width:]], axis=0
    )
    outputs = attend(queries, key_rows, value_rows, allowed)
    returned = lax.all_to_all(
        outputs.reshape(branches, capacity, -1), "branch", split_axis=0, concat_axis=0, tiled=True
    )
    return jnp.dot(
        placing.T, returned.reshape(width, -1), preferred_element_type=jnp.float32
    ).astype(jnp.bfloat16)


def solution(mesh):
    in_specs = (
        P(("groups", "branch"), None, None),
        P(("groups", "branch"), None, None),
        P(("groups", "branch"), None),
        P(("groups", "branch"), None, None),
        P(("groups", "branch")),
        P(("groups", "branch"), None),
        P(("groups", "branch"), None),
        P(("groups", "branch"), None),
        P(("groups", "branch"), None),
    )
    out_specs = P(("groups", "branch"), None)
    return jax.shard_map(body, mesh=mesh, in_specs=in_specs, out_specs=out_specs, check_vma=False)
```

profile of v0, /device:TPU:0, one launch (start us, length us, event | category | flops | bytes accessed | tf_op | source)
XLA Modules:
  0.0 170.8 jit_solution(4831581094639258558)
XLA Ops:
  0.0 1.3 fusion.24
  1.3 1.9 %fusion.20 = s32[16,1,1]{0,2,1:T(1,128)S(1)} fusion(s32[1,16]{1,0:T(1,128)} %param.16, s32[]{:T(128)} %bitcast.11, s32[]{:T(128)} %bitcast.10), kind=kLoop, calls=%fused_computation.46 | loop fusion | flops 64 | bytes 136 | tf_op jit(solution)/shard_map/jit(_where)/select_n | solution.py:46
  3.9 7.4 %all-to-all-start = ((s32[16,1,1]{2,1,0:T(1,128)}), s32[16,1,1]{2,1,0:T(1,128)S(1)}, u32[]{:S(2)}, u32[]{:S(2)}) async-start(s32[16,1,1]{2,1,0:T(1,128)} %copy.54), calls=%async_computation | async-start | bytes 16384 | tf_op jit(solution)/shard_map/all_to_all | solution.py:92
  11.3 0.9 convert_reduce_fusion
  13.7 4.0 %all-to-all-done = s32[16,1,1]{2,1,0:T(1,128)S(1)} async-done(((s32[16,1,1]{2,1,0:T(1,128)}), s32[16,1,1]{2,1,0:T(1,128)S(1)}, u32[]{:S(2)}, u32[]{:S(2)}) %all-to-all-start) | async-done | bytes 96 | tf_op jit(solution)/shard_map/all_to_all | solution.py:92
  17.6 3.4 %all-to-all-start.1 = ((s32[16,1,2]{2,1,0:T(1,128)}), s32[16,1,2]{2,1,0:T(1,128)S(1)}, u32[]{:S(2)}, u32[]{:S(2)}) async-start(s32[16,1,2]{2,1,0:T(1,128)} %bitcast.13), calls=%async_computation.1 | async-start | bytes 16384 | tf_op jit(solution)/shard_map/all_to_all | solution.py:87
  21.1 1.1 convolution_convert_fusion.2
  23.0 4.5 %all-to-all-done.1 = s32[16,1,2]{2,1,0:T(1,128)S(1)} async-done(((s32[16,1,2]{2,1,0:T(1,128)}), s32[16,1,2]{2,1,0:T(1,128)S(1)}, u32[]{:S(2)}, u32[]{:S(2)}) %all-to-all-start.1) | async-done | bytes 160 | tf_op jit(solution)/shard_map/all_to_all | solution.py:87
  27.5 3.5 %all-to-all-start.4 = ((bf16[16,2,2048]{2,1,0:T(2,128)(2,1)}), bf16[16,2,2048]{2,1,0:T(2,128)(2,1)S(1)}, u32[]{:S(2)}, u32[]{:S(2)}) async-start(bf16[16,2,2048]{2,1,0:T(2,128)(2,1)} %reshape.133), calls=%async_computation.4 | async-start | bytes 262144 | tf_op jit(solution)/shard_map/all_to_all | solution.py:86
  31.4 1.1 reshape.131
  32.5 6.3 %all-to-all-done.4 = bf16[16,2,2048]{2,1,0:T(2,128)(2,1)S(1)} async-done(((bf16[16,2,2048]{2,1,0:T(2,128)(2,1)}), bf16[16,2,2048]{2,1,0:T(2,128)(2,1)S(1)}, u32[]{:S(2)}, u32[]{:S(2)}) %all-to-all-start.4) | async-done | bytes 131104 | tf_op jit(solution)/shard_map/all_to_all | solution.py:86
  38.9 3.6 %all-to-all-start.2 = ((bf16[16,2,8192]{2,1,0:T(2,128)(2,1)}), bf16[16,2,8192]{2,1,0:T(2,128)(2,1)S(1)}, u32[]{:S(2)}, u32[]{:S(2)}) async-start(bf16[16,2,8192]{2,1,0:T(2,128)(2,1)} %reshape.131), calls=%async_computation.2 | async-start | bytes 1048576 | tf_op jit(solution)/shard_map/all_to_all | solution.py:85
  42.5 1.4 select_select_fusion
  43.9 13.0 %all-to-all-done.2 = bf16[16,2,8192]{2,1,0:T(2,128)(2,1)S(1)} async-done(((bf16[16,2,8192]{2,1,0:T(2,128)(2,1)}), bf16[16,2,8192]{2,1,0:T(2,128)(2,1)S(1)}, u32[]{:S(2)}, u32[]{:S(2)}) %all-to-all-start.2) | async-done | bytes 524320 | tf_op jit(solution)/shard_map/all_to_all | solution.py:85
  56.9 4.0 %all-to-all-start.3 = ((bf16[16,24,2048]{2,1,0:T(8,128)(2,1)}), bf16[16,24,2048]{2,1,0:T(8,128)(2,1)S(1)}, u32[]{:S(2)}, u32[]{:S(2)}) async-start(bf16[16,24,2048]{2,1,0:T(8,128)(2,1)} %select_select_fusion), calls=%async_computation.3 | async-start | bytes 3145728 | tf_op jit(solution)/shard_map/all_to_all | solution.py:91
  60.9 3.9 %copy.56 = bf16[1,1024,1024]{1,2,0:T(8,128)(2,1)} copy(bf16[1,1024,1024]{2,1,0:T(8,128)(2,1)} %param.11) | data formatting | bytes 4194304 | tf_op args[0]
  64.9 4.0 %copy.59 = bf16[1,1024,1024]{1,2,0:T(8,128)(2,1)} copy(bf16[1,1024,1024]{2,1,0:T(8,128)(2,1)} %param.12) | data formatting | bytes 4194304 | tf_op args[1]
  71.4 1.2 reshape_reshape.6
  72.6 20.3 %all-to-all-done.3 = bf16[16,24,2048]{2,1,0:T(8,128)(2,1)S(1)} async-done(((bf16[16,24,2048]{2,1,0:T(8,128)(2,1)}), bf16[16,24,2048]{2,1,0:T(8,128)(2,1)S(1)}, u32[]{:S(2)}, u32[]{:S(2)}) %all-to-all-start.3) | async-done | bytes 1572896 | tf_op jit(solution)/shard_map/all_to_all | solution.py:91
  92.9 1.0 fusion.22
  93.9 1.2 copy.57
  95.1 2.2 %maximum_bitcast_fusion = bf16[8,1440,128]{1,2,0:T(8,128)(2,1)S(1)} fusion(bf16[32,8,128]{0,2,1:T(8,128)(2,1)} %bitcast.73, bf16[384,8,128]{0,2,1:T(8,128)(2,1)} %bitcast.69, bf16[1024,8,128]{0,2,1:T(8,128)(2,1)} %bitcast.67), kind=kLoop, calls=%fused_computation.20 | loop fusion | flops 8847360 | bytes 5898240 | tf_op jit(solution)/shard_map/transpose | solution.py:18
  97.3 2.8 %copy.63 = bf16[8,1440,128]{2,1,0:T(8,128)(2,1)} copy(bf16[8,1440,128]{1,2,0:T(8,128)(2,1)S(1)} %maximum_bitcast_fusion) | data formatting | bytes 5898240 | tf_op jit(solution)/shard_map/while | solution.py:36
  100.1 2.3 %copy.60 = bf16[384,1024]{0,1:T(8,128)(2,1)} copy(bf16[384,1024]{1,0:T(8,128)(2,1)} %get-tuple-element.82) | data formatting | bytes 1572864 | tf_op jit(solution)/shard_map/slice | solution.py:117
  102.4 2.2 %maximum_bitcast_fusion.1 = bf16[8,1440,128]{1,2,0:T(8,128)(2,1)S(1)} fusion(bf16[32,8,128]{0,2,1:T(8,128)(2,1)} %bitcast.72, bf16[384,8,128]{0,2,1:T(8,128)(2,1)} %bitcast.70, bf16[1024,8,128]{0,2,1:T(8,128)(2,1)} %bitcast.66), kind=kLoop, calls=%fused_computation.21 | loop fusion | flops 8847360 | bytes 5898240 | tf_op jit(solution)/shard_map/transpose | solution.py:19
  104.6 2.8 %copy.64 = bf16[8,1440,128]{2,1,0:T(8,128)(2,1)} copy(bf16[8,1440,128]{1,2,0:T(8,128)(2,1)S(1)} %maximum_bitcast_fusion.1) | data formatting | bytes 5898240 | tf_op jit(solution)/shard_map/while | solution.py:36
  107.4 37.5 %while.10 = (s32[]{:T(128)}, bf16[8,8,32,128]{3,2,1,0:T(8,128)(2,1)}, pred[32,1440]{1,0:T(8,128)(4,1)S(1)}, bf16[8,8,32,128]{3,1,0,2:T(8,128)(2,1)}, bf16[8,1440...) while((s32[]{:T(128)}, bf16[8,8,32,128]{3,2,1,0:T(8,128)(2,1)}, ...), condition=%wide.region_5.6_spmd, body=%wide.region_2.5_spmd.sunk | while | flops 191389184 | bytes 5475921 | solution.py:36
  108.2 1.4 fusion.35
  110.1 2.0 %fusion.37 = bf16[8,8,32,128]{3,2,1,0:T(8,128)(2,1)} fusion(bf16[8,8,32,128]{3,2,1,0:T(8,128)(2,1)} %get-tuple-element.141, s32[]{:T(128)} %get-tuple-element.140, f32[8,32,1440]{2,1,0:T(8,128)S(1)} %get-tuple-element.131, f32[8,32]{1,0:T(8,128)S(1)} %get-tuple-element.132, bf16[8,1440,128]{2,1,0:T(8,128)(2,1)} %get-tuple-element.152, ...), kind=kOutput, calls=%fused_computation.8.clone.1 | convolution fusion | flops 95174656 | bytes 1911808 | tf_op jit(solution)/shard_map/while/body/eval_jaxpr/gsk,kd->gsd/dot_general | solution.py:33
  112.1 0.8 constant_dynamic-slice_fusion.2
  112.9 1.4 fusion.35
  114.7 2.0 %fusion.37 = bf16[8,8,32,128]{3,2,1,0:T(8,128)(2,1)} fusion(bf16[8,8,32,128]{3,2,1,0:T(8,128)(2,1)} %get-tuple-element.141, s32[]{:T(128)} %get-tuple-element.140, f32[8,32,1440]{2,1,0:T(8,128)S(1)} %get-tuple-element.131, f32[8,32]{1,0:T(8,128)S(1)} %get-tuple-element.132, bf16[8,1440,128]{2,1,0:T(8,128)(2,1)} %get-tuple-element.152, ...), kind=kOutput, calls=%fused_computation.8.clone.1 | convolution fusion | flops 95174656 | bytes 1911808 | tf_op jit(solution)/shard_map/while/body/eval_jaxpr/gsk,kd->gsd/dot_general | solution.py:33
  117.6 1.4 fusion.35
  119.4 2.0 %fusion.37 = bf16[8,8,32,128]{3,2,1,0:T(8,128)(2,1)} fusion(bf16[8,8,32,128]{3,2,1,0:T(8,128)(2,1)} %get-tuple-element.141, s32[]{:T(128)} %get-tuple-element.140, f32[8,32,1440]{2,1,0:T(8,128)S(1)} %get-tuple-element.131, f32[8,32]{1,0:T(8,128)S(1)} %get-tuple-element.132, bf16[8,1440,128]{2,1,0:T(8,128)(2,1)} %get-tuple-element.152, ...), kind=kOutput, calls=%fused_computation.8.clone.1 | convolution fusion | flops 95174656 | bytes 1911808 | tf_op jit(solution)/shard_map/while/body/eval_jaxpr/gsk,kd->gsd/dot_general | solution.py:33
  122.3 1.4 fusion.35
  124.1 2.0 %fusion.37 = bf16[8,8,32,128]{3,2,1,0:T(8,128)(2,1)} fusion(bf16[8,8,32,128]{3,2,1,0:T(8,128)(2,1)} %get-tuple-element.141, s32[]{:T(128)} %get-tuple-element.140, f32[8,32,1440]{2,1,0:T(8,128)S(1)} %get-tuple-element.131, f32[8,32]{1,0:T(8,128)S(1)} %get-tuple-element.132, bf16[8,1440,128]{2,1,0:T(8,128)(2,1)} %get-tuple-element.152, ...), kind=kOutput, calls=%fused_computation.8.clone.1 | convolution fusion | flops 95174656 | bytes 1911808 | tf_op jit(solution)/shard_map/while/body/eval_jaxpr/gsk,kd->gsd/dot_general | solution.py:33
  126.2 0.8 constant_dynamic-slice_fusion.2
  127.0 1.4 fusion.35
  128.8 2.0 %fusion.37 = bf16[8,8,32,128]{3,2,1,0:T(8,128)(2,1)} fusion(bf16[8,8,32,128]{3,2,1,0:T(8,128)(2,1)} %get-tuple-element.141, s32[]{:T(128)} %get-tuple-element.140, f32[8,32,1440]{2,1,0:T(8,128)S(1)} %get-tuple-element.131, f32[8,32]{1,0:T(8,128)S(1)} %get-tuple-element.132, bf16[8,1440,128]{2,1,0:T(8,128)(2,1)} %get-tuple-element.152, ...), kind=kOutput, calls=%fused_computation.8.clone.1 | convolution fusion | flops 95174656 | bytes 1911808 | tf_op jit(solution)/shard_map/while/body/eval_jaxpr/gsk,kd->gsd/dot_general | solution.py:33
  131.7 1.4 fusion.35
  133.5 2.0 %fusion.37 = bf16[8,8,32,128]{3,2,1,0:T(8,128)(2,1)} fusion(bf16[8,8,32,128]{3,2,1,0:T(8,128)(2,1)} %get-tuple-element.141, s32[]{:T(128)} %get-tuple-element.140, f32[8,32,1440]{2,1,0:T(8,128)S(1)} %get-tuple-element.131, f32[8,32]{1,0:T(8,128)S(1)} %get-tuple-element.132, bf16[8,1440,128]{2,1,0:T(8,128)(2,1)} %get-tuple-element.152, ...), kind=kOutput, calls=%fused_computation.8.clone.1 | convolution fusion | flops 95174656 | bytes 1911808 | tf_op jit(solution)/shard_map/while/body/eval_jaxpr/gsk,kd->gsd/dot_general | solution.py:33
  136.4 1.4 fusion.35
  138.2 2.0 %fusion.37 = bf16[8,8,32,128]{3,2,1,0:T(8,128)(2,1)} fusion(bf16[8,8,32,128]{3,2,1,0:T(8,128)(2,1)} %get-tuple-element.141, s32[]{:T(128)} %get-tuple-element.140, f32[8,32,1440]{2,1,0:T(8,128)S(1)} %get-tuple-element.131, f32[8,32]{1,0:T(8,128)S(1)} %get-tuple-element.132, bf16[8,1440,128]{2,1,0:T(8,128)(2,1)} %get-tuple-element.152, ...), kind=kOutput, calls=%fused_computation.8.clone.1 | convolution fusion | flops 95174656 | bytes 1911808 | tf_op jit(solution)/shard_map/while/body/eval_jaxpr/gsk,kd->gsd/dot_general | solution.py:33
  141.1 1.4 fusion.35
  142.9 2.0 %fusion.37 = bf16[8,8,32,128]{3,2,1,0:T(8,128)(2,1)} fusion(bf16[8,8,32,128]{3,2,1,0:T(8,128)(2,1)} %get-tuple-element.141, s32[]{:T(128)} %get-tuple-element.140, f32[8,32,1440]{2,1,0:T(8,128)S(1)} %get-tuple-element.131, f32[8,32]{1,0:T(8,128)S(1)} %get-tuple-element.132, bf16[8,1440,128]{2,1,0:T(8,128)(2,1)} %get-tuple-element.152, ...), kind=kOutput, calls=%fused_computation.8.clone.1 | convolution fusion | flops 95174656 | bytes 1911808 | tf_op jit(solution)/shard_map/while/body/eval_jaxpr/gsk,kd->gsd/dot_general | solution.py:33
  144.9 1.2 copy.65
  146.3 23.4 %all_to_all.32 = bf16[16,2,8192]{2,1,0:T(2,128)(2,1)S(1)} all-to-all(bf16[16,2,8192]{2,1,0:T(2,128)(2,1)S(1)} %reshape_reshape.7), channel_id=1, replica_groups=mesh['groups'=2,'branch'=16] {'branch'}, dimensions={0} | all-to-all | bytes 1048576 | tf_op jit(solution)/shard_map/all_to_all | solution.py:120
  169.8 1.0 convolution_convert_fusion.1
  (48 shorter events, 14.1 us)
Async XLA Ops:
  0.0 31.0 %copy-start = (bf16[16,8192]{1,0:T(8,128)(2,1)S(1)}, bf16[16,8192]{1,0:T(8,128)(2,1)}, u32[]{:S(2)}) copy-start(bf16[16,8192]{1,0:T(8,128)(2,1)} %param.17) | copy-start | bytes 786436
  0.0 42.5 %copy-start.2 = (s32[1,16]{1,0:T(1,128)S(1)}, s32[1,16]{1,0:T(1,128)}, u32[]{:S(2)}) copy-start(s32[1,16]{1,0:T(1,128)} %param.16) | copy-start | bytes 196
  0.0 42.5 %copy-start.1 = (bf16[2,24,2048]{2,1,0:T(8,128)(2,1)S(1)}, bf16[2,24,2048]{2,1,0:T(8,128)(2,1)}, u32[]{:S(2)}) copy-start(bf16[2,24,2048]{2,1,0:T(8,128)(2,1)} %param.14) | copy-start | bytes 589828
  3.9 13.7 %all-to-all-start = ((s32[16,1,1]{2,1,0:T(1,128)}), s32[16,1,1]{2,1,0:T(1,128)S(1)}, u32[]{:S(2)}, u32[]{:S(2)}) async-start(s32[16,1,1]{2,1,0:T(1,128)} %copy.54), calls=%async_computation | async-start | bytes 16384 | tf_op jit(solution)/shard_map/all_to_all | solution.py:92
  17.6 9.8 %all-to-all-start.1 = ((s32[16,1,2]{2,1,0:T(1,128)}), s32[16,1,2]{2,1,0:T(1,128)S(1)}, u32[]{:S(2)}, u32[]{:S(2)}) async-start(s32[16,1,2]{2,1,0:T(1,128)} %bitcast.13), calls=%async_computation.1 | async-start | bytes 16384 | tf_op jit(solution)/shard_map/all_to_all | solution.py:87
  27.5 11.4 %all-to-all-start.4 = ((bf16[16,2,2048]{2,1,0:T(2,128)(2,1)}), bf16[16,2,2048]{2,1,0:T(2,128)(2,1)S(1)}, u32[]{:S(2)}, u32[]{:S(2)}) async-start(bf16[16,2,2048]{2,1,0:T(2,128)(2,1)} %reshape.133), calls=%async_computation.4 | async-start | bytes 262144 | tf_op jit(solution)/shard_map/all_to_all | solution.py:86
  38.9 18.0 %all-to-all-start.2 = ((bf16[16,2,8192]{2,1,0:T(2,128)(2,1)}), bf16[16,2,8192]{2,1,0:T(2,128)(2,1)S(1)}, u32[]{:S(2)}, u32[]{:S(2)}) async-start(bf16[16,2,8192]{2,1,0:T(2,128)(2,1)} %reshape.131), calls=%async_computation.2 | async-start | bytes 1048576 | tf_op jit(solution)/shard_map/all_to_all | solution.py:85
  56.9 36.0 %all-to-all-start.3 = ((bf16[16,24,2048]{2,1,0:T(8,128)(2,1)}), bf16[16,24,2048]{2,1,0:T(8,128)(2,1)S(1)}, u32[]{:S(2)}, u32[]{:S(2)}) async-start(bf16[16,24,2048]{2,1,0:T(8,128)(2,1)} %select_select_fusion), calls=%async_computation.3 | async-start | bytes 3145728 | tf_op jit(solution)/shard_map/all_to_all | solution.py:91
  64.9 4.0 %copy-start.3 = (s32[1,8]{1,0:T(1,128)S(1)}, s32[1,8]{1,0:T(1,128)}, u32[]{:S(2)}) copy-start(s32[1,8]{1,0:T(1,128)} %param.13) | copy-start | bytes 100
where the time goes:
time: 173 us; the launch traced here: 171 us
  waiting for transfers between devices  48.1 us (28%)
  local copies, waits for them, and re-layouts  34 us (20%)
  matrix products  30.3 us (18%)
  blocking collectives  23.4 us (14%)
  starting transfers between devices  21.9 us (13%)
  other arithmetic  12.9 us (7%)
    all_to_all x1, blocking collectives, body(): lax.all_to_all(outputs.reshape(branches, capacity, -1), 'branch', split_a...  23.4 us
    all_to_all x1, waiting for transfers between devices, body(): lax.all_to_all(outgoing, 'branch', split_axis=0, concat_axis=0, tiled=True)  20.3 us
    dot_general x8, matrix products, one_head(): jnp.einsum('gsk,kd->gsd', probs, value_group, preferred_element_type=jnp....  16.3 us
    all_to_all x1, waiting for transfers between devices, body(): lax.all_to_all(send_q, 'branch', split_axis=0, concat_axis=0, tiled=True)  13 us
    dot_general x8, matrix products, one_head(): jnp.einsum('gsd,kd->gsk', query_group, key_group, preferred_element_type=...  11.5 us
    unnamed x10, local copies, waits for them, and re-layouts  7.9 us
    all_to_all x1, starting transfers between devices, body(): lax.all_to_all(outgoing_len, 'branch', split_axis=0, concat_axis=0, tiled...  7.39 us
    dynamic_slice x8, local copies, waits for them, and re-layouts, attend(): heads = lax.map(one_head, (grouped, key_heads, value_heads))  6.75 us
  transfers between devices with their start and end apart: 5, of which 5 were waited for; matrix products, arithmetic and copies ran while one was open for 11% of the time, Pallas kernels for 0%

commit v1 on v0

v1 whole, which is shorter than its diff:
```python
import functools
import math

import jax
import jax.numpy as jnp
from jax import lax
from jax.experimental import pallas as pl
from jax.experimental.pallas import tpu as pltpu
from jax.sharding import PartitionSpec as P

HD = 128
GRP = 8
CAP = 2
TILE = 16
NONE = -1e30
ABSENT = 512.0
VMEM = pl.BlockSpec(memory_space=pltpu.VMEM)
SMEM = pl.BlockSpec(memory_space=pltpu.SMEM)


def payload_kernel(pick_ref, len_ref, shared_ref, out_ref):
    results, rows, width = shared_ref.shape
    branches = pick_ref.shape[1]
    lane = lax.broadcasted_iota(jnp.int32, (TILE, HD), 1)
    meta = jnp.zeros((TILE, HD), jnp.int32)
    for b in range(branches):
        meta = jnp.where(lane == b, pick_ref[0, b], meta)
    for r in range(results):
        meta = jnp.where(lane == branches + r, len_ref[r], meta)
    out_ref[0:TILE, :] = meta.astype(jnp.float32).astype(jnp.bfloat16)
    live = results * rows
    for j in range(width // HD):
        part = shared_ref[:, :, j * HD : (j + 1) * HD].astype(jnp.float32)
        out_ref[TILE + j * live : TILE + (j + 1) * live, :] = part.reshape(live, HD).astype(jnp.bfloat16)


def place_rows(owner_ref, index_ref, count_ref):
    branches = count_ref.shape[0]
    for b in range(branches):
        count_ref[b] = 0
    for i in range(owner_ref.shape[0]):
        b = owner_ref[i]
        rank = count_ref[b]
        if index_ref is not None:
            index_ref[b * CAP + rank] = i
        count_ref[b] = rank + 1


def prep_kernel(owner_ref, q_ref, kv_ref, out_ref, index_ref, count_ref, q3_ref, kv3_ref):
    rows, q_width = q_ref.shape
    branches = out_ref.shape[0]
    heads = q_width // HD
    kv_heads = heads // GRP
    for b in range(branches * CAP):
        index_ref[b] = 0
    place_rows(owner_ref, index_ref, count_ref)
    q3_ref[...] = q_ref[...].astype(jnp.float32).reshape(rows, heads, HD)
    kv3_ref[...] = kv_ref[...].astype(jnp.float32).reshape(rows, 2 * kv_heads, HD)

    @pl.loop(0, branches)
    def _(b):
        index = [index_ref[b * CAP + c] for c in range(CAP)]
        parts = [q3_ref[i].reshape(kv_heads, 1, GRP, HD) for i in index]
        tiles = jnp.concatenate(parts, axis=1).reshape(heads * CAP, HD)
        pairs = [kv3_ref[i] for i in index]
        there = [count_ref[b] > c for c in range(CAP)]
        keys = [jnp.where(t, p[:kv_heads], ABSENT) for t, p in zip(there, pairs)]
        values = [jnp.where(t, p[kv_heads:], 0.0) for t, p in zip(there, pairs)]
        out_ref[b] = jnp.concatenate([tiles] + keys + values, axis=0).astype(jnp.bfloat16)


def attend_kernel(full, split, me_ref, mask_ref, pk_ref, pv_ref, recv_ref, *refs):
    out_ref = refs[-1]
    blocks = [(ref, ref, TILE * 1) for ref in refs[:full]]
    halves = refs[full : full + 2 * split]
    blocks += [(halves[2 * i], halves[2 * i + 1], 0) for i in range(split)]
    branches = recv_ref.shape[0]
    kv_heads = pk_ref.shape[2] // HD
    prompt = pk_ref.shape[1]
    width = branches * CAP
    live = (refs[0].shape[0] - TILE) // (2 * kv_heads)
    rows = live // 2
    heads = kv_heads * GRP
    factor = math.log2(math.e) / math.sqrt(HD)
    me = me_ref[0]

    lane = lax.broadcasted_iota(jnp.int32, (1, HD), 1)
    column = lax.broadcasted_iota(jnp.int32, (1, live), 1)
    biases = []
    for key_ref, _, _ in blocks:
        meta = key_ref[0:TILE, :].astype(jnp.float32)[0:1, :]
        pick = jnp.sum(jnp.where(lane == me, meta, 0.0), axis=1, keepdims=True)
        ok = jnp.zeros((1, live), jnp.bool_)
        for r in range(2):
            length = jnp.sum(jnp.where(lane == branches + r, meta, 0.0), axis=1, keepdims=True)
            place = (column - r * rows).astype(jnp.float32)
            ok = ok | ((place >= 0.0) & (place < length) & (pick == float(r)))
        biases.append(jnp.where(ok, 0.0, NONE))
    shared_bias = jnp.concatenate(biases, axis=1)

    blocks_seen = mask_ref.shape[1]
    span = prompt // blocks_seen
    prompt_bias = jnp.concatenate(
        [jnp.full((1, span), jnp.where(mask_ref[0, j] > 0, 0.0, NONE)) for j in range(blocks_seen)], axis=1
    )

    all_keys = recv_ref[:, heads * CAP : heads * CAP + TILE, :].reshape(branches * TILE, HD)
    all_values = recv_ref[:, heads * CAP + TILE : heads * CAP + 2 * TILE, :].reshape(branches * TILE, HD)
    chunk = min(branches, 16)
    chunk_rows = chunk * CAP * GRP
    nt = (((1,), (1,)), ((), ()))

    @pl.loop(0, kv_heads)
    def _(g):
        at = pl.multiple_of(g * HD, HD)
        spot = pl.multiple_of(g * live, TILE)
        prompt_keys = pk_ref[0, :, pl.ds(at, HD)]
        prompt_values = pv_ref[0, :, pl.ds(at, HD)]
        shared_keys = jnp.concatenate([k[pl.ds(TILE + spot, live), :] for k, _, _ in blocks], axis=0)
        shared_values = jnp.concatenate(
            [v[pl.ds((TILE + kv_heads * live if whole else 0) + spot, live), :] for _, v, whole in blocks], axis=0
        )
        place = lax.broadcasted_iota(jnp.int32, (width, branches * TILE), 1)
        slot = lax.broadcasted_iota(jnp.int32, (width, branches * TILE), 0)
        choose = jnp.where(place == slot * kv_heads + g, 1.0, 0.0).astype(jnp.bfloat16)
        keys = jnp.dot(choose, all_keys, preferred_element_type=jnp.float32).astype(jnp.bfloat16)
        values = jnp.dot(choose, all_values, preferred_element_type=jnp.float32).astype(jnp.bfloat16)
        first = jnp.where(lax.broadcasted_iota(jnp.int32, (TILE, HD), 1) == 0, 1.0, 0.0).astype(jnp.bfloat16)
        flag = lax.dot_general(first, keys, nt, preferred_element_type=jnp.float32)[0:1, :]

        @pl.loop(0, branches // chunk)
        def _(part):
            base = part * chunk
            queries = recv_ref[pl.ds(base, chunk), pl.ds(pl.multiple_of(g * TILE, TILE), TILE), :]
            queries = queries.reshape(chunk_rows, HD)

            def scores(k):
                return lax.dot_general(queries, k, nt, preferred_element_type=jnp.float32)

            own_slot = base * CAP + lax.broadcasted_iota(jnp.int32, (chunk_rows, width), 0) // GRP
            key_slot = lax.broadcasted_iota(jnp.int32, (chunk_rows, width), 1)
            seen = (key_slot <= own_slot) & (flag < ABSENT / 2)
            sets = [
                (scores(prompt_keys) + prompt_bias, prompt_values),
                (scores(shared_keys) + shared_bias, shared_values),
                (jnp.where(seen, scores(keys), NONE), values),
            ]
            largest = functools.reduce(
                jnp.maximum, [jnp.max(s, axis=1, keepdims=True) for s, _ in sets]
            )
            total = jnp.zeros((chunk_rows, 1), jnp.float32)
            mixed = jnp.zeros((chunk_rows, HD), jnp.float32)
            for s, v in sets:
                weights = jnp.exp2((s - largest) * factor)
                total = total + jnp.sum(weights, axis=1, keepdims=True)
                mixed = mixed + jnp.dot(weights.astype(jnp.bfloat16), v, preferred_element_type=jnp.float32)
            result = (mixed / total).astype(jnp.bfloat16)
            out_ref[pl.ds(base, chunk), pl.ds(pl.multiple_of(g * TILE, TILE), TILE), :] = result.reshape(
                chunk, TILE, HD
            )


def post_kernel(owner_ref, back_ref, out_ref, count_ref, o3_ref):
    rows, width = out_ref.shape
    heads = width // HD
    branches = back_ref.shape[0]
    for b in range(branches):
        count_ref[b] = 0

    @pl.loop(0, rows)
    def _(i):
        b = owner_ref[i]
        rank = count_ref[b]
        count_ref[b] = rank + 1
        tiles = back_ref[b].astype(jnp.float32).reshape(heads // GRP, CAP, GRP, HD)
        o3_ref[i] = jnp.where(rank == 0, tiles[:, 0], tiles[:, 1]).reshape(heads, HD)

    out_ref[...] = o3_ref[...].reshape(rows, width).astype(jnp.bfloat16)


def body(
    prompt_k, prompt_v, prompt_mask, shared_kv, shared_len, send_pick, unique_q, unique_kv, unique_owner
):
    branches = lax.axis_size("branch")
    chips = branches // 2
    row_count, q_width = unique_q.shape
    heads = q_width // HD
    kv_width = unique_kv.shape[1] // 2
    kv_heads = kv_width // HD
    results, result_rows, _ = shared_kv.shape
    owner_of = unique_owner[:, 0]
    live = results * result_rows
    payload_rows = TILE + 2 * kv_heads * live
    slot_rows = CAP * heads + 2 * TILE
    params = pltpu.CompilerParams(vmem_limit_bytes=32 << 20)

    payload = pl.pallas_call(
        payload_kernel,
        out_shape=jax.ShapeDtypeStruct((payload_rows, HD), jnp.bfloat16),
        in_specs=[SMEM, SMEM, VMEM],
        out_specs=VMEM,
        compiler_params=params,
        name="payload",
    )(send_pick, shared_len, shared_kv)
    send = pl.pallas_call(
        prep_kernel,
        out_shape=jax.ShapeDtypeStruct((branches, slot_rows, HD), jnp.bfloat16),
        in_specs=[SMEM, VMEM, VMEM],
        out_specs=VMEM,
        scratch_shapes=[
            pltpu.SMEM((branches * CAP,), jnp.int32),
            pltpu.SMEM((branches,), jnp.int32),
            pltpu.VMEM((row_count, heads, HD), jnp.float32),
            pltpu.VMEM((row_count, 2 * kv_heads, HD), jnp.float32),
        ],
        compiler_params=params,
        name="prep",
    )(owner_of, unique_q, unique_kv)
    recv = lax.all_to_all(send, "branch", split_axis=0, concat_axis=0, tiled=True)

    order = list(range(0, chips, 2)) + list(range(1, chips, 2))[::-1]

    def along(x, step):
        pairs = [
            (order[p] * 2 + core, order[(p + step) % chips] * 2 + core)
            for p in range(chips)
            for core in range(2)
        ]
        return lax.ppermute(x, "branch", pairs)

    def across(x):
        return lax.ppermute(x, "branch", [(i, i ^ 1) for i in range(branches)])

    cut = TILE + kv_heads * live
    whole = [payload]
    ahead = behind = payload
    for _ in range(chips // 2 - 1):
        ahead, behind = along(ahead, 1), along(behind, -1)
        whole += [ahead, behind]
    last = [along(ahead[:cut], 1), along(behind[cut:], -1)]
    blocks = whole + [across(x) for x in whole]
    halves = last + [across(x) for x in last]
    me = jnp.full((1,), lax.axis_index("branch"), jnp.int32)
    keys = prompt_k.shape[1] + branches * live + CAP * branches
    outputs = pl.pallas_call(
        functools.partial(attend_kernel, len(blocks), len(halves) // 2),
        out_shape=jax.ShapeDtypeStruct((branches, CAP * heads, HD), jnp.bfloat16),
        in_specs=[SMEM, SMEM] + [VMEM] * (3 + len(blocks) + len(halves)),
        out_specs=VMEM,
        compiler_params=params,
        cost_estimate=pl.CostEstimate(
            flops=4 * branches * CAP * heads * HD * keys,
            bytes_accessed=4 * prompt_k.size,
            transcendentals=branches * CAP * heads * keys,
        ),
        name="attend",
    )(me, prompt_mask, prompt_k, prompt_v, recv, *blocks, *halves)
    back = lax.all_to_all(outputs, "branch", split_axis=0, concat_axis=0, tiled=True)
    return pl.pallas_call(
        post_kernel,
        out_shape=jax.ShapeDtypeStruct((row_count, q_width), jnp.bfloat16),
        in_specs=[SMEM, VMEM],
        out_specs=VMEM,
        scratch_shapes=[
            pltpu.SMEM((branches,), jnp.int32),
            pltpu.VMEM((row_count, heads, HD), jnp.float32),
        ],
        compiler_params=params,
        name="post",
    )(owner_of, back)


def solution(mesh):
    split = ("groups", "branch")
    in_specs = (
        P(split, None, None),
        P(split, None, None),
        P(split, None),
        P(split, None, None),
        P(split),
        P(split, None),
        P(split, None),
        P(split, None),
        P(split, None),
    )
    return jax.shard_map(body, mesh=mesh, in_specs=in_specs, out_specs=P(split, None), check_vma=False)
```

time: 173 us -> 97.2 us (0.56)
  matrix products: 30.3 us -> 0 us
  waiting for transfers between devices: 48.1 us -> 26.3 us
  local copies, waits for them, and re-layouts: 34 us -> 13.8 us
  Pallas kernels: 0 us -> 15.2 us
  other arithmetic: 12.9 us -> 0 us
  blocking collectives: 23.4 us -> 19.2 us
    all_to_all x5 -> x1, waiting for transfers between devices: 48.1 us -> 0.01 us  [body(): lax.all_to_all(send, 'branch', split_axis=0, concat_axis=0, tiled=True)]
    dot_general x19 -> x0, matrix products: 30.3 us -> none  [the longest x8 16.3 us: one_head(): jnp.einsum('gsk,kd->gsd', probs, value_group, preferred_element_type=jnp....]
    ppermute x0 -> x17, waiting for transfers between devices: none -> 26.3 us  [the longest x8 24.7 us: along(): return lax.ppermute(x, 'branch', pairs)]
    pallas_call x0 -> x4, Pallas kernels: none -> 15.2 us  [the longest x1 11.3 us: body(): pl.pallas_call(functools.partial(attend_kernel, len(blocks), len(halves)...]
    ppermute x0 -> x17, starting transfers between devices: none -> 14.6 us  [the longest x8 13.1 us: along(): return lax.ppermute(x, 'branch', pairs)]
    all_to_all x5 -> x1, starting transfers between devices: 21.9 us -> 7.39 us  [body(): lax.all_to_all(send, 'branch', split_axis=0, concat_axis=0, tiled=True)]
    dynamic_slice x8 -> x0, local copies, waits for them, and re-layouts: 6.75 us -> none  [attend(): heads = lax.map(one_head, (grouped, key_heads, value_heads))]
    unnamed x10 -> x44, local copies, waits for them, and re-layouts: 7.9 us -> 13.8 us
  transfers between devices with their start and end apart: 5 -> 18, of which waited for: 5 -> 7; matrix products, arithmetic and copies ran while one was open for 11% -> 0% of each run, Pallas kernels for 0% -> 1%
where the time goes in v1:
time: 97.2 us; the launch traced here: 96.7 us
  waiting for transfers between devices  26.3 us (27%)
  starting transfers between devices  22 us (23%)
  blocking collectives  19.2 us (20%)
  Pallas kernels  15.2 us (16%)
  local copies, waits for them, and re-layouts  13.8 us (14%)
    ppermute x8, waiting for transfers between devices, along(): return lax.ppermute(x, 'branch', pairs)  24.7 us
    all_to_all x1, blocking collectives, body(): lax.all_to_all(outputs, 'branch', split_axis=0, concat_axis=0, tiled=True)  19.2 us
    unnamed x44, local copies, waits for them, and re-layouts  13.8 us
    ppermute x8, starting transfers between devices, along(): return lax.ppermute(x, 'branch', pairs)  13.1 us
    pallas_call x1, Pallas kernels, body(): pl.pallas_call(functools.partial(attend_kernel, len(blocks), len(halves)...  11.3 us
    all_to_all x1, starting transfers between devices, body(): lax.all_to_all(send, 'branch', split_axis=0, concat_axis=0, tiled=True)  7.39 us
  transfers between devices with their start and end apart: 18, of which 7 were waited for; matrix products, arithmetic and copies ran while one was open for 0% of the time, Pallas kernels for 1%

profile of v1, /device:TPU:0, one launch (start us, length us, event | category | flops | bytes accessed | tf_op | source)
XLA Modules:
  0.0 96.7 jit_solution(1070401992810115157)
XLA Ops:
  0.0 1.1 %copy-done.2 = bf16[16,8192]{1,0:T(8,128)(2,1)S(1)} copy-done((bf16[16,8192]{1,0:T(8,128)(2,1)S(1)}, bf16[16,8192]{1,0:T(8,128)(2,1)}, u32[]{:S(2)}) %copy-start.2) | copy-done | bytes 262168
  1.1 0.8 copy-done.16
  1.9 0.7 copy-done.17
  2.6 1.7 %prep.1 = bf16[16,160,128]{2,1,0:T(8,128)(2,1)} custom-call(s32[16]{0:T(128)S(1)} %bitcast.2, bf16[16,8192]{1,0:T(8,128)(2,1)S(1)} %copy-done.2, bf16[16,2048]{1,0:T(8,128)(2,1)S(1)} %copy-done.16), custom_call_target="tpu_custom_call" | custom-call | tf_op jit(solution)/shard_map/prep/pallas_call | solution.py:205
  4.3 7.4 %all-to-all-start = ((bf16[16,160,128]{2,1,0:T(8,128)(2,1)}), bf16[16,160,128]{2,1,0:T(8,128)(2,1)S(1)}, u32[]{:S(2)}, u32[]{:S(2)}) async-start(bf16[16,160,128]{2,1,0:T(8,128)(2,1)} %prep.1), calls=%async_computation | async-start | bytes 1310720 | tf_op jit(solution)/shard_map/all_to_all | solution.py:219
  11.8 0.6 payload.1.refs_0_
  12.4 2.0 %collective-permute-start = (bf16[784,128]{1,0:T(8,128)(2,1)S(1)}, bf16[784,128]{1,0:T(8,128)(2,1)S(1)}, u32[]{:S(2)}, u32[]{:S(2)}) collective-permute-start(bf16[784,128]{1,0:T(8,128)(2,1)S(1)} %payload.1.refs_0_), channel_id=1, source_target_pairs={{0,4},{1,5},{4,8},{5,9},{8,12},{9,13},{12,14},{13,15},{14,10},{15,... | collective-permute-start | bytes 602120 | tf_op jit(solution)/shard_map/ppermute | solution.py:229
  14.3 0.1 collective-permute-start.1
  14.4 13.2 %collective-permute-done.refs_1_ = bf16[784,128]{1,0:T(8,128)(2,1)S(1)} collective-permute-done((bf16[784,128]{1,0:T(8,128)(2,1)S(1)}, bf16[784,128]{1,0:T(8,128)(2,1)S(1)}, u32[]{:S(2)}, u32[]{:S(2)}) %collective-permute-start) | collective-permute-done | bytes 200736 | tf_op jit(solution)/shard_map/ppermute | solution.py:229
  27.7 5.2 %collective-permute-start.2 = (bf16[784,128]{1,0:T(8,128)(2,1)S(1)}, bf16[784,128]{1,0:T(8,128)(2,1)S(1)}, u32[]{:S(2)}, u32[]{:S(2)}) collective-permute-start(bf16[784,128]{1,0:T(8,128)(2,1)S(1)} %collective-permute-done.refs_1_), channel_id=1, source_target_pairs={{0,4},{1,5},{4,8},{5,9},{8,12},{9,13},{12,14},{13,15},{14,10},{15,... | collective-permute-start | bytes 602120 | tf_op jit(solution)/shard_map/ppermute | solution.py:229
  32.8 0.0 collective-permute-done.1.refs_2_
  32.8 0.0 collective-permute-start.3
  32.8 4.0 %collective-permute-done.2.refs_3_ = bf16[784,128]{1,0:T(8,128)(2,1)S(1)} collective-permute-done((bf16[784,128]{1,0:T(8,128)(2,1)S(1)}, bf16[784,128]{1,0:T(8,128)(2,1)S(1)}, u32[]{:S(2)}, u32[]{:S(2)}) %collective-permute-start.2) | collective-permute-done | bytes 200736 | tf_op jit(solution)/shard_map/ppermute | solution.py:229
  36.9 2.5 %collective-permute-start.4 = (bf16[784,128]{1,0:T(8,128)(2,1)S(1)}, bf16[784,128]{1,0:T(8,128)(2,1)S(1)}, u32[]{:S(2)}, u32[]{:S(2)}) collective-permute-start(bf16[784,128]{1,0:T(8,128)(2,1)S(1)} %collective-permute-done.2.refs_3_), channel_id=1, source_target_pairs={{0,4},{1,5},{4,8},{5,9},{8,12},{9,13},{12,14},{13,15},{14,10},{15,... | collective-permute-start | bytes 602120 | tf_op jit(solution)/shard_map/ppermute | solution.py:229
  39.4 0.0 collective-permute-start.6
  39.4 0.5 collective-permute-start.7
  39.9 0.1 collective-permute-done.3.refs_4_
  39.9 1.6 %collective-permute-start.5 = (bf16[784,128]{1,0:T(8,128)(2,1)}, bf16[784,128]{1,0:T(8,128)(2,1)S(1)}, u32[]{:S(2)}, u32[]{:S(2)}) collective-permute-start(bf16[784,128]{1,0:T(8,128)(2,1)} %collective-permute-done.3.refs_4_), channel_id=1, source_target_pairs={{0,2},{1,3},{4,0},{5,1},{8,4},{9,5},{12,8},{13,9},{14,12},{15,13},... | collective-permute-start | bytes 602120 | tf_op jit(solution)/shard_map/ppermute | solution.py:229
  41.5 3.7 %collective-permute-done.4.refs_5_ = bf16[784,128]{1,0:T(8,128)(2,1)S(1)} collective-permute-done((bf16[784,128]{1,0:T(8,128)(2,1)S(1)}, bf16[784,128]{1,0:T(8,128)(2,1)S(1)}, u32[]{:S(2)}, u32[]{:S(2)}) %collective-permute-start.4) | collective-permute-done | bytes 200736 | tf_op jit(solution)/shard_map/ppermute | solution.py:229
  45.2 0.0 collective-permute-start.9
  45.2 0.7 copy-done.5
  45.9 0.0 collective-permute-done.6.refs_7_
  46.0 0.7 copy-done.7
  46.6 0.0 collective-permute-start.13
  46.6 0.0 collective-permute-done.7.refs_8_
  46.6 0.7 copy-done.9
  47.3 0.5 collective-permute-start.10
  47.8 0.0 collective-permute-done.8.refs_9_
  47.8 0.7 copy-done.11
  48.5 0.0 collective-permute-start.11
  48.5 0.5 collective-permute-start.12
  49.0 0.7 copy-done.13
  49.7 1.7 %collective-permute-start.14 = (bf16[384,128]{1,0:T(8,128)(2,1)S(1)}, bf16[384,128]{1,0:T(8,128)(2,1)}, u32[]{:S(2)}, u32[]{:S(2)}) collective-permute-start(bf16[384,128]{1,0:T(8,128)(2,1)S(1)} %slice.9), channel_id=1, source_target_pairs={{0,2},{1,3},{4,0},{5,1},{8,4},{9,5},{12,8},{13,9},{14,12},{15,13},... | collective-permute-start | bytes 294920 | tf_op jit(solution)/shard_map/ppermute | solution.py:229
  51.5 0.5 collective-permute-done.13.refs_14_
  52.0 3.1 %collective-permute-done.14.refs_15_ = bf16[384,128]{1,0:T(8,128)(2,1)} collective-permute-done((bf16[384,128]{1,0:T(8,128)(2,1)S(1)}, bf16[384,128]{1,0:T(8,128)(2,1)}, u32[]{:S(2)}, u32[]{:S(2)}) %collective-permute-start.14) | collective-permute-done | bytes 98336 | tf_op jit(solution)/shard_map/ppermute | solution.py:229
  55.2 1.6 %collective-permute-done.16.refs_17_ = bf16[384,128]{1,0:T(8,128)(2,1)} collective-permute-done((bf16[384,128]{1,0:T(8,128)(2,1)}, bf16[384,128]{1,0:T(8,128)(2,1)}, u32[]{:S(2)}, u32[]{:S(2)}) %collective-permute-start.16) | collective-permute-done | bytes 98336 | tf_op jit(solution)/shard_map/ppermute | solution.py:232
  56.8 0.0 copy-start.1
  56.8 1.6 %copy-done.1 = bf16[1,1024,1024]{2,1,0:T(8,128)(2,1)S(1)} copy-done((bf16[1,1024,1024]{2,1,0:T(8,128)(2,1)S(1)}, bf16[1,1024,1024]{2,1,0:T(8,128)(2,1)}, u32[]{:S(2)}) %copy-start.1) | copy-done | bytes 2097176
  58.4 0.9 copy-done.4
  59.4 0.9 copy-done.6
  60.3 0.9 copy-done.8
  61.2 0.9 copy-done.10
  62.1 0.9 copy-done.12
  63.1 0.9 copy-done.14
  64.0 0.7 copy-done.21
  64.7 11.3 %attend.1 = bf16[16,128,128]{2,1,0:T(8,128)(2,1)S(1)} custom-call(s32[1]{0:T(128)} %bitcast.1.me_ref, s32[1,8]{1,0:T(1,128)S(1)} %copy-done.21, bf16[1,1024,1024]{2,1,0:T(8,128)(2,1)S(1)} %copy-done, bf16[1,1024,1024]{2,1,0:T(8,128)(2,1)S(1)} %copy-done.1, bf16[16,160,128]{2,1,0:T(8,128)(2,1)S(1)} %all-to-all-done.recv_ref, ...), custom_call_target="tpu_custom_call" | custom-call | flops 1912602624 | bytes 4194304 | tf_op jit(solution)/shard_map/attend/pallas_call | solution.py:245
  75.9 19.2 %all_to_all.10.back_ref = bf16[16,128,128]{2,1,0:T(8,128)(2,1)S(1)} all-to-all(bf16[16,128,128]{2,1,0:T(8,128)(2,1)S(1)} %attend.1), channel_id=1, replica_groups=mesh['groups'=2,'branch'=16] {'branch'}, dimensions={0} | all-to-all | bytes 1048576 | tf_op jit(solution)/shard_map/all_to_all | solution.py:258
  95.2 1.5 %post.1 = bf16[16,8192]{1,0:T(8,128)(2,1)} custom-call(s32[16]{0:T(128)S(1)} %bitcast.3, bf16[16,128,128]{2,1,0:T(8,128)(2,1)S(1)} %all_to_all.10.back_ref), custom_call_target="tpu_custom_call" | custom-call | tf_op jit(solution)/shard_map/post/pallas_call | solution.py:259
  (39 shorter events, 0.1 us)
Async XLA Ops:
  0.0 56.8 %copy-start = (bf16[1,1024,1024]{2,1,0:T(8,128)(2,1)S(1)}, bf16[1,1024,1024]{2,1,0:T(8,128)(2,1)}, u32[]{:S(2)}) copy-start(bf16[1,1024,1024]{2,1,0:T(8,128)(2,1)} %pk_ref.1) | copy-start | bytes 6291460
  0.0 1.1 %copy-start.2 = (bf16[16,8192]{1,0:T(8,128)(2,1)S(1)}, bf16[16,8192]{1,0:T(8,128)(2,1)}, u32[]{:S(2)}) copy-start(bf16[16,8192]{1,0:T(8,128)(2,1)} %q_ref.1) | copy-start | bytes 786436
  1.1 0.8 copy-start.16
  1.9 0.7 copy-start.17
  2.6 9.1 %copy-start.15 = (bf16[2,24,2048]{2,1,0:T(8,128)(2,1)S(1)}, bf16[2,24,2048]{2,1,0:T(8,128)(2,1)}, u32[]{:S(2)}) copy-start(bf16[2,24,2048]{2,1,0:T(8,128)(2,1)} %shared_ref.1) | copy-start | bytes 589828
  2.6 9.2 %copy-start.19 = (s32[1,16]{1,0:T(1,128)S(1)}, s32[1,16]{1,0:T(1,128)}, u32[]{:S(2)}) copy-start(s32[1,16]{1,0:T(1,128)} %pick_ref.1) | copy-start | bytes 196
  2.6 9.2 %copy-start.20 = (s32[2]{0:T(128)S(1)}, s32[2]{0:T(128)}, u32[]{:S(2)}) copy-start(s32[2]{0:T(128)} %len_ref.1) | copy-start | bytes 28
  4.3 52.5 %all-to-all-start = ((bf16[16,160,128]{2,1,0:T(8,128)(2,1)}), bf16[16,160,128]{2,1,0:T(8,128)(2,1)S(1)}, u32[]{:S(2)}, u32[]{:S(2)}) async-start(bf16[16,160,128]{2,1,0:T(8,128)(2,1)} %prep.1), calls=%async_computation | async-start | bytes 1310720 | tf_op jit(solution)/shard_map/all_to_all | solution.py:219
  12.4 15.3 %collective-permute-start = (bf16[784,128]{1,0:T(8,128)(2,1)S(1)}, bf16[784,128]{1,0:T(8,128)(2,1)S(1)}, u32[]{:S(2)}, u32[]{:S(2)}) collective-permute-start(bf16[784,128]{1,0:T(8,128)(2,1)S(1)} %payload.1.refs_0_), channel_id=1, source_target_pairs={{0,4},{1,5},{4,8},{5,9},{8,12},{9,13},{12,14},{13,15},{14,10},{15,... | collective-permute-start | bytes 602120 | tf_op jit(solution)/shard_map/ppermute | solution.py:229
  14.3 18.5 %collective-permute-start.1 = (bf16[784,128]{1,0:T(8,128)(2,1)S(1)}, bf16[784,128]{1,0:T(8,128)(2,1)S(1)}, u32[]{:S(2)}, u32[]{:S(2)}) collective-permute-start(bf16[784,128]{1,0:T(8,128)(2,1)S(1)} %payload.1.refs_0_), channel_id=1, source_target_pairs={{0,2},{1,3},{4,0},{5,1},{8,4},{9,5},{12,8},{13,9},{14,12},{15,13},... | collective-permute-start | bytes 602120 | tf_op jit(solution)/shard_map/ppermute | solution.py:229
  27.7 9.2 %collective-permute-start.2 = (bf16[784,128]{1,0:T(8,128)(2,1)S(1)}, bf16[784,128]{1,0:T(8,128)(2,1)S(1)}, u32[]{:S(2)}, u32[]{:S(2)}) collective-permute-start(bf16[784,128]{1,0:T(8,128)(2,1)S(1)} %collective-permute-done.refs_1_), channel_id=1, source_target_pairs={{0,4},{1,5},{4,8},{5,9},{8,12},{9,13},{12,14},{13,15},{14,10},{15,... | collective-permute-start | bytes 602120 | tf_op jit(solution)/shard_map/ppermute | solution.py:229
  32.8 15.7 %copy-start.3 = (bf16[784,128]{1,0:T(8,128)(2,1)}, bf16[784,128]{1,0:T(8,128)(2,1)S(1)}, u32[]{:S(2)}) copy-start(bf16[784,128]{1,0:T(8,128)(2,1)S(1)} %collective-permute-done.1.refs_2_) | copy-start | bytes 602116
  32.8 7.1 %collective-permute-start.3 = (bf16[784,128]{1,0:T(8,128)(2,1)S(1)}, bf16[784,128]{1,0:T(8,128)(2,1)}, u32[]{:S(2)}, u32[]{:S(2)}) collective-permute-start(bf16[784,128]{1,0:T(8,128)(2,1)S(1)} %collective-permute-done.1.refs_2_), channel_id=1, source_target_pairs={{0,2},{1,3},{4,0},{5,1},{8,4},{9,5},{12,8},{13,9},{14,12},{15,13},... | collective-permute-start | bytes 602120 | tf_op jit(solution)/shard_map/ppermute | solution.py:229
  36.9 8.3 %collective-permute-start.4 = (bf16[784,128]{1,0:T(8,128)(2,1)S(1)}, bf16[784,128]{1,0:T(8,128)(2,1)S(1)}, u32[]{:S(2)}, u32[]{:S(2)}) collective-permute-start(bf16[784,128]{1,0:T(8,128)(2,1)S(1)} %collective-permute-done.2.refs_3_), channel_id=1, source_target_pairs={{0,4},{1,5},{4,8},{5,9},{8,12},{9,13},{12,14},{13,15},{14,10},{15,... | collective-permute-start | bytes 602120 | tf_op jit(solution)/shard_map/ppermute | solution.py:229
  39.4 6.6 %collective-permute-start.6 = (bf16[784,128]{1,0:T(8,128)(2,1)S(1)}, bf16[784,128]{1,0:T(8,128)(2,1)S(1)}, u32[]{:S(2)}, u32[]{:S(2)}) collective-permute-start(bf16[784,128]{1,0:T(8,128)(2,1)S(1)} %payload.1.refs_0_), channel_id=1, source_target_pairs={{0,1},{1,0},{2,3},{3,2},{4,5},{5,4},{6,7},{7,6},{8,9},{9,8},{10,11... | collective-permute-start | bytes 602120 | tf_op jit(solution)/shard_map/ppermute | solution.py:232
  39.4 7.3 %collective-permute-start.7 = (bf16[784,128]{1,0:T(8,128)(2,1)S(1)}, bf16[784,128]{1,0:T(8,128)(2,1)S(1)}, u32[]{:S(2)}, u32[]{:S(2)}) collective-permute-start(bf16[784,128]{1,0:T(8,128)(2,1)S(1)} %collective-permute-done.refs_1_), channel_id=1, source_target_pairs={{0,1},{1,0},{2,3},{3,2},{4,5},{5,4},{6,7},{7,6},{8,9},{9,8},{10,11... | collective-permute-start | bytes 602120 | tf_op jit(solution)/shard_map/ppermute | solution.py:232
  39.9 7.9 %collective-permute-start.8 = (bf16[784,128]{1,0:T(8,128)(2,1)S(1)}, bf16[784,128]{1,0:T(8,128)(2,1)S(1)}, u32[]{:S(2)}, u32[]{:S(2)}) collective-permute-start(bf16[784,128]{1,0:T(8,128)(2,1)S(1)} %collective-permute-done.1.refs_2_), channel_id=1, source_target_pairs={{0,1},{1,0},{2,3},{3,2},{4,5},{5,4},{6,7},{7,6},{8,9},{9,8},{10,11... | collective-permute-start | bytes 602120 | tf_op jit(solution)/shard_map/ppermute | solution.py:232
  39.9 8.6 %collective-permute-start.5 = (bf16[784,128]{1,0:T(8,128)(2,1)}, bf16[784,128]{1,0:T(8,128)(2,1)S(1)}, u32[]{:S(2)}, u32[]{:S(2)}) collective-permute-start(bf16[784,128]{1,0:T(8,128)(2,1)} %collective-permute-done.3.refs_4_), channel_id=1, source_target_pairs={{0,2},{1,3},{4,0},{5,1},{8,4},{9,5},{12,8},{13,9},{14,12},{15,13},... | collective-permute-start | bytes 602120 | tf_op jit(solution)/shard_map/ppermute | solution.py:229
  45.2 3.8 %collective-permute-start.9 = (bf16[784,128]{1,0:T(8,128)(2,1)S(1)}, bf16[784,128]{1,0:T(8,128)(2,1)S(1)}, u32[]{:S(2)}, u32[]{:S(2)}) collective-permute-start(bf16[784,128]{1,0:T(8,128)(2,1)S(1)} %collective-permute-done.2.refs_3_), channel_id=1, source_target_pairs={{0,1},{1,0},{2,3},{3,2},{4,5},{5,4},{6,7},{7,6},{8,9},{9,8},{10,11... | collective-permute-start | bytes 602120 | tf_op jit(solution)/shard_map/ppermute | solution.py:232
  45.2 0.7 copy-start.5
  46.0 0.7 copy-start.7
  46.6 5.4 %collective-permute-start.13 = (bf16[400,128]{1,0:T(8,128)(2,1)S(1)}, bf16[400,128]{1,0:T(8,128)(2,1)}, u32[]{:S(2)}, u32[]{:S(2)}) collective-permute-start(bf16[400,128]{1,0:T(8,128)(2,1)S(1)} %slice.8), channel_id=1, source_target_pairs={{0,4},{1,5},{4,8},{5,9},{8,12},{9,13},{12,14},{13,15},{14,10},{15,... | collective-permute-start | bytes 307208 | tf_op jit(solution)/shard_map/ppermute | solution.py:229
  46.6 0.7 copy-start.9
  47.3 7.8 %collective-permute-start.10 = (bf16[784,128]{1,0:T(8,128)(2,1)}, bf16[784,128]{1,0:T(8,128)(2,1)}, u32[]{:S(2)}, u32[]{:S(2)}) collective-permute-start(bf16[784,128]{1,0:T(8,128)(2,1)} %collective-permute-done.3.refs_4_), channel_id=1, source_target_pairs={{0,1},{1,0},{2,3},{3,2},{4,5},{5,4},{6,7},{7,6},{8,9},{9,8},{10,11... | collective-permute-start | bytes 602120 | tf_op jit(solution)/shard_map/ppermute | solution.py:232
  47.8 0.7 copy-start.11
  48.5 8.3 %collective-permute-start.11 = (bf16[784,128]{1,0:T(8,128)(2,1)S(1)}, bf16[784,128]{1,0:T(8,128)(2,1)}, u32[]{:S(2)}, u32[]{:S(2)}) collective-permute-start(bf16[784,128]{1,0:T(8,128)(2,1)S(1)} %collective-permute-done.4.refs_5_), channel_id=1, source_target_pairs={{0,1},{1,0},{2,3},{3,2},{4,5},{5,4},{6,7},{7,6},{8,9},{9,8},{10,11... | collective-permute-start | bytes 602120 | tf_op jit(solution)/shard_map/ppermute | solution.py:232
  48.5 8.3 %collective-permute-start.12 = (bf16[784,128]{1,0:T(8,128)(2,1)S(1)}, bf16[784,128]{1,0:T(8,128)(2,1)}, u32[]{:S(2)}, u32[]{:S(2)}) collective-permute-start(bf16[784,128]{1,0:T(8,128)(2,1)S(1)} %collective-permute-done.5.refs_6_), channel_id=1, source_target_pairs={{0,1},{1,0},{2,3},{3,2},{4,5},{5,4},{6,7},{7,6},{8,9},{9,8},{10,11... | collective-permute-start | bytes 602120 | tf_op jit(solution)/shard_map/ppermute | solution.py:232
  49.0 0.7 copy-start.13
  49.7 5.4 %collective-permute-start.14 = (bf16[384,128]{1,0:T(8,128)(2,1)S(1)}, bf16[384,128]{1,0:T(8,128)(2,1)}, u32[]{:S(2)}, u32[]{:S(2)}) collective-permute-start(bf16[384,128]{1,0:T(8,128)(2,1)S(1)} %slice.9), channel_id=1, source_target_pairs={{0,2},{1,3},{4,0},{5,1},{8,4},{9,5},{12,8},{13,9},{14,12},{15,13},... | collective-permute-start | bytes 294920 | tf_op jit(solution)/shard_map/ppermute | solution.py:229
  52.0 4.8 %collective-permute-start.15 = (bf16[400,128]{1,0:T(8,128)(2,1)}, bf16[400,128]{1,0:T(8,128)(2,1)}, u32[]{:S(2)}, u32[]{:S(2)}) collective-permute-start(bf16[400,128]{1,0:T(8,128)(2,1)} %collective-permute-done.13.refs_14_), channel_id=1, source_target_pairs={{0,1},{1,0},{2,3},{3,2},{4,5},{5,4},{6,7},{7,6},{8,9},{9,8},{10,11... | collective-permute-start | bytes 307208 | tf_op jit(solution)/shard_map/ppermute | solution.py:232
  55.1 1.6 %collective-permute-start.16 = (bf16[384,128]{1,0:T(8,128)(2,1)}, bf16[384,128]{1,0:T(8,128)(2,1)}, u32[]{:S(2)}, u32[]{:S(2)}) collective-permute-start(bf16[384,128]{1,0:T(8,128)(2,1)} %collective-permute-done.14.refs_15_), channel_id=1, source_target_pairs={{0,1},{1,0},{2,3},{3,2},{4,5},{5,4},{6,7},{7,6},{8,9},{9,8},{10,11... | collective-permute-start | bytes 294920 | tf_op jit(solution)/shard_map/ppermute | solution.py:232
  56.8 1.6 %copy-start.1 = (bf16[1,1024,1024]{2,1,0:T(8,128)(2,1)S(1)}, bf16[1,1024,1024]{2,1,0:T(8,128)(2,1)}, u32[]{:S(2)}) copy-start(bf16[1,1024,1024]{2,1,0:T(8,128)(2,1)} %pv_ref.1) | copy-start | bytes 6291460
  58.4 0.9 copy-start.4
  59.4 0.9 copy-start.6
  60.3 0.9 copy-start.8
  61.2 0.9 copy-start.10
  62.1 0.9 copy-start.12
  63.1 0.9 copy-start.14
  64.0 0.7 copy-start.21
  64.7 30.5 %copy-start.18 = (s32[16,1]{0,1:T(1,128)S(1)}, s32[16,1]{0,1:T(1,128)}, u32[]{:S(2)}) copy-start(s32[16,1]{0,1:T(1,128)} %param.17) | copy-start | bytes 196

commit v2 on v1

v2 whole, which is shorter than its diff:
```python
import functools
import math

import jax
import jax.numpy as jnp
from jax import lax
from jax.experimental import pallas as pl
from jax.experimental.pallas import tpu as pltpu
from jax.sharding import PartitionSpec as P

HD = 128
GRP = 8
CAP = 2
TILE = 16
NONE = -1e30
ABSENT = 512.0
VMEM = pl.BlockSpec(memory_space=pltpu.VMEM)
SMEM = pl.BlockSpec(memory_space=pltpu.SMEM)
ANY = pl.BlockSpec(memory_space=pl.ANY)


def grant(mebibytes):
    return pltpu.CompilerParams(vmem_limit_bytes=mebibytes << 20)


def payload_kernel(pick_hbm, len_hbm, shared_hbm, out_ref, pick_ref, len_ref, shared_ref, sems):
    results, rows, width = shared_ref.shape
    branches = pick_ref.shape[1]
    moves = [
        pltpu.make_async_copy(source, target, sems.at[n])
        for n, (source, target) in enumerate(
            ((shared_hbm, shared_ref), (pick_hbm, pick_ref), (len_hbm, len_ref))
        )
    ]
    for move in moves:
        move.start()
    for move in moves:
        move.wait()
    live = results * rows
    lane = lax.broadcasted_iota(jnp.int32, (live, HD), 1)
    meta = jnp.zeros((live, HD), jnp.int32)
    for b in range(branches):
        meta = jnp.where(lane == b, pick_ref[0, b], meta)
    for r in range(results):
        meta = jnp.where(lane == branches + r, len_ref[0, r], meta)
    slabs = width // HD
    out_ref[slabs] = meta.astype(jnp.float32).astype(jnp.bfloat16)
    for j in range(slabs):
        part = shared_ref[:, :, j * HD : (j + 1) * HD].astype(jnp.float32)
        out_ref[j] = part.reshape(live, HD).astype(jnp.bfloat16)


def place_rows(owner_ref, index_ref, count_ref):
    branches = count_ref.shape[0]
    for b in range(branches):
        count_ref[b] = 0
    for i in range(owner_ref.shape[0]):
        b = owner_ref[i]
        rank = count_ref[b]
        if index_ref is not None:
            index_ref[b * CAP + rank] = i
        count_ref[b] = rank + 1


def prep_kernel(owner_ref, q_hbm, kv_hbm, after_hbm, out_ref, index_ref, count_ref, q_ref, kv_ref, q3_ref, kv3_ref, sems):
    del after_hbm
    rows, q_width = q_ref.shape
    branches = out_ref.shape[0]
    heads = q_width // HD
    kv_heads = heads // GRP
    moves = [
        pltpu.make_async_copy(q_hbm, q_ref, sems.at[0]),
        pltpu.make_async_copy(kv_hbm, kv_ref, sems.at[1]),
    ]
    for move in moves:
        move.start()
    for b in range(branches * CAP):
        index_ref[b] = 0
    place_rows(owner_ref, index_ref, count_ref)
    for move in moves:
        move.wait()
    q3_ref[...] = q_ref[...].astype(jnp.float32).reshape(rows, heads, HD)
    kv3_ref[...] = kv_ref[...].astype(jnp.float32).reshape(rows, 2 * kv_heads, HD)

    @pl.loop(0, branches)
    def _(b):
        index = [index_ref[b * CAP + c] for c in range(CAP)]
        parts = [q3_ref[i].reshape(kv_heads, 1, GRP, HD) for i in index]
        tiles = jnp.concatenate(parts, axis=1).reshape(heads * CAP, HD)
        pairs = [kv3_ref[i] for i in index]
        there = [count_ref[b] > c for c in range(CAP)]
        keys = [jnp.where(t, p[:kv_heads], ABSENT) for t, p in zip(there, pairs)]
        values = [jnp.where(t, p[kv_heads:], 0.0) for t, p in zip(there, pairs)]
        out_ref[b] = jnp.concatenate([tiles] + keys + values, axis=0).astype(jnp.bfloat16)


def dot_nt(a, b):
    return lax.dot_general(a, b, (((1,), (1,)), ((), ())), preferred_element_type=jnp.float32)


FACTOR = math.log2(math.e) / math.sqrt(HD)


def starter(sems):
    free = iter(range(sems.shape[0]))

    def start(source, target):
        copy = pltpu.make_async_copy(source, target, sems.at[next(free)])
        copy.start()
        return copy

    return start


def bias_of(meta, me, branches, live):
    lane = lax.broadcasted_iota(jnp.int32, (1, HD), 1)
    column = lax.broadcasted_iota(jnp.int32, (1, live), 1)
    rows = live // 2
    pick = jnp.sum(jnp.where(lane == me, meta, 0.0), axis=1, keepdims=True)
    seen = jnp.zeros((1, live), jnp.bool_)
    for r in range(2):
        length = jnp.sum(jnp.where(lane == branches + r, meta, 0.0), axis=1, keepdims=True)
        place = (column - r * rows).astype(jnp.float32)
        seen = seen | ((place >= 0.0) & (place < length) & (pick == float(r)))
    return jnp.where(seen, 0.0, NONE)


def gather_kernel(whole, branches, me_ref, mask_ref, pk_hbm, pv_hbm, *refs):
    blocks = refs[:whole]
    key_ref, value_hbm, bias_ref, value_ref, meta_ref, sems = refs[whole:]
    kv_heads = key_ref.shape[0]
    prompt = pk_hbm.shape[1]
    live = meta_ref.shape[1]
    start = starter(sems)
    moves, metas = [], []
    for n, block in enumerate(blocks):
        span = pl.ds(prompt + n * live, live)
        metas.append(start(block.at[2 * kv_heads], meta_ref.at[n]))
        moves.append(start(block.at[kv_heads : 2 * kv_heads], value_ref.at[:, span, :]))
        moves.append(start(block.at[0:kv_heads], key_ref.at[:, span, :]))
    for g in range(kv_heads):
        lanes = pl.ds(g * HD, HD)
        moves.append(start(pv_hbm.at[0, :, lanes], value_ref.at[g, pl.ds(0, prompt), :]))
        moves.append(start(pk_hbm.at[0, :, lanes], key_ref.at[g, pl.ds(0, prompt), :]))
    for copy in metas:
        copy.wait()
    seen = mask_ref.shape[1]
    biases = [
        jnp.full((1, prompt // seen), jnp.where(mask_ref[0, j] > 0, 0.0, NONE)) for j in range(seen)
    ]
    for n in range(whole):
        meta = meta_ref[n, 0:TILE, :].astype(jnp.float32)[0:1, :]
        biases.append(bias_of(meta, me_ref[0], branches, live))
    bias = jnp.concatenate(biases, axis=1)
    bias_ref[...] = jnp.broadcast_to(bias, bias_ref.shape)
    for copy in moves:
        copy.wait()
    leaving = start(value_ref, value_hbm)
    leaving.wait()


def attend_kernel(
    split, me_ref, key_ref, bias_ref, value_hbm, recv_hbm, *refs
):
    out_ref, late_key_ref, late_value_ref, first_ref, second_ref, value_ref, recv_ref = refs[
        2 * split : 2 * split + 7
    ]
    halves, sems = refs[2 * split + 7 : -1], refs[-1]
    kv_heads = key_ref.shape[0]
    start = starter(sems)
    rows_move = start(recv_hbm, recv_ref)
    half_moves = [start(source, target) for source, target in zip(refs[: 2 * split], halves)]
    value_moves = [start(value_hbm.at[g], value_ref.at[g]) for g in range(kv_heads)]
    branches = recv_ref.shape[0]
    heads = kv_heads * GRP
    width = branches * CAP
    early = key_ref.shape[1]
    late = late_key_ref.shape[1]
    live = halves[0].shape[1]
    far = split * live

    chunk = min(branches, 16)
    count = chunk * TILE

    def score(g, base, target):
        queries = recv_ref[pl.ds(base, chunk), g * TILE : (g + 1) * TILE, :].reshape(count, HD)
        target[:, 0:early] = dot_nt(queries, key_ref[g]) + bias_ref[0:1, :]

    rows_move.wait()
    if branches == chunk:
        score(0, 0, first_ref)
    for copy in half_moves:
        copy.wait()

    late_bias = [
        bias_of(halves[2 * n][kv_heads, 0:TILE, :].astype(jnp.float32)[0:1, :], me_ref[0], branches, live)
        for n in range(split)
    ]
    late_bias = jnp.concatenate(late_bias + [jnp.zeros((1, width), jnp.float32)], axis=1)
    size = branches * TILE
    place = lax.broadcasted_iota(jnp.int32, (size, size), 1)
    wanted = lax.broadcasted_iota(jnp.int32, (size, size), 0)
    choose = jnp.where(place == lax.rem(wanted, width) * kv_heads + wanted // width, 1.0, 0.0).astype(jnp.bfloat16)
    for which, target in ((0, late_key_ref), (1, late_value_ref)):
        first = heads * CAP + which * TILE
        rows = recv_ref[:, first : first + TILE, :].reshape(size, HD)
        rows = jnp.dot(choose, rows, preferred_element_type=jnp.float32).astype(jnp.bfloat16)
        target[:, far:late, :] = rows.reshape(kv_heads, width, HD)
        for n in range(split):
            target[:, n * live : (n + 1) * live, :] = halves[2 * n + which][0:kv_heads]
    one = jnp.where(lax.broadcasted_iota(jnp.int32, (TILE, HD), 1) == 0, 1.0, 0.0).astype(jnp.bfloat16)
    absent = dot_nt(one, late_key_ref[0])[0:1, :] > ABSENT / 2
    for copy in value_moves:
        copy.wait()

    column = lax.broadcasted_iota(jnp.int32, (count, late), 1) - far
    own_slot = lax.broadcasted_iota(jnp.int32, (count, late), 0) // GRP

    def run(base):
        late_hidden = jnp.where((column >= 0) & (absent | (column > own_slot + base * CAP)), NONE, late_bias)

        def score_late(g, target):
            queries = recv_ref[pl.ds(base, chunk), g * TILE : (g + 1) * TILE, :].reshape(count, HD)
            target[:, early : early + late] = dot_nt(queries, late_key_ref[g]) + late_hidden

        def finish(g, source):
            scores = source[...]
            largest = jnp.max(scores, axis=1, keepdims=True)
            weights = jnp.exp2((scores - largest) * FACTOR)
            total = jnp.sum(weights, axis=1, keepdims=True)
            probs = weights.astype(jnp.bfloat16)
            mixed = jnp.dot(probs[:, 0:early], value_ref[g], preferred_element_type=jnp.float32)
            mixed = mixed + jnp.dot(probs[:, early:], late_value_ref[g], preferred_element_type=jnp.float32)
            result = (mixed / total).astype(jnp.bfloat16)
            out_ref[pl.ds(base, chunk), g * TILE : (g + 1) * TILE, :] = result.reshape(chunk, TILE, HD)

        buffers = (first_ref, second_ref)
        if branches > chunk:
            score(0, base, buffers[0])
        score_late(0, buffers[0])
        for g in range(kv_heads):
            if g + 1 < kv_heads:
                score(g + 1, base, buffers[(g + 1) % 2])
                score_late(g + 1, buffers[(g + 1) % 2])
            finish(g, buffers[g % 2])

    if branches == chunk:
        run(0)
    else:
        @pl.loop(0, branches // chunk)
        def _(part):
            run(part * chunk)


def post_kernel(owner_ref, back_ref, out_ref, count_ref, o3_ref):
    rows, width = out_ref.shape
    heads = width // HD
    branches = back_ref.shape[0]
    for b in range(branches):
        count_ref[b] = 0

    @pl.loop(0, rows)
    def _(i):
        b = owner_ref[i]
        rank = count_ref[b]
        count_ref[b] = rank + 1
        tiles = back_ref[b].astype(jnp.float32).reshape(heads // GRP, CAP, GRP, HD)
        o3_ref[i] = jnp.where(rank == 0, tiles[:, 0], tiles[:, 1]).reshape(heads, HD)

    out_ref[...] = o3_ref[...].reshape(rows, width).astype(jnp.bfloat16)


def body(
    prompt_k, prompt_v, prompt_mask, shared_kv, shared_len, send_pick, unique_q, unique_kv, unique_owner
):
    branches = lax.axis_size("branch")
    chips = branches // 2
    row_count, q_width = unique_q.shape
    heads = q_width // HD
    kv_width = unique_kv.shape[1] // 2
    kv_heads = kv_width // HD
    results, result_rows, _ = shared_kv.shape
    owner_of = unique_owner[:, 0]
    live = results * result_rows
    slot_rows = CAP * heads + 2 * TILE

    def bf16(*shape):
        return jax.ShapeDtypeStruct(shape, jnp.bfloat16)

    block = pl.pallas_call(
        payload_kernel,
        out_shape=bf16(2 * kv_heads + 1, live, HD),
        in_specs=[ANY] * 3,
        out_specs=VMEM,
        scratch_shapes=[
            pltpu.SMEM(send_pick.shape, jnp.int32),
            pltpu.SMEM((1, results), jnp.int32),
            pltpu.VMEM(shared_kv.shape, jnp.bfloat16),
            pltpu.SemaphoreType.DMA((3,)),
        ],
        compiler_params=grant(56),
        name="payload",
    )(send_pick, shared_len.reshape(1, results), shared_kv)

    order = list(range(0, chips, 2)) + list(range(1, chips, 2))[::-1]

    def along(x, step):
        pairs = [
            (order[p] * 2 + core, order[(p + step) % chips] * 2 + core)
            for p in range(chips)
            for core in range(2)
        ]
        return lax.ppermute(x, "branch", pairs)

    def across(x):
        return lax.ppermute(x, "branch", [(i, i ^ 1) for i in range(branches)])

    send = pl.pallas_call(
        prep_kernel,
        out_shape=bf16(branches, slot_rows, HD),
        in_specs=[SMEM, ANY, ANY, ANY],
        out_specs=VMEM,
        scratch_shapes=[
            pltpu.SMEM((branches * CAP,), jnp.int32),
            pltpu.SMEM((branches,), jnp.int32),
            pltpu.VMEM(unique_q.shape, jnp.bfloat16),
            pltpu.VMEM(unique_kv.shape, jnp.bfloat16),
            pltpu.VMEM((row_count, heads, HD), jnp.float32),
            pltpu.VMEM((row_count, 2 * kv_heads, HD), jnp.float32),
            pltpu.SemaphoreType.DMA((2,)),
        ],
        compiler_params=grant(56),
        cost_estimate=pl.CostEstimate(flops=0, bytes_accessed=1024, transcendentals=0),
        name="prep",
    )(owner_of, unique_q, unique_kv, block)

    blocks = [block]
    ahead = behind = block
    recv = None
    for step in range(chips // 2 - 1):
        ahead, behind = along(ahead, 1), along(behind, -1)
        blocks += [ahead, behind]
        if step == chips // 2 - 2:
            send, ahead, behind = lax.optimization_barrier((send, ahead, behind))
            recv = lax.all_to_all(send, "branch", split_axis=0, concat_axis=0, tiled=True)
    upper = jnp.concatenate([ahead[:kv_heads], ahead[2 * kv_heads :]], axis=0)
    halves = [along(upper, 1), along(behind[kv_heads : 2 * kv_heads], -1)]
    blocks = blocks + [across(x) for x in blocks]
    me = jnp.full((1,), lax.axis_index("branch"), jnp.int32)
    prompt = prompt_k.shape[1]
    whole, split = len(blocks), 2
    early = prompt + whole * live
    late = split * live + CAP * branches
    rows = CAP * branches * GRP
    keys, values, bias = pl.pallas_call(
        functools.partial(gather_kernel, whole, branches),
        out_shape=(
            pltpu.VMEM((kv_heads, early, HD), jnp.bfloat16),
            pltpu.HBM((kv_heads, early, HD), jnp.bfloat16),
            pltpu.VMEM((8, early), jnp.float32),
        ),
        in_specs=[SMEM, SMEM] + [ANY] * (2 + whole),
        out_specs=(VMEM, ANY, VMEM),
        scratch_shapes=[
            pltpu.VMEM((kv_heads, early, HD), jnp.bfloat16),
            pltpu.VMEM((whole, live, HD), jnp.bfloat16),
            pltpu.SemaphoreType.DMA((3 * whole + 2 * kv_heads + 1,)),
        ],
        compiler_params=grant(16),
        cost_estimate=pl.CostEstimate(flops=0, bytes_accessed=8 * prompt_k.size, transcendentals=0),
        name="gather",
    )(me, prompt_mask, *[pltpu.with_memory_space_constraint(x, pltpu.HBM) for x in (prompt_k, prompt_v, *blocks)])
    halves, keys = lax.optimization_barrier((halves, keys))
    halves = halves + [across(x) for x in halves]
    outputs = pl.pallas_call(
        functools.partial(attend_kernel, split),
        out_shape=bf16(branches, CAP * heads, HD),
        in_specs=[SMEM, VMEM, VMEM] + [ANY] * (2 + 2 * split),
        out_specs=VMEM,
        scratch_shapes=[
            pltpu.VMEM((kv_heads, late, HD), jnp.bfloat16),
            pltpu.VMEM((kv_heads, late, HD), jnp.bfloat16),
            pltpu.VMEM((min(branches, 16) * TILE, early + late), jnp.float32),
            pltpu.VMEM((min(branches, 16) * TILE, early + late), jnp.float32),
            pltpu.VMEM((kv_heads, early, HD), jnp.bfloat16),
            pltpu.VMEM(recv.shape, jnp.bfloat16),
            *[pltpu.VMEM(x.shape, jnp.bfloat16) for x in halves],
            pltpu.SemaphoreType.DMA((1 + 2 * split + kv_heads,)),
        ],
        compiler_params=grant(40),
        cost_estimate=pl.CostEstimate(
            flops=4 * kv_heads * rows * HD * (early + late),
            bytes_accessed=4 * prompt_k.size,
            transcendentals=kv_heads * rows * (early + late),
        ),
        name="attend",
    )(me, keys, bias, *[pltpu.with_memory_space_constraint(x, pltpu.HBM) for x in (values, recv, *halves)])
    back = lax.all_to_all(outputs, "branch", split_axis=0, concat_axis=0, tiled=True)
    return pl.pallas_call(
        post_kernel,
        out_shape=jax.ShapeDtypeStruct((row_count, q_width), jnp.bfloat16),
        in_specs=[SMEM, VMEM],
        out_specs=VMEM,
        scratch_shapes=[
            pltpu.SMEM((branches,), jnp.int32),
            pltpu.VMEM((row_count, heads, HD), jnp.float32),
        ],
        compiler_params=grant(8),
        name="post",
    )(owner_of, back)


def solution(mesh):
    split = ("groups", "branch")
    in_specs = (
        P(split, None, None),
        P(split, None, None),
        P(split, None),
        P(split, None, None),
        P(split),
        P(split, None),
        P(split, None),
        P(split, None),
        P(split, None),
    )
    return jax.shard_map(body, mesh=mesh, in_specs=in_specs, out_specs=P(split, None), check_vma=False)
```

time: 97.2 us -> 78.2 us (0.80)
  local copies, waits for them, and re-layouts: 13.8 us -> 2.47 us
  waiting for transfers between devices: 26.3 us -> 15.3 us
  starting transfers between devices: 22 us -> 16.6 us
  Pallas kernels: 15.2 us -> 20.3 us
  blocking collectives: 19.2 us -> 22.4 us
    ppermute x8, waiting for transfers between devices: 24.7 us -> 12.6 us  [along(): return lax.ppermute(x, 'branch', pairs)]
    unnamed x44 -> x30, local copies, waits for them, and re-layouts: 13.8 us -> 1.82 us
    pallas_call x3 -> x4, Pallas kernels: 13.6 us -> 18.7 us  [the longest x1 8.17 us: body(): pl.pallas_call(functools.partial(attend_kernel, split), out_shape=bf16(br...]
    ppermute x8, starting transfers between devices: 13.1 us -> 9.21 us  [along(): return lax.ppermute(x, 'branch', pairs)]
    all_to_all x1, blocking collectives: 19.2 us -> 22.4 us  [body(): lax.all_to_all(outputs, 'branch', split_axis=0, concat_axis=0, tiled=True)]
    all_to_all x1, starting transfers between devices: 7.39 us -> 4.97 us  [body(): lax.all_to_all(send, 'branch', split_axis=0, concat_axis=0, tiled=True)]
    all_to_all x1, waiting for transfers between devices: 0.01 us -> 1.13 us  [body(): lax.all_to_all(send, 'branch', split_axis=0, concat_axis=0, tiled=True)]
  transfers between devices with their start and end apart: 18 -> 18, of which waited for: 7 -> 8; matrix products, arithmetic and copies ran while one was open for 0% -> 2% of each run, Pallas kernels for 1% -> 11%
where the time goes in v2:
time: 78.2 us; the launch traced here: 77.9 us
  blocking collectives  22.4 us (29%)
  Pallas kernels  20.3 us (26%)
  starting transfers between devices  16.6 us (21%)
  waiting for transfers between devices  15.3 us (20%)
  local copies, waits for them, and re-layouts  2.47 us (3%)
    all_to_all x1, blocking collectives, body(): lax.all_to_all(outputs, 'branch', split_axis=0, concat_axis=0, tiled=True)  22.4 us
    ppermute x8, waiting for transfers between devices, along(): return lax.ppermute(x, 'branch', pairs)  12.6 us
    ppermute x8, starting transfers between devices, along(): return lax.ppermute(x, 'branch', pairs)  9.21 us
    pallas_call x1, Pallas kernels, body(): pl.pallas_call(functools.partial(attend_kernel, split), out_shape=bf16(br...  8.17 us
    pallas_call x1, Pallas kernels, body(): pl.pallas_call(functools.partial(gather_kernel, whole, branches), out_sha...  6.06 us
    all_to_all x1, starting transfers between devices, body(): lax.all_to_all(send, 'branch', split_axis=0, concat_axis=0, tiled=True)  4.97 us
    pallas_call x1, Pallas kernels, body(): pl.pallas_call(prep_kernel, out_shape=bf16(branches, slot_rows, HD), in_s...  2.81 us
    ppermute x9, starting transfers between devices, across(): return lax.ppermute(x, 'branch', [(i, i ^ 1) for i in range(branches)])  2.41 us
  transfers between devices with their start and end apart: 18, of which 8 were waited for; matrix products, arithmetic and copies ran while one was open for 2% of the time, Pallas kernels for 11%

profile of v2, /device:TPU:0, one launch (start us, length us, event | category | flops | bytes accessed | tf_op | source)
XLA Modules:
  0.0 77.9 jit_solution(2046418091561198622)
XLA Ops:
  0.0 1.7 %payload.1.after_hbm.refs_0_ = bf16[17,48,128]{2,1,0:T(8,128)(2,1)} custom-call(s32[1,16]{1,0:T(1,128)} %pick_hbm.1, s32[1,2]{1,0:T(1,128)} %bitcast.5, bf16[2,24,2048]{2,1,0:T(8,128)(2,1)} %shared_hbm.1), custom_call_target="tpu_custom_call" | custom-call | tf_op jit(solution)/shard_map/payload/pallas_call | solution.py:290
  1.7 3.1 %collective-permute-start = (bf16[17,48,128]{2,1,0:T(8,128)(2,1)}, bf16[17,48,128]{2,1,0:T(8,128)(2,1)S(1)}, u32[]{:S(2)}, u32[]{:S(2)}) collective-permute-start(bf16[17,48,128]{2,1,0:T(8,128)(2,1)} %payload.1.after_hbm.refs_0_), channel_id=1, source_target_pairs={{0,4},{1,5},{4,8},{5,9},{8,12},{9,13},{12,14},{13,15},{14,10},{15,... | collective-permute-start | bytes 626696 | tf_op jit(solution)/shard_map/ppermute | solution.py:313
  4.8 0.0 collective-permute-start.3
  4.8 5.3 %collective-permute-done.refs_1_ = bf16[17,48,128]{2,1,0:T(8,128)(2,1)S(1)} collective-permute-done((bf16[17,48,128]{2,1,0:T(8,128)(2,1)}, bf16[17,48,128]{2,1,0:T(8,128)(2,1)S(1)}, u32[]{:S(2)}, u32[]{:S(2)}) %collective-permute-start) | collective-permute-done | bytes 208928 | tf_op jit(solution)/shard_map/ppermute | solution.py:313
  10.1 1.8 %collective-permute-start.1 = (bf16[17,48,128]{2,1,0:T(8,128)(2,1)S(1)}, bf16[17,48,128]{2,1,0:T(8,128)(2,1)S(1)}, u32[]{:S(2)}, u32[]{:S(2)}) collective-permute-start(bf16[17,48,128]{2,1,0:T(8,128)(2,1)S(1)} %collective-permute-done.refs_1_), channel_id=1, source_target_pairs={{0,4},{1,5},{4,8},{5,9},{8,12},{9,13},{12,14},{13,15},{14,10},{15,... | collective-permute-start | bytes 626696 | tf_op jit(solution)/shard_map/ppermute | solution.py:313
  11.9 0.0 collective-permute-done.3.refs_2_
  11.9 0.2 collective-permute-start.4
  12.1 4.3 %collective-permute-done.1.refs_3_ = bf16[17,48,128]{2,1,0:T(8,128)(2,1)S(1)} collective-permute-done((bf16[17,48,128]{2,1,0:T(8,128)(2,1)S(1)}, bf16[17,48,128]{2,1,0:T(8,128)(2,1)S(1)}, u32[]{:S(2)}, u32[]{:S(2)}) %collective-permute-start.1) | collective-permute-done | bytes 208928 | tf_op jit(solution)/shard_map/ppermute | solution.py:313
  16.5 1.5 %collective-permute-start.2 = (bf16[17,48,128]{2,1,0:T(8,128)(2,1)S(1)}, bf16[17,48,128]{2,1,0:T(8,128)(2,1)S(1)}, u32[]{:S(2)}, u32[]{:S(2)}) collective-permute-start(bf16[17,48,128]{2,1,0:T(8,128)(2,1)S(1)} %collective-permute-done.1.refs_3_), channel_id=1, source_target_pairs={{0,4},{1,5},{4,8},{5,9},{8,12},{9,13},{12,14},{13,15},{14,10},{15,... | collective-permute-start | bytes 626696 | tf_op jit(solution)/shard_map/ppermute | solution.py:313
  17.9 0.0 collective-permute-done.4.refs_4_
  17.9 0.5 collective-permute-start.5
  18.5 2.8 %prep.1 = bf16[16,160,128]{2,1,0:T(8,128)(2,1)} custom-call(s32[16]{0:T(128)} %bitcast.3, bf16[16,8192]{1,0:T(8,128)(2,1)} %q_hbm.1, bf16[16,2048]{1,0:T(8,128)(2,1)} %kv_hbm.1, bf16[17,48,128]{2,1,0:T(8,128)(2,1)} %payload.1.after_hbm.refs_0_), custom_call_target="tpu_custom_call" | custom-call | bytes 1024 | tf_op jit(solution)/shard_map/prep/pallas_call | solution.py:318
  21.3 1.0 %collective-permute-done.2.refs_5_ = bf16[17,48,128]{2,1,0:T(8,128)(2,1)S(1)} collective-permute-done((bf16[17,48,128]{2,1,0:T(8,128)(2,1)S(1)}, bf16[17,48,128]{2,1,0:T(8,128)(2,1)S(1)}, u32[]{:S(2)}, u32[]{:S(2)}) %collective-permute-start.2) | collective-permute-done | bytes 208928 | tf_op jit(solution)/shard_map/ppermute | solution.py:313
  22.3 1.5 %collective-permute-done.5.refs_6_ = bf16[17,48,128]{2,1,0:T(8,128)(2,1)S(1)} collective-permute-done((bf16[17,48,128]{2,1,0:T(8,128)(2,1)S(1)}, bf16[17,48,128]{2,1,0:T(8,128)(2,1)S(1)}, u32[]{:S(2)}, u32[]{:S(2)}) %collective-permute-start.5) | collective-permute-done | bytes 208928 | tf_op jit(solution)/shard_map/ppermute | solution.py:313
  23.8 5.0 %all-to-all-start = ((bf16[16,160,128]{2,1,0:T(8,128)(2,1)}), bf16[16,160,128]{2,1,0:T(8,128)(2,1)}, u32[]{:S(2)}, u32[]{:S(2)}) async-start(bf16[16,160,128]{2,1,0:T(8,128)(2,1)} %prep.1), calls=%async_computation | async-start | bytes 1310720 | tf_op jit(solution)/shard_map/all_to_all | solution.py:345
  28.7 0.4 collective-permute-start.8
  29.1 0.2 collective-permute-start.10
  29.3 0.3 collective-permute-start.9
  29.6 0.2 collective-permute-start.11
  29.8 0.3 collective-permute-start.12
  30.1 0.3 collective-permute-done.8.refs_7_
  30.5 0.3 collective-permute-start.13
  30.8 0.0 collective-permute-done.10.refs_9_
  30.8 0.2 collective-permute-start.14
  31.0 0.7 pad_maximum_fusion
  31.7 0.0 collective-permute-done.9.refs_8_
  31.7 1.8 %collective-permute-start.6 = (bf16[9,48,128]{2,1,0:T(8,128)(2,1)}, bf16[9,48,128]{2,1,0:T(8,128)(2,1)}, u32[]{:S(2)}, u32[]{:S(2)}) collective-permute-start(bf16[9,48,128]{2,1,0:T(8,128)(2,1)} %pad_maximum_fusion), channel_id=1, source_target_pairs={{0,4},{1,5},{4,8},{5,9},{8,12},{9,13},{12,14},{13,15},{14,10},{15,... | collective-permute-start | bytes 331784 | tf_op jit(solution)/shard_map/ppermute | solution.py:313
  33.5 0.6 slice.11
  34.1 0.0 collective-permute-done.11.refs_10_
  34.1 0.3 collective-permute-start.7
  34.4 0.4 copy-done.11
  34.8 0.0 collective-permute-done.12.refs_11_
  34.8 0.0 collective-permute-done.13.refs_12_
  34.8 0.0 collective-permute-done.14.refs_13_
  34.9 0.6 copy-done.12
  35.5 0.1 copy-done.13
  35.6 0.7 copy-done.14
  36.3 6.1 %gather.1 = (bf16[8,1696,128]{2,1,0:T(8,128)(2,1)S(1)}, bf16[8,1696,128]{2,1,0:T(8,128)(2,1)}, f32[8,1696]{1,0:T(8,128)S(1)}) custom-call(s32[1]{0:T(128)} %bitcast.1.me_ref, s32[1,8]{1,0:T(1,128)S(1)} %copy-done.1, bf16[1,1024,1024]{2,1,0:T(8,128)(2,1)} %pk_hbm.1, bf16[1,1024,1024]{2,1,0:T(8,128)(2,1)} %pv_hbm.1, ...), custom_call_target="tpu_custom_call" | custom-call | bytes 8388608 | tf_op jit(solution)/shard_map/gather/pallas_call | solution.py:355
  42.3 0.5 collective-permute-done.7.refs_1_
  42.8 0.0 collective-permute-done.6.refs_0_
  42.8 0.0 collective-permute-start.15
  42.8 0.5 collective-permute-start.16
  43.3 1.3 %collective-permute-done.16.refs_3_ = bf16[8,48,128]{2,1,0:T(8,128)(2,1)} collective-permute-done((bf16[8,48,128]{2,1,0:T(8,128)(2,1)}, bf16[8,48,128]{2,1,0:T(8,128)(2,1)}, u32[]{:S(2)}, u32[]{:S(2)}) %collective-permute-start.16) | collective-permute-done | bytes 98336 | tf_op jit(solution)/shard_map/ppermute | solution.py:316
  44.6 0.0 collective-permute-done.15.refs_2_
  44.6 1.1 %all-to-all-done.recv_hbm = bf16[16,160,128]{2,1,0:T(8,128)(2,1)} async-done(((bf16[16,160,128]{2,1,0:T(8,128)(2,1)}), bf16[16,160,128]{2,1,0:T(8,128)(2,1)}, u32[]{:S(2)}, u32[]{:S(2)}) %all-to-all-start) | async-done | bytes 655392 | tf_op jit(solution)/shard_map/all_to_all | solution.py:345
  45.8 8.2 %attend.1 = bf16[16,128,128]{2,1,0:T(8,128)(2,1)S(1)} custom-call(s32[1]{0:T(128)} %bitcast.1.me_ref, bf16[8,1696,128]{2,1,0:T(8,128)(2,1)S(1)} %get-tuple-element.17.key_ref, f32[8,1696]{1,0:T(8,128)S(1)} %get-tuple-element.18.bias_ref, bf16[8,1696,128]{2,1,0:T(8,128)(2,1)} %get-tuple-element.19.value_hbm, bf16[16,160,128]{2,1,0:T(8,128)(2,1)} %all-to-all-done.recv_hbm, ...), custom_call_target="tpu_custom_call" | custom-call | flops 1912602624 | bytes 4194304 | tf_op jit(solution)/shard_map/attend/pallas_call | solution.py:375
  53.9 22.4 %all_to_all.10.back_ref = bf16[16,128,128]{2,1,0:T(8,128)(2,1)S(1)} all-to-all(bf16[16,128,128]{2,1,0:T(8,128)(2,1)S(1)} %attend.1), channel_id=1, replica_groups=mesh['groups'=2,'branch'=16] {'branch'}, dimensions={0} | all-to-all | bytes 1048576 | tf_op jit(solution)/shard_map/all_to_all | solution.py:398
  76.4 1.5 %post.1 = bf16[16,8192]{1,0:T(8,128)(2,1)} custom-call(s32[16]{0:T(128)S(1)} %bitcast.4, bf16[16,128,128]{2,1,0:T(8,128)(2,1)S(1)} %all_to_all.10.back_ref), custom_call_target="tpu_custom_call" | custom-call | tf_op jit(solution)/shard_map/post/pallas_call | solution.py:399
  (28 shorter events, 0.1 us)
Async XLA Ops:
  0.0 36.3 %copy-start.1 = (s32[1,8]{1,0:T(1,128)S(1)}, s32[1,8]{1,0:T(1,128)}, u32[]{:S(2)}) copy-start(s32[1,8]{1,0:T(1,128)} %mask_ref.1) | copy-start | bytes 100
  1.7 8.4 %collective-permute-start = (bf16[17,48,128]{2,1,0:T(8,128)(2,1)}, bf16[17,48,128]{2,1,0:T(8,128)(2,1)S(1)}, u32[]{:S(2)}, u32[]{:S(2)}) collective-permute-start(bf16[17,48,128]{2,1,0:T(8,128)(2,1)} %payload.1.after_hbm.refs_0_), channel_id=1, source_target_pairs={{0,4},{1,5},{4,8},{5,9},{8,12},{9,13},{12,14},{13,15},{14,10},{15,... | collective-permute-start | bytes 626696 | tf_op jit(solution)/shard_map/ppermute | solution.py:313
  4.8 7.1 %collective-permute-start.3 = (bf16[17,48,128]{2,1,0:T(8,128)(2,1)}, bf16[17,48,128]{2,1,0:T(8,128)(2,1)S(1)}, u32[]{:S(2)}, u32[]{:S(2)}) collective-permute-start(bf16[17,48,128]{2,1,0:T(8,128)(2,1)} %payload.1.after_hbm.refs_0_), channel_id=1, source_target_pairs={{0,2},{1,3},{4,0},{5,1},{8,4},{9,5},{12,8},{13,9},{14,12},{15,13},... | collective-permute-start | bytes 626696 | tf_op jit(solution)/shard_map/ppermute | solution.py:313
  10.1 24.7 %copy-start.4 = (bf16[17,48,128]{2,1,0:T(8,128)(2,1)}, bf16[17,48,128]{2,1,0:T(8,128)(2,1)S(1)}, u32[]{:S(2)}) copy-start(bf16[17,48,128]{2,1,0:T(8,128)(2,1)S(1)} %collective-permute-done.refs_1_) | copy-start | bytes 626692
  10.1 6.4 %collective-permute-start.1 = (bf16[17,48,128]{2,1,0:T(8,128)(2,1)S(1)}, bf16[17,48,128]{2,1,0:T(8,128)(2,1)S(1)}, u32[]{:S(2)}, u32[]{:S(2)}) collective-permute-start(bf16[17,48,128]{2,1,0:T(8,128)(2,1)S(1)} %collective-permute-done.refs_1_), channel_id=1, source_target_pairs={{0,4},{1,5},{4,8},{5,9},{8,12},{9,13},{12,14},{13,15},{14,10},{15,... | collective-permute-start | bytes 626696 | tf_op jit(solution)/shard_map/ppermute | solution.py:313
  11.9 22.9 %copy-start.5 = (bf16[17,48,128]{2,1,0:T(8,128)(2,1)}, bf16[17,48,128]{2,1,0:T(8,128)(2,1)S(1)}, u32[]{:S(2)}) copy-start(bf16[17,48,128]{2,1,0:T(8,128)(2,1)S(1)} %collective-permute-done.3.refs_2_) | copy-start | bytes 626692
  11.9 6.0 %collective-permute-start.4 = (bf16[17,48,128]{2,1,0:T(8,128)(2,1)S(1)}, bf16[17,48,128]{2,1,0:T(8,128)(2,1)S(1)}, u32[]{:S(2)}, u32[]{:S(2)}) collective-permute-start(bf16[17,48,128]{2,1,0:T(8,128)(2,1)S(1)} %collective-permute-done.3.refs_2_), channel_id=1, source_target_pairs={{0,2},{1,3},{4,0},{5,1},{8,4},{9,5},{12,8},{13,9},{14,12},{15,13},... | collective-permute-start | bytes 626696 | tf_op jit(solution)/shard_map/ppermute | solution.py:313
  16.5 18.4 %copy-start.6 = (bf16[17,48,128]{2,1,0:T(8,128)(2,1)}, bf16[17,48,128]{2,1,0:T(8,128)(2,1)S(1)}, u32[]{:S(2)}) copy-start(bf16[17,48,128]{2,1,0:T(8,128)(2,1)S(1)} %collective-permute-done.1.refs_3_) | copy-start | bytes 626692
  16.5 5.8 %collective-permute-start.2 = (bf16[17,48,128]{2,1,0:T(8,128)(2,1)S(1)}, bf16[17,48,128]{2,1,0:T(8,128)(2,1)S(1)}, u32[]{:S(2)}, u32[]{:S(2)}) collective-permute-start(bf16[17,48,128]{2,1,0:T(8,128)(2,1)S(1)} %collective-permute-done.1.refs_3_), channel_id=1, source_target_pairs={{0,4},{1,5},{4,8},{5,9},{8,12},{9,13},{12,14},{13,15},{14,10},{15,... | collective-permute-start | bytes 626696 | tf_op jit(solution)/shard_map/ppermute | solution.py:313
  17.9 16.9 %copy-start.7 = (bf16[17,48,128]{2,1,0:T(8,128)(2,1)}, bf16[17,48,128]{2,1,0:T(8,128)(2,1)S(1)}, u32[]{:S(2)}) copy-start(bf16[17,48,128]{2,1,0:T(8,128)(2,1)S(1)} %collective-permute-done.4.refs_4_) | copy-start | bytes 626692
  17.9 5.8 %collective-permute-start.5 = (bf16[17,48,128]{2,1,0:T(8,128)(2,1)S(1)}, bf16[17,48,128]{2,1,0:T(8,128)(2,1)S(1)}, u32[]{:S(2)}, u32[]{:S(2)}) collective-permute-start(bf16[17,48,128]{2,1,0:T(8,128)(2,1)S(1)} %collective-permute-done.4.refs_4_), channel_id=1, source_target_pairs={{0,2},{1,3},{4,0},{5,1},{8,4},{9,5},{12,8},{13,9},{14,12},{15,13},... | collective-permute-start | bytes 626696 | tf_op jit(solution)/shard_map/ppermute | solution.py:313
  22.3 12.6 %copy-start.2 = (bf16[17,48,128]{2,1,0:T(8,128)(2,1)}, bf16[17,48,128]{2,1,0:T(8,128)(2,1)S(1)}, u32[]{:S(2)}) copy-start(bf16[17,48,128]{2,1,0:T(8,128)(2,1)S(1)} %collective-permute-done.2.refs_5_) | copy-start | bytes 626692
  23.8 11.1 %copy-start.3 = (bf16[17,48,128]{2,1,0:T(8,128)(2,1)}, bf16[17,48,128]{2,1,0:T(8,128)(2,1)S(1)}, u32[]{:S(2)}) copy-start(bf16[17,48,128]{2,1,0:T(8,128)(2,1)S(1)} %collective-permute-done.5.refs_6_) | copy-start | bytes 626692
  23.8 22.0 %all-to-all-start = ((bf16[16,160,128]{2,1,0:T(8,128)(2,1)}), bf16[16,160,128]{2,1,0:T(8,128)(2,1)}, u32[]{:S(2)}, u32[]{:S(2)}) async-start(bf16[16,160,128]{2,1,0:T(8,128)(2,1)} %prep.1), calls=%async_computation | async-start | bytes 1310720 | tf_op jit(solution)/shard_map/all_to_all | solution.py:345
  28.7 1.7 %collective-permute-start.8 = (bf16[17,48,128]{2,1,0:T(8,128)(2,1)}, bf16[17,48,128]{2,1,0:T(8,128)(2,1)S(1)}, u32[]{:S(2)}, u32[]{:S(2)}) collective-permute-start(bf16[17,48,128]{2,1,0:T(8,128)(2,1)} %payload.1.after_hbm.refs_0_), channel_id=1, source_target_pairs={{0,1},{1,0},{2,3},{3,2},{4,5},{5,4},{6,7},{7,6},{8,9},{9,8},{10,11... | collective-permute-start | bytes 626696 | tf_op jit(solution)/shard_map/ppermute | solution.py:316
  29.1 1.7 %collective-permute-start.10 = (bf16[17,48,128]{2,1,0:T(8,128)(2,1)S(1)}, bf16[17,48,128]{2,1,0:T(8,128)(2,1)S(1)}, u32[]{:S(2)}, u32[]{:S(2)}) collective-permute-start(bf16[17,48,128]{2,1,0:T(8,128)(2,1)S(1)} %collective-permute-done.3.refs_2_), channel_id=1, source_target_pairs={{0,1},{1,0},{2,3},{3,2},{4,5},{5,4},{6,7},{7,6},{8,9},{9,8},{10,11... | collective-permute-start | bytes 626696 | tf_op jit(solution)/shard_map/ppermute | solution.py:316
  29.3 2.4 %collective-permute-start.9 = (bf16[17,48,128]{2,1,0:T(8,128)(2,1)S(1)}, bf16[17,48,128]{2,1,0:T(8,128)(2,1)S(1)}, u32[]{:S(2)}, u32[]{:S(2)}) collective-permute-start(bf16[17,48,128]{2,1,0:T(8,128)(2,1)S(1)} %collective-permute-done.refs_1_), channel_id=1, source_target_pairs={{0,1},{1,0},{2,3},{3,2},{4,5},{5,4},{6,7},{7,6},{8,9},{9,8},{10,11... | collective-permute-start | bytes 626696 | tf_op jit(solution)/shard_map/ppermute | solution.py:316
  29.6 4.5 %collective-permute-start.11 = (bf16[17,48,128]{2,1,0:T(8,128)(2,1)S(1)}, bf16[17,48,128]{2,1,0:T(8,128)(2,1)S(1)}, u32[]{:S(2)}, u32[]{:S(2)}) collective-permute-start(bf16[17,48,128]{2,1,0:T(8,128)(2,1)S(1)} %collective-permute-done.1.refs_3_), channel_id=1, source_target_pairs={{0,1},{1,0},{2,3},{3,2},{4,5},{5,4},{6,7},{7,6},{8,9},{9,8},{10,11... | collective-permute-start | bytes 626696 | tf_op jit(solution)/shard_map/ppermute | solution.py:316
  29.8 5.0 %collective-permute-start.12 = (bf16[17,48,128]{2,1,0:T(8,128)(2,1)S(1)}, bf16[17,48,128]{2,1,0:T(8,128)(2,1)S(1)}, u32[]{:S(2)}, u32[]{:S(2)}) collective-permute-start(bf16[17,48,128]{2,1,0:T(8,128)(2,1)S(1)} %collective-permute-done.4.refs_4_), channel_id=1, source_target_pairs={{0,1},{1,0},{2,3},{3,2},{4,5},{5,4},{6,7},{7,6},{8,9},{9,8},{10,11... | collective-permute-start | bytes 626696 | tf_op jit(solution)/shard_map/ppermute | solution.py:316
  30.5 3.7 %copy-start.8 = (bf16[17,48,128]{2,1,0:T(8,128)(2,1)}, bf16[17,48,128]{2,1,0:T(8,128)(2,1)S(1)}, u32[]{:S(2)}) copy-start(bf16[17,48,128]{2,1,0:T(8,128)(2,1)S(1)} %collective-permute-done.8.refs_7_) | copy-start | bytes 626692
  30.5 4.4 %collective-permute-start.13 = (bf16[17,48,128]{2,1,0:T(8,128)(2,1)S(1)}, bf16[17,48,128]{2,1,0:T(8,128)(2,1)S(1)}, u32[]{:S(2)}, u32[]{:S(2)}) collective-permute-start(bf16[17,48,128]{2,1,0:T(8,128)(2,1)S(1)} %collective-permute-done.2.refs_5_), channel_id=1, source_target_pairs={{0,1},{1,0},{2,3},{3,2},{4,5},{5,4},{6,7},{7,6},{8,9},{9,8},{10,11... | collective-permute-start | bytes 626696 | tf_op jit(solution)/shard_map/ppermute | solution.py:316
  30.8 3.6 %copy-start.9 = (bf16[17,48,128]{2,1,0:T(8,128)(2,1)}, bf16[17,48,128]{2,1,0:T(8,128)(2,1)S(1)}, u32[]{:S(2)}) copy-start(bf16[17,48,128]{2,1,0:T(8,128)(2,1)S(1)} %collective-permute-done.10.refs_9_) | copy-start | bytes 626692
  30.8 4.1 %collective-permute-start.14 = (bf16[17,48,128]{2,1,0:T(8,128)(2,1)S(1)}, bf16[17,48,128]{2,1,0:T(8,128)(2,1)S(1)}, u32[]{:S(2)}, u32[]{:S(2)}) collective-permute-start(bf16[17,48,128]{2,1,0:T(8,128)(2,1)S(1)} %collective-permute-done.5.refs_6_), channel_id=1, source_target_pairs={{0,1},{1,0},{2,3},{3,2},{4,5},{5,4},{6,7},{7,6},{8,9},{9,8},{10,11... | collective-permute-start | bytes 626696 | tf_op jit(solution)/shard_map/ppermute | solution.py:316
  31.7 2.7 %copy-start.10 = (bf16[17,48,128]{2,1,0:T(8,128)(2,1)}, bf16[17,48,128]{2,1,0:T(8,128)(2,1)S(1)}, u32[]{:S(2)}) copy-start(bf16[17,48,128]{2,1,0:T(8,128)(2,1)S(1)} %collective-permute-done.9.refs_8_) | copy-start | bytes 626692
  31.7 11.2 %collective-permute-start.6 = (bf16[9,48,128]{2,1,0:T(8,128)(2,1)}, bf16[9,48,128]{2,1,0:T(8,128)(2,1)}, u32[]{:S(2)}, u32[]{:S(2)}) collective-permute-start(bf16[9,48,128]{2,1,0:T(8,128)(2,1)} %pad_maximum_fusion), channel_id=1, source_target_pairs={{0,4},{1,5},{4,8},{5,9},{8,12},{9,13},{12,14},{13,15},{14,10},{15,... | collective-permute-start | bytes 331784 | tf_op jit(solution)/shard_map/ppermute | solution.py:313
  34.1 0.7 copy-start.11
  34.1 8.7 %collective-permute-start.7 = (bf16[8,48,128]{2,1,0:T(8,128)(2,1)}, bf16[8,48,128]{2,1,0:T(8,128)(2,1)}, u32[]{:S(2)}, u32[]{:S(2)}) collective-permute-start(bf16[8,48,128]{2,1,0:T(8,128)(2,1)} %slice.11), channel_id=1, source_target_pairs={{0,2},{1,3},{4,0},{5,1},{8,4},{9,5},{12,8},{13,9},{14,12},{15,13},... | collective-permute-start | bytes 294920 | tf_op jit(solution)/shard_map/ppermute | solution.py:313
  34.8 0.7 copy-start.12
  34.8 0.8 copy-start.13
  35.6 0.7 copy-start.14
  42.8 1.8 %collective-permute-start.15 = (bf16[9,48,128]{2,1,0:T(8,128)(2,1)}, bf16[9,48,128]{2,1,0:T(8,128)(2,1)}, u32[]{:S(2)}, u32[]{:S(2)}) collective-permute-start(bf16[9,48,128]{2,1,0:T(8,128)(2,1)} %collective-permute-done.6.refs_0_), channel_id=1, source_target_pairs={{0,1},{1,0},{2,3},{3,2},{4,5},{5,4},{6,7},{7,6},{8,9},{9,8},{10,11... | collective-permute-start | bytes 331784 | tf_op jit(solution)/shard_map/ppermute | solution.py:316
  42.8 1.8 %collective-permute-start.16 = (bf16[8,48,128]{2,1,0:T(8,128)(2,1)}, bf16[8,48,128]{2,1,0:T(8,128)(2,1)}, u32[]{:S(2)}, u32[]{:S(2)}) collective-permute-start(bf16[8,48,128]{2,1,0:T(8,128)(2,1)} %collective-permute-done.7.refs_1_), channel_id=1, source_target_pairs={{0,1},{1,0},{2,3},{3,2},{4,5},{5,4},{6,7},{7,6},{8,9},{9,8},{10,11... | collective-permute-start | bytes 294920 | tf_op jit(solution)/shard_map/ppermute | solution.py:316
  45.8 30.6 %copy-start = (s32[16,1]{0,1:T(1,128)S(1)}, s32[16,1]{0,1:T(1,128)}, u32[]{:S(2)}) copy-start(s32[16,1]{0,1:T(1,128)} %param.17) | copy-start | bytes 196

commit v3 on v2

--- a/solution.py
+++ b/solution.py
@@ -37,17 +37,19 @@
     for move in moves:
         move.wait()
     live = results * rows
-    lane = lax.broadcasted_iota(jnp.int32, (live, HD), 1)
-    meta = jnp.zeros((live, HD), jnp.int32)
+    lane = lax.broadcasted_iota(jnp.int32, (TILE, HD), 1)
+    meta = jnp.zeros((TILE, HD), jnp.int32)
     for b in range(branches):
         meta = jnp.where(lane == b, pick_ref[0, b], meta)
     for r in range(results):
         meta = jnp.where(lane == branches + r, len_ref[0, r], meta)
     slabs = width // HD
-    out_ref[slabs] = meta.astype(jnp.float32).astype(jnp.bfloat16)
+    middle = slabs // 2 * live
+    out_ref[middle : middle + TILE, :] = meta.astype(jnp.float32).astype(jnp.bfloat16)
     for j in range(slabs):
         part = shared_ref[:, :, j * HD : (j + 1) * HD].astype(jnp.float32)
-        out_ref[j] = part.reshape(live, HD).astype(jnp.bfloat16)
+        at = j * live + (TILE if 2 * j >= slabs else 0)
+        out_ref[at : at + live, :] = part.reshape(live, HD).astype(jnp.bfloat16)
 
 
 def place_rows(owner_ref, index_ref, count_ref):
@@ -112,108 +114,123 @@
     return start
 
 
-def bias_of(meta, me, branches, live):
+def picked(meta, me, branches):
     lane = lax.broadcasted_iota(jnp.int32, (1, HD), 1)
-    column = lax.broadcasted_iota(jnp.int32, (1, live), 1)
+    meta = meta.astype(jnp.float32)[0:1, :]
+    pick = jnp.sum(jnp.where(lane == me, meta, 0.0)).astype(jnp.int32)
+    length = jnp.sum(jnp.where(lane == branches + pick, meta, 0.0)).astype(jnp.int32)
+    return pick, jnp.where(pick < 0, 0, length)
+
+
+def rows_picked(slab, pick):
+    both = slab.astype(jnp.float32)
+    rows = slab.shape[0] // 2
+    return jnp.where(pick == 0, both[0:rows], both[rows:])
+
+
+def gather_kernel(whole, split, me_ref, mask_ref, pk_hbm, pv_hbm, *refs):
+    sources = refs[:whole]
+    key_ref, value_hbm, bias_ref, value_ref, taken_ref, *blocks, sems = refs[whole:]
+    slabs, room, _ = taken_ref.shape
+    kv_heads = slabs // 2
+    prompt = pk_hbm.shape[1]
+    live = (blocks[0].shape[0] - TILE) // slabs
     rows = live // 2
-    pick = jnp.sum(jnp.where(lane == me, meta, 0.0), axis=1, keepdims=True)
-    seen = jnp.zeros((1, live), jnp.bool_)
-    for r in range(2):
-        length = jnp.sum(jnp.where(lane == branches + r, meta, 0.0), axis=1, keepdims=True)
-        place = (column - r * rows).astype(jnp.float32)
-        seen = seen | ((place >= 0.0) & (place < length) & (pick == float(r)))
-    return jnp.where(seen, 0.0, NONE)
-
-
-def gather_kernel(whole, branches, me_ref, mask_ref, pk_hbm, pv_hbm, *refs):
-    blocks = refs[:whole]
-    key_ref, value_hbm, bias_ref, value_ref, meta_ref, sems = refs[whole:]
-    kv_heads = key_ref.shape[0]
-    prompt = pk_hbm.shape[1]
-    live = meta_ref.shape[1]
+    branches = whole + split
+    middle = kv_heads * live
     start = starter(sems)
-    moves, metas = [], []
-    for n, block in enumerate(blocks):
-        span = pl.ds(prompt + n * live, live)
-        metas.append(start(block.at[2 * kv_heads], meta_ref.at[n]))
-        moves.append(start(block.at[kv_heads : 2 * kv_heads], value_ref.at[:, span, :]))
-        moves.append(start(block.at[0:kv_heads], key_ref.at[:, span, :]))
+    moves = [start(source, target) for source, target in zip(sources, blocks)]
+    wide = []
     for g in range(kv_heads):
         lanes = pl.ds(g * HD, HD)
-        moves.append(start(pv_hbm.at[0, :, lanes], value_ref.at[g, pl.ds(0, prompt), :]))
-        moves.append(start(pk_hbm.at[0, :, lanes], key_ref.at[g, pl.ds(0, prompt), :]))
-    for copy in metas:
+        wide.append(start(pv_hbm.at[0, :, lanes], value_ref.at[g, pl.ds(0, prompt), :]))
+        wide.append(start(pk_hbm.at[0, :, lanes], key_ref.at[g, pl.ds(0, prompt), :]))
+    column = lax.broadcasted_iota(jnp.int32, (1, room), 1)
+    seen = jnp.zeros((1, room), jnp.bool_)
+    taken_ref[...] = jnp.zeros(taken_ref.shape, jnp.float32)
+    for copy in moves:
         copy.wait()
-    seen = mask_ref.shape[1]
+    slot = jnp.int32(0)
+    for block in blocks:
+        pick, length = picked(block[middle : middle + TILE, :], me_ref[0], branches)
+        at = pl.multiple_of(jnp.minimum(slot * rows, room - rows), 8)
+        place = column - at
+        seen = seen | ((place >= 0) & (place < length))
+
+        @pl.when(pick >= 0)
+        def _(block=block, pick=pick, at=at):
+            for j in range(slabs):
+                base = j * live + (TILE if j >= kv_heads else 0)
+                taken_ref[j, pl.ds(at, rows), :] = rows_picked(block[base : base + live, :], pick)
+
+        slot = slot + (pick >= 0).astype(jnp.int32)
+    for g in range(kv_heads):
+        key_ref[g, prompt : prompt + room, :] = taken_ref[g].astype(jnp.bfloat16)
+        value_ref[g, prompt : prompt + room, :] = taken_ref[kv_heads + g].astype(jnp.bfloat16)
+    blocks_seen = mask_ref.shape[1]
     biases = [
-        jnp.full((1, prompt // seen), jnp.where(mask_ref[0, j] > 0, 0.0, NONE)) for j in range(seen)
+        jnp.full((1, prompt // blocks_seen), jnp.where(mask_ref[0, j] > 0, 0.0, NONE))
+        for j in range(blocks_seen)
     ]
-    for n in range(whole):
-        meta = meta_ref[n, 0:TILE, :].astype(jnp.float32)[0:1, :]
-        biases.append(bias_of(meta, me_ref[0], branches, live))
-    bias = jnp.concatenate(biases, axis=1)
-    bias_ref[...] = jnp.broadcast_to(bias, bias_ref.shape)
-    for copy in moves:
+    bias = jnp.concatenate(biases + [jnp.where(seen, 0.0, NONE)], axis=1)
+    bias_ref[...] = bias
+    for copy in wide:
         copy.wait()
     leaving = start(value_ref, value_hbm)
     leaving.wait()
 
 
-def attend_kernel(
-    split, me_ref, key_ref, bias_ref, value_hbm, recv_hbm, *refs
-):
-    out_ref, late_key_ref, late_value_ref, first_ref, second_ref, value_ref, recv_ref = refs[
-        2 * split : 2 * split + 7
-    ]
-    halves, sems = refs[2 * split + 7 : -1], refs[-1]
-    kv_heads = key_ref.shape[0]
+def attend_kernel(split, me_ref, key_ref, bias_ref, recv_ref, value_hbm, *refs):
+    out_ref, late_key_ref, late_value_ref, first_ref, second_ref, value_ref, *halves, sems = refs[2 * split :]
+    kv_heads, early, _ = key_ref.shape
     start = starter(sems)
-    rows_move = start(recv_hbm, recv_ref)
     half_moves = [start(source, target) for source, target in zip(refs[: 2 * split], halves)]
     value_moves = [start(value_hbm.at[g], value_ref.at[g]) for g in range(kv_heads)]
     branches = recv_ref.shape[0]
     heads = kv_heads * GRP
     width = branches * CAP
-    early = key_ref.shape[1]
     late = late_key_ref.shape[1]
-    live = halves[0].shape[1]
-    far = split * live
-
+    live = halves[1].shape[0] // kv_heads
+    far = live // 2
+    tail = late - width - split * far
+    main = early - tail
     chunk = min(branches, 16)
     count = chunk * TILE
 
     def score(g, base, target):
         queries = recv_ref[pl.ds(base, chunk), g * TILE : (g + 1) * TILE, :].reshape(count, HD)
-        target[:, 0:early] = dot_nt(queries, key_ref[g]) + bias_ref[0:1, :]
-
-    rows_move.wait()
+        target[:, 0:main] = dot_nt(queries, key_ref[g, 0:main, :]) + bias_ref[0:1, 0:main]
+
     if branches == chunk:
         score(0, 0, first_ref)
     for copy in half_moves:
         copy.wait()
-
-    late_bias = [
-        bias_of(halves[2 * n][kv_heads, 0:TILE, :].astype(jnp.float32)[0:1, :], me_ref[0], branches, live)
-        for n in range(split)
-    ]
-    late_bias = jnp.concatenate(late_bias + [jnp.zeros((1, width), jnp.float32)], axis=1)
     size = branches * TILE
     place = lax.broadcasted_iota(jnp.int32, (size, size), 1)
     wanted = lax.broadcasted_iota(jnp.int32, (size, size), 0)
     choose = jnp.where(place == lax.rem(wanted, width) * kv_heads + wanted // width, 1.0, 0.0).astype(jnp.bfloat16)
-    for which, target in ((0, late_key_ref), (1, late_value_ref)):
+    unique = []
+    for which in range(2):
         first = heads * CAP + which * TILE
         rows = recv_ref[:, first : first + TILE, :].reshape(size, HD)
-        rows = jnp.dot(choose, rows, preferred_element_type=jnp.float32).astype(jnp.bfloat16)
-        target[:, far:late, :] = rows.reshape(kv_heads, width, HD)
-        for n in range(split):
-            target[:, n * live : (n + 1) * live, :] = halves[2 * n + which][0:kv_heads]
+        unique.append(jnp.dot(choose, rows, preferred_element_type=jnp.float32).reshape(kv_heads, width, HD))
+    for copy in value_moves:
+        copy.wait()
+    choices = [picked(halves[2 * n][kv_heads * live :, :], me_ref[0], branches) for n in range(split)]
+    for which, source, target in ((0, key_ref, late_key_ref), (1, value_ref, late_value_ref)):
+        for g in range(kv_heads):
+            rows = [rows_picked(halves[2 * n + which][g * live : (g + 1) * live, :], choices[n][0]) for n in range(split)]
+            if tail:
+                rows = [source[g, main:early, :].astype(jnp.float32)] + rows
+            target[g] = jnp.concatenate(rows + [unique[which][g]], axis=0).astype(jnp.bfloat16)
     one = jnp.where(lax.broadcasted_iota(jnp.int32, (TILE, HD), 1) == 0, 1.0, 0.0).astype(jnp.bfloat16)
     absent = dot_nt(one, late_key_ref[0])[0:1, :] > ABSENT / 2
-    for copy in value_moves:
-        copy.wait()
-
-    column = lax.broadcasted_iota(jnp.int32, (count, late), 1) - far
+    spot = lax.broadcasted_iota(jnp.int32, (1, far), 1)
+    late_bias = [jnp.where(spot < length, 0.0, NONE) for _, length in choices]
+    if tail:
+        late_bias = [bias_ref[0:1, main:early]] + late_bias
+    late_bias = jnp.concatenate(late_bias + [jnp.zeros((1, width), jnp.float32)], axis=1)
+    column = lax.broadcasted_iota(jnp.int32, (count, late), 1) - (late - width)
     own_slot = lax.broadcasted_iota(jnp.int32, (count, late), 0) // GRP
 
     def run(base):
@@ -221,7 +238,7 @@
 
         def score_late(g, target):
             queries = recv_ref[pl.ds(base, chunk), g * TILE : (g + 1) * TILE, :].reshape(count, HD)
-            target[:, early : early + late] = dot_nt(queries, late_key_ref[g]) + late_hidden
+            target[:, main : main + late] = dot_nt(queries, late_key_ref[g]) + late_hidden
 
         def finish(g, source):
             scores = source[...]
@@ -229,8 +246,8 @@
             weights = jnp.exp2((scores - largest) * FACTOR)
             total = jnp.sum(weights, axis=1, keepdims=True)
             probs = weights.astype(jnp.bfloat16)
-            mixed = jnp.dot(probs[:, 0:early], value_ref[g], preferred_element_type=jnp.float32)
-            mixed = mixed + jnp.dot(probs[:, early:], late_value_ref[g], preferred_element_type=jnp.float32)
+            mixed = jnp.dot(probs[:, 0:main], value_ref[g, 0:main, :], preferred_element_type=jnp.float32)
+            mixed = mixed + jnp.dot(probs[:, main:], late_value_ref[g], preferred_element_type=jnp.float32)
             result = (mixed / total).astype(jnp.bfloat16)
             out_ref[pl.ds(base, chunk), g * TILE : (g + 1) * TILE, :] = result.reshape(chunk, TILE, HD)
 
@@ -289,7 +306,7 @@
 
     block = pl.pallas_call(
         payload_kernel,
-        out_shape=bf16(2 * kv_heads + 1, live, HD),
+        out_shape=bf16(2 * kv_heads * live + TILE, HD),
         in_specs=[ANY] * 3,
         out_specs=VMEM,
         scratch_shapes=[
@@ -336,65 +353,70 @@
 
     blocks = [block]
     ahead = behind = block
-    recv = None
     for step in range(chips // 2 - 1):
         ahead, behind = along(ahead, 1), along(behind, -1)
         blocks += [ahead, behind]
-        if step == chips // 2 - 2:
-            send, ahead, behind = lax.optimization_barrier((send, ahead, behind))
-            recv = lax.all_to_all(send, "branch", split_axis=0, concat_axis=0, tiled=True)
-    upper = jnp.concatenate([ahead[:kv_heads], ahead[2 * kv_heads :]], axis=0)
-    halves = [along(upper, 1), along(behind[kv_heads : 2 * kv_heads], -1)]
+        if step == 0:
+            send, ahead = lax.optimization_barrier((send, ahead))
+    send, ahead, behind = lax.optimization_barrier((send, ahead, behind))
+    recv = lax.all_to_all(send, "branch", split_axis=0, concat_axis=0, tiled=True)
+    cut = kv_heads * live + TILE
+    halves = [along(ahead[:cut], 1), along(behind[cut:], -1)]
     blocks = blocks + [across(x) for x in blocks]
     me = jnp.full((1,), lax.axis_index("branch"), jnp.int32)
     prompt = prompt_k.shape[1]
     whole, split = len(blocks), 2
-    early = prompt + whole * live
-    late = split * live + CAP * branches
-    rows = CAP * branches * GRP
+    room = branches * 3 // 4 * result_rows
+    early = prompt + room
+    width = CAP * branches
+    tail = early % HD
+    chunk_rows = min(branches, 16) * TILE
+    rows = width * GRP
+    arrays = [pltpu.with_memory_space_constraint(x, pltpu.HBM) for x in (prompt_k, prompt_v, *blocks)]
     keys, values, bias = pl.pallas_call(
-        functools.partial(gather_kernel, whole, branches),
+        functools.partial(gather_kernel, whole, split),
         out_shape=(
             pltpu.VMEM((kv_heads, early, HD), jnp.bfloat16),
             pltpu.HBM((kv_heads, early, HD), jnp.bfloat16),
-            pltpu.VMEM((8, early), jnp.float32),
+            pltpu.VMEM((1, early), jnp.float32),
         ),
-        in_specs=[SMEM, SMEM] + [ANY] * (2 + whole),
+        in_specs=[SMEM, SMEM] + [ANY] * len(arrays),
         out_specs=(VMEM, ANY, VMEM),
         scratch_shapes=[
             pltpu.VMEM((kv_heads, early, HD), jnp.bfloat16),
-            pltpu.VMEM((whole, live, HD), jnp.bfloat16),
-            pltpu.SemaphoreType.DMA((3 * whole + 2 * kv_heads + 1,)),
+            pltpu.VMEM((2 * kv_heads, room, HD), jnp.float32),
+            *[pltpu.VMEM(x.shape, jnp.bfloat16) for x in arrays[2:]],
+            pltpu.SemaphoreType.DMA((len(arrays) - 2 + 2 * kv_heads + 1,)),
         ],
-        compiler_params=grant(16),
+        compiler_params=grant(40 if branches > 16 else 20),
         cost_estimate=pl.CostEstimate(flops=0, bytes_accessed=8 * prompt_k.size, transcendentals=0),
         name="gather",
-    )(me, prompt_mask, *[pltpu.with_memory_space_constraint(x, pltpu.HBM) for x in (prompt_k, prompt_v, *blocks)])
+    )(me, prompt_mask, *arrays)
     halves, keys = lax.optimization_barrier((halves, keys))
     halves = halves + [across(x) for x in halves]
+    late = tail + split * result_rows + width
     outputs = pl.pallas_call(
         functools.partial(attend_kernel, split),
         out_shape=bf16(branches, CAP * heads, HD),
-        in_specs=[SMEM, VMEM, VMEM] + [ANY] * (2 + 2 * split),
+        in_specs=[SMEM, VMEM, VMEM, VMEM] + [ANY] * (1 + 2 * split),
         out_specs=VMEM,
         scratch_shapes=[
             pltpu.VMEM((kv_heads, late, HD), jnp.bfloat16),
             pltpu.VMEM((kv_heads, late, HD), jnp.bfloat16),
-            pltpu.VMEM((min(branches, 16) * TILE, early + late), jnp.float32),
-            pltpu.VMEM((min(branches, 16) * TILE, early + late), jnp.float32),
+            pltpu.VMEM((chunk_rows, early - tail + late), jnp.float32),
+            pltpu.VMEM((chunk_rows, early - tail + late), jnp.float32),
             pltpu.VMEM((kv_heads, early, HD), jnp.bfloat16),
-            pltpu.VMEM(recv.shape, jnp.bfloat16),
             *[pltpu.VMEM(x.shape, jnp.bfloat16) for x in halves],
-            pltpu.SemaphoreType.DMA((1 + 2 * split + kv_heads,)),
+            pltpu.SemaphoreType.DMA((2 * split + kv_heads,)),
         ],
         compiler_params=grant(40),
         cost_estimate=pl.CostEstimate(
-            flops=4 * kv_heads * rows * HD * (early + late),
+            flops=4 * kv_heads * rows * HD * (early + width),
             bytes_accessed=4 * prompt_k.size,
-            transcendentals=kv_heads * rows * (early + late),
+            transcendentals=kv_heads * rows * (early + width),
         ),
         name="attend",
-    )(me, keys, bias, *[pltpu.with_memory_space_constraint(x, pltpu.HBM) for x in (values, recv, *halves)])
+    )(me, keys, bias, recv, *[pltpu.with_memory_space_constraint(x, pltpu.HBM) for x in (values, *halves)])
     back = lax.all_to_all(outputs, "branch", split_axis=0, concat_axis=0, tiled=True)
     return pl.pallas_call(
         post_kernel,

time: 78.2 us -> 76.7 us (0.981)
  waiting for transfers between devices: 15.3 us -> 13.4 us
    pallas_call x2, Pallas kernels: 7.76 us -> 9.6 us  [the longest x1 7.91 us: body(): pl.pallas_call(functools.partial(gather_kernel, whole, split), out_shape=...]
    pallas_call x1, Pallas kernels: 8.17 us -> 6.65 us  [body(): pl.pallas_call(functools.partial(attend_kernel, split), out_shape=bf16(br...]
    ppermute x8, waiting for transfers between devices: 12.6 us -> 11.6 us  [along(): return lax.ppermute(x, 'branch', pairs)]
    all_to_all x1, waiting for transfers between devices: 1.13 us -> 0.29 us  [body(): lax.all_to_all(send, 'branch', split_axis=0, concat_axis=0, tiled=True)]
    unnamed x30 -> x34, local copies, waits for them, and re-layouts: 1.82 us -> 1.76 us
  transfers between devices with their start and end apart: 18 -> 18, of which waited for: 8 -> 7; matrix products, arithmetic and copies ran while one was open for 2% -> 2% of each run, Pallas kernels for 11% -> 14%
where the time goes in v3:
time: 76.7 us; the launch traced here: 76.3 us
  blocking collectives  22.5 us (29%)
  Pallas kernels  20.6 us (27%)
  starting transfers between devices  16.6 us (22%)
  waiting for transfers between devices  13.4 us (17%)
  local copies, waits for them, and re-layouts  3.03 us (4%)
    all_to_all x1, blocking collectives, body(): lax.all_to_all(outputs, 'branch', split_axis=0, concat_axis=0, tiled=True)  22.5 us
    ppermute x8, waiting for transfers between devices, along(): return lax.ppermute(x, 'branch', pairs)  11.6 us
    ppermute x8, starting transfers between devices, along(): return lax.ppermute(x, 'branch', pairs)  9.16 us
    pallas_call x1, Pallas kernels, body(): pl.pallas_call(functools.partial(gather_kernel, whole, split), out_shape=...  7.91 us
    pallas_call x1, Pallas kernels, body(): pl.pallas_call(functools.partial(attend_kernel, split), out_shape=bf16(br...  6.65 us
    all_to_all x1, starting transfers between devices, body(): lax.all_to_all(send, 'branch', split_axis=0, concat_axis=0, tiled=True)  4.93 us
    pallas_call x1, Pallas kernels, body(): pl.pallas_call(prep_kernel, out_shape=bf16(branches, slot_rows, HD), in_s...  2.8 us
    ppermute x9, starting transfers between devices, across(): return lax.ppermute(x, 'branch', [(i, i ^ 1) for i in range(branches)])  2.51 us
  transfers between devices with their start and end apart: 18, of which 7 were waited for; matrix products, arithmetic and copies ran while one was open for 2% of the time, Pallas kernels for 14%

profile of v3, /device:TPU:0, one launch (start us, length us, event | category | flops | bytes accessed | tf_op | source)
XLA Modules:
  0.0 76.3 jit_solution(16861045944031847192)
XLA Ops:
  0.0 1.7 %payload.1.after_hbm.refs_0_ = bf16[784,128]{1,0:T(8,128)(2,1)} custom-call(s32[1,16]{1,0:T(1,128)} %pick_hbm.1, s32[1,2]{1,0:T(1,128)} %bitcast.5, bf16[2,24,2048]{2,1,0:T(8,128)(2,1)} %shared_hbm.1), custom_call_target="tpu_custom_call" | custom-call | tf_op jit(solution)/shard_map/payload/pallas_call | solution.py:307
  1.7 3.1 %collective-permute-start = (bf16[784,128]{1,0:T(8,128)(2,1)}, bf16[784,128]{1,0:T(8,128)(2,1)S(1)}, u32[]{:S(2)}, u32[]{:S(2)}) collective-permute-start(bf16[784,128]{1,0:T(8,128)(2,1)} %payload.1.after_hbm.refs_0_), channel_id=1, source_target_pairs={{0,4},{1,5},{4,8},{5,9},{8,12},{9,13},{12,14},{13,15},{14,10},{15,... | collective-permute-start | bytes 602120 | tf_op jit(solution)/shard_map/ppermute | solution.py:330
  4.8 0.0 collective-permute-start.3
  4.8 2.8 %prep.1 = bf16[16,160,128]{2,1,0:T(8,128)(2,1)} custom-call(s32[16]{0:T(128)} %bitcast.3, bf16[16,8192]{1,0:T(8,128)(2,1)} %q_hbm.1, bf16[16,2048]{1,0:T(8,128)(2,1)} %kv_hbm.1, bf16[784,128]{1,0:T(8,128)(2,1)} %payload.1.after_hbm.refs_0_), custom_call_target="tpu_custom_call" | custom-call | bytes 1024 | tf_op jit(solution)/shard_map/prep/pallas_call | solution.py:335
  7.6 2.3 %collective-permute-done.refs_1_ = bf16[784,128]{1,0:T(8,128)(2,1)S(1)} collective-permute-done((bf16[784,128]{1,0:T(8,128)(2,1)}, bf16[784,128]{1,0:T(8,128)(2,1)S(1)}, u32[]{:S(2)}, u32[]{:S(2)}) %collective-permute-start) | collective-permute-done | bytes 200736 | tf_op jit(solution)/shard_map/ppermute | solution.py:330
  9.9 1.8 %collective-permute-start.1 = (bf16[784,128]{1,0:T(8,128)(2,1)S(1)}, bf16[784,128]{1,0:T(8,128)(2,1)S(1)}, u32[]{:S(2)}, u32[]{:S(2)}) collective-permute-start(bf16[784,128]{1,0:T(8,128)(2,1)S(1)} %collective-permute-done.refs_1_), channel_id=1, source_target_pairs={{0,4},{1,5},{4,8},{5,9},{8,12},{9,13},{12,14},{13,15},{14,10},{15,... | collective-permute-start | bytes 602120 | tf_op jit(solution)/shard_map/ppermute | solution.py:330
  11.7 0.0 collective-permute-done.3.refs_2_
  11.7 0.2 collective-permute-start.4
  12.0 4.1 %collective-permute-done.1.refs_3_ = bf16[784,128]{1,0:T(8,128)(2,1)S(1)} collective-permute-done((bf16[784,128]{1,0:T(8,128)(2,1)S(1)}, bf16[784,128]{1,0:T(8,128)(2,1)S(1)}, u32[]{:S(2)}, u32[]{:S(2)}) %collective-permute-start.1) | collective-permute-done | bytes 200736 | tf_op jit(solution)/shard_map/ppermute | solution.py:330
  16.1 1.5 %collective-permute-start.2 = (bf16[784,128]{1,0:T(8,128)(2,1)S(1)}, bf16[784,128]{1,0:T(8,128)(2,1)S(1)}, u32[]{:S(2)}, u32[]{:S(2)}) collective-permute-start(bf16[784,128]{1,0:T(8,128)(2,1)S(1)} %collective-permute-done.1.refs_3_), channel_id=1, source_target_pairs={{0,4},{1,5},{4,8},{5,9},{8,12},{9,13},{12,14},{13,15},{14,10},{15,... | collective-permute-start | bytes 602120 | tf_op jit(solution)/shard_map/ppermute | solution.py:330
  17.6 0.0 collective-permute-done.4.refs_4_
  17.6 0.5 collective-permute-start.5
  18.1 3.7 %collective-permute-done.2.refs_5_ = bf16[784,128]{1,0:T(8,128)(2,1)S(1)} collective-permute-done((bf16[784,128]{1,0:T(8,128)(2,1)S(1)}, bf16[784,128]{1,0:T(8,128)(2,1)S(1)}, u32[]{:S(2)}, u32[]{:S(2)}) %collective-permute-start.2) | collective-permute-done | bytes 200736 | tf_op jit(solution)/shard_map/ppermute | solution.py:330
  21.8 1.5 %collective-permute-done.5.refs_6_ = bf16[784,128]{1,0:T(8,128)(2,1)S(1)} collective-permute-done((bf16[784,128]{1,0:T(8,128)(2,1)S(1)}, bf16[784,128]{1,0:T(8,128)(2,1)S(1)}, u32[]{:S(2)}, u32[]{:S(2)}) %collective-permute-start.5) | collective-permute-done | bytes 200736 | tf_op jit(solution)/shard_map/ppermute | solution.py:330
  23.3 4.9 %all-to-all-start = ((bf16[16,160,128]{2,1,0:T(8,128)(2,1)}), bf16[16,160,128]{2,1,0:T(8,128)(2,1)S(1)}, u32[]{:S(2)}, u32[]{:S(2)}) async-start(bf16[16,160,128]{2,1,0:T(8,128)(2,1)} %prep.1), calls=%async_computation | async-start | bytes 1310720 | tf_op jit(solution)/shard_map/all_to_all | solution.py:362
  28.2 0.4 collective-permute-start.8
  28.7 0.2 collective-permute-start.10
  28.8 0.3 collective-permute-start.9
  29.2 0.2 collective-permute-start.11
  29.3 0.3 collective-permute-start.12
  29.7 0.3 collective-permute-done.8.refs_7_
  30.0 0.3 collective-permute-start.13
  30.3 0.0 collective-permute-done.10.refs_9_
  30.3 0.2 collective-permute-start.14
  30.5 0.6 slice.6
  31.1 0.0 collective-permute-done.9.refs_8_
  31.1 1.9 %collective-permute-start.6 = (bf16[400,128]{1,0:T(8,128)(2,1)}, bf16[400,128]{1,0:T(8,128)(2,1)}, u32[]{:S(2)}, u32[]{:S(2)}) collective-permute-start(bf16[400,128]{1,0:T(8,128)(2,1)} %slice.6), channel_id=1, source_target_pairs={{0,4},{1,5},{4,8},{5,9},{8,12},{9,13},{12,14},{13,15},{14,10},{15,... | collective-permute-start | bytes 307208 | tf_op jit(solution)/shard_map/ppermute | solution.py:330
  33.0 0.6 slice.7
  33.6 0.0 collective-permute-done.11.refs_10_
  33.6 0.2 collective-permute-start.7
  33.8 0.0 collective-permute-done.12.refs_11_
  33.8 0.0 collective-permute-done.13.refs_12_
  33.8 0.0 collective-permute-done.14.refs_13_
  33.9 0.4 copy-done.11
  34.3 0.2 copy-done.12
  34.5 0.1 copy-done.13
  34.6 0.7 copy-done.14
  35.3 7.9 %gather.1 = (bf16[8,1312,128]{2,1,0:T(8,128)(2,1)S(1)}, bf16[8,1312,128]{2,1,0:T(8,128)(2,1)}, f32[1,1312]{1,0:T(1,128)S(1)}) custom-call(s32[1]{0:T(128)} %bitcast.1.me_ref, s32[1,8]{1,0:T(1,128)S(1)} %copy-done.1, bf16[1,1024,1024]{2,1,0:T(8,128)(2,1)} %pk_hbm.1, bf16[1,1024,1024]{2,1,0:T(8,128)(2,1)} %pv_hbm.1, ...), custom_call_target="tpu_custom_call" | custom-call | bytes 8388608 | tf_op jit(solution)/shard_map/gather/pallas_call | solution.py:376
  43.2 0.0 collective-permute-done.6.refs_0_
  43.2 0.1 collective-permute-start.15
  43.3 0.5 collective-permute-start.16
  43.8 1.2 %collective-permute-done.16.refs_3_ = bf16[384,128]{1,0:T(8,128)(2,1)S(1)} collective-permute-done((bf16[384,128]{1,0:T(8,128)(2,1)}, bf16[384,128]{1,0:T(8,128)(2,1)S(1)}, u32[]{:S(2)}, u32[]{:S(2)}) %collective-permute-start.16) | collective-permute-done | bytes 98336 | tf_op jit(solution)/shard_map/ppermute | solution.py:333
  44.9 0.3 all-to-all-done.recv_ref
  45.2 0.3 copy-done.16
  45.6 0.0 copy-done.15
  45.6 6.7 %attend.1 = bf16[16,128,128]{2,1,0:T(8,128)(2,1)S(1)} custom-call(s32[1]{0:T(128)} %bitcast.1.me_ref, bf16[8,1312,128]{2,1,0:T(8,128)(2,1)S(1)} %get-tuple-element.21.key_ref, f32[1,1312]{1,0:T(1,128)S(1)} %get-tuple-element.22.bias_ref, bf16[16,160,128]{2,1,0:T(8,128)(2,1)S(1)} %all-to-all-done.recv_ref, bf16[8,1312,128]{2,1,0:T(8,128)(2,1)} %get-tuple-element.24.value_hbm, ...), custom_call_target="tpu_custom_call" | custom-call | flops 1409286144 | bytes 4194304 | tf_op jit(solution)/shard_map/attend/pallas_call | solution.py:398
  52.3 22.5 %all_to_all.10.back_ref = bf16[16,128,128]{2,1,0:T(8,128)(2,1)S(1)} all-to-all(bf16[16,128,128]{2,1,0:T(8,128)(2,1)S(1)} %attend.1), channel_id=1, replica_groups=mesh['groups'=2,'branch'=16] {'branch'}, dimensions={0} | all-to-all | bytes 1048576 | tf_op jit(solution)/shard_map/all_to_all | solution.py:420
  74.8 1.5 %post.1 = bf16[16,8192]{1,0:T(8,128)(2,1)} custom-call(s32[16]{0:T(128)S(1)} %bitcast.4, bf16[16,128,128]{2,1,0:T(8,128)(2,1)S(1)} %all_to_all.10.back_ref), custom_call_target="tpu_custom_call" | custom-call | tf_op jit(solution)/shard_map/post/pallas_call | solution.py:421
  (30 shorter events, 0.1 us)
Async XLA Ops:
  0.0 35.3 %copy-start.1 = (s32[1,8]{1,0:T(1,128)S(1)}, s32[1,8]{1,0:T(1,128)}, u32[]{:S(2)}) copy-start(s32[1,8]{1,0:T(1,128)} %mask_ref.1) | copy-start | bytes 100
  1.7 8.2 %collective-permute-start = (bf16[784,128]{1,0:T(8,128)(2,1)}, bf16[784,128]{1,0:T(8,128)(2,1)S(1)}, u32[]{:S(2)}, u32[]{:S(2)}) collective-permute-start(bf16[784,128]{1,0:T(8,128)(2,1)} %payload.1.after_hbm.refs_0_), channel_id=1, source_target_pairs={{0,4},{1,5},{4,8},{5,9},{8,12},{9,13},{12,14},{13,15},{14,10},{15,... | collective-permute-start | bytes 602120 | tf_op jit(solution)/shard_map/ppermute | solution.py:330
  4.8 6.9 %collective-permute-start.3 = (bf16[784,128]{1,0:T(8,128)(2,1)}, bf16[784,128]{1,0:T(8,128)(2,1)S(1)}, u32[]{:S(2)}, u32[]{:S(2)}) collective-permute-start(bf16[784,128]{1,0:T(8,128)(2,1)} %payload.1.after_hbm.refs_0_), channel_id=1, source_target_pairs={{0,2},{1,3},{4,0},{5,1},{8,4},{9,5},{12,8},{13,9},{14,12},{15,13},... | collective-permute-start | bytes 602120 | tf_op jit(solution)/shard_map/ppermute | solution.py:330
  9.9 23.9 %copy-start.4 = (bf16[784,128]{1,0:T(8,128)(2,1)}, bf16[784,128]{1,0:T(8,128)(2,1)S(1)}, u32[]{:S(2)}) copy-start(bf16[784,128]{1,0:T(8,128)(2,1)S(1)} %collective-permute-done.refs_1_) | copy-start | bytes 602116
  9.9 6.2 %collective-permute-start.1 = (bf16[784,128]{1,0:T(8,128)(2,1)S(1)}, bf16[784,128]{1,0:T(8,128)(2,1)S(1)}, u32[]{:S(2)}, u32[]{:S(2)}) collective-permute-start(bf16[784,128]{1,0:T(8,128)(2,1)S(1)} %collective-permute-done.refs_1_), channel_id=1, source_target_pairs={{0,4},{1,5},{4,8},{5,9},{8,12},{9,13},{12,14},{13,15},{14,10},{15,... | collective-permute-start | bytes 602120 | tf_op jit(solution)/shard_map/ppermute | solution.py:330
  11.7 22.1 %copy-start.5 = (bf16[784,128]{1,0:T(8,128)(2,1)}, bf16[784,128]{1,0:T(8,128)(2,1)S(1)}, u32[]{:S(2)}) copy-start(bf16[784,128]{1,0:T(8,128)(2,1)S(1)} %collective-permute-done.3.refs_2_) | copy-start | bytes 602116
  11.7 5.9 %collective-permute-start.4 = (bf16[784,128]{1,0:T(8,128)(2,1)S(1)}, bf16[784,128]{1,0:T(8,128)(2,1)S(1)}, u32[]{:S(2)}, u32[]{:S(2)}) collective-permute-start(bf16[784,128]{1,0:T(8,128)(2,1)S(1)} %collective-permute-done.3.refs_2_), channel_id=1, source_target_pairs={{0,2},{1,3},{4,0},{5,1},{8,4},{9,5},{12,8},{13,9},{14,12},{15,13},... | collective-permute-start | bytes 602120 | tf_op jit(solution)/shard_map/ppermute | solution.py:330
  16.1 17.7 %copy-start.6 = (bf16[784,128]{1,0:T(8,128)(2,1)}, bf16[784,128]{1,0:T(8,128)(2,1)S(1)}, u32[]{:S(2)}) copy-start(bf16[784,128]{1,0:T(8,128)(2,1)S(1)} %collective-permute-done.1.refs_3_) | copy-start | bytes 602116
  16.1 5.7 %collective-permute-start.2 = (bf16[784,128]{1,0:T(8,128)(2,1)S(1)}, bf16[784,128]{1,0:T(8,128)(2,1)S(1)}, u32[]{:S(2)}, u32[]{:S(2)}) collective-permute-start(bf16[784,128]{1,0:T(8,128)(2,1)S(1)} %collective-permute-done.1.refs_3_), channel_id=1, source_target_pairs={{0,4},{1,5},{4,8},{5,9},{8,12},{9,13},{12,14},{13,15},{14,10},{15,... | collective-permute-start | bytes 602120 | tf_op jit(solution)/shard_map/ppermute | solution.py:330
  17.6 16.3 %copy-start.7 = (bf16[784,128]{1,0:T(8,128)(2,1)}, bf16[784,128]{1,0:T(8,128)(2,1)S(1)}, u32[]{:S(2)}) copy-start(bf16[784,128]{1,0:T(8,128)(2,1)S(1)} %collective-permute-done.4.refs_4_) | copy-start | bytes 602116
  17.6 5.7 %collective-permute-start.5 = (bf16[784,128]{1,0:T(8,128)(2,1)S(1)}, bf16[784,128]{1,0:T(8,128)(2,1)S(1)}, u32[]{:S(2)}, u32[]{:S(2)}) collective-permute-start(bf16[784,128]{1,0:T(8,128)(2,1)S(1)} %collective-permute-done.4.refs_4_), channel_id=1, source_target_pairs={{0,2},{1,3},{4,0},{5,1},{8,4},{9,5},{12,8},{13,9},{14,12},{15,13},... | collective-permute-start | bytes 602120 | tf_op jit(solution)/shard_map/ppermute | solution.py:330
  21.8 13.4 %copy-start.2 = (bf16[784,128]{1,0:T(8,128)(2,1)}, bf16[784,128]{1,0:T(8,128)(2,1)S(1)}, u32[]{:S(2)}) copy-start(bf16[784,128]{1,0:T(8,128)(2,1)S(1)} %collective-permute-done.2.refs_5_) | copy-start | bytes 602116
  23.3 10.6 %copy-start.3 = (bf16[784,128]{1,0:T(8,128)(2,1)}, bf16[784,128]{1,0:T(8,128)(2,1)S(1)}, u32[]{:S(2)}) copy-start(bf16[784,128]{1,0:T(8,128)(2,1)S(1)} %collective-permute-done.5.refs_6_) | copy-start | bytes 602116
  23.3 21.9 %all-to-all-start = ((bf16[16,160,128]{2,1,0:T(8,128)(2,1)}), bf16[16,160,128]{2,1,0:T(8,128)(2,1)S(1)}, u32[]{:S(2)}, u32[]{:S(2)}) async-start(bf16[16,160,128]{2,1,0:T(8,128)(2,1)} %prep.1), calls=%async_computation | async-start | bytes 1310720 | tf_op jit(solution)/shard_map/all_to_all | solution.py:362
  28.2 1.7 %collective-permute-start.8 = (bf16[784,128]{1,0:T(8,128)(2,1)}, bf16[784,128]{1,0:T(8,128)(2,1)S(1)}, u32[]{:S(2)}, u32[]{:S(2)}) collective-permute-start(bf16[784,128]{1,0:T(8,128)(2,1)} %payload.1.after_hbm.refs_0_), channel_id=1, source_target_pairs={{0,1},{1,0},{2,3},{3,2},{4,5},{5,4},{6,7},{7,6},{8,9},{9,8},{10,11... | collective-permute-start | bytes 602120 | tf_op jit(solution)/shard_map/ppermute | solution.py:333
  28.7 1.7 %collective-permute-start.10 = (bf16[784,128]{1,0:T(8,128)(2,1)S(1)}, bf16[784,128]{1,0:T(8,128)(2,1)S(1)}, u32[]{:S(2)}, u32[]{:S(2)}) collective-permute-start(bf16[784,128]{1,0:T(8,128)(2,1)S(1)} %collective-permute-done.3.refs_2_), channel_id=1, source_target_pairs={{0,1},{1,0},{2,3},{3,2},{4,5},{5,4},{6,7},{7,6},{8,9},{9,8},{10,11... | collective-permute-start | bytes 602120 | tf_op jit(solution)/shard_map/ppermute | solution.py:333
  28.8 2.3 %collective-permute-start.9 = (bf16[784,128]{1,0:T(8,128)(2,1)S(1)}, bf16[784,128]{1,0:T(8,128)(2,1)S(1)}, u32[]{:S(2)}, u32[]{:S(2)}) collective-permute-start(bf16[784,128]{1,0:T(8,128)(2,1)S(1)} %collective-permute-done.refs_1_), channel_id=1, source_target_pairs={{0,1},{1,0},{2,3},{3,2},{4,5},{5,4},{6,7},{7,6},{8,9},{9,8},{10,11... | collective-permute-start | bytes 602120 | tf_op jit(solution)/shard_map/ppermute | solution.py:333
  29.2 4.5 %collective-permute-start.11 = (bf16[784,128]{1,0:T(8,128)(2,1)S(1)}, bf16[784,128]{1,0:T(8,128)(2,1)S(1)}, u32[]{:S(2)}, u32[]{:S(2)}) collective-permute-start(bf16[784,128]{1,0:T(8,128)(2,1)S(1)} %collective-permute-done.1.refs_3_), channel_id=1, source_target_pairs={{0,1},{1,0},{2,3},{3,2},{4,5},{5,4},{6,7},{7,6},{8,9},{9,8},{10,11... | collective-permute-start | bytes 602120 | tf_op jit(solution)/shard_map/ppermute | solution.py:333
  29.3 4.5 %collective-permute-start.12 = (bf16[784,128]{1,0:T(8,128)(2,1)S(1)}, bf16[784,128]{1,0:T(8,128)(2,1)S(1)}, u32[]{:S(2)}, u32[]{:S(2)}) collective-permute-start(bf16[784,128]{1,0:T(8,128)(2,1)S(1)} %collective-permute-done.4.refs_4_), channel_id=1, source_target_pairs={{0,1},{1,0},{2,3},{3,2},{4,5},{5,4},{6,7},{7,6},{8,9},{9,8},{10,11... | collective-permute-start | bytes 602120 | tf_op jit(solution)/shard_map/ppermute | solution.py:333
  30.0 3.9 %copy-start.8 = (bf16[784,128]{1,0:T(8,128)(2,1)}, bf16[784,128]{1,0:T(8,128)(2,1)S(1)}, u32[]{:S(2)}) copy-start(bf16[784,128]{1,0:T(8,128)(2,1)S(1)} %collective-permute-done.8.refs_7_) | copy-start | bytes 602116
  30.0 3.8 %collective-permute-start.13 = (bf16[784,128]{1,0:T(8,128)(2,1)S(1)}, bf16[784,128]{1,0:T(8,128)(2,1)S(1)}, u32[]{:S(2)}, u32[]{:S(2)}) collective-permute-start(bf16[784,128]{1,0:T(8,128)(2,1)S(1)} %collective-permute-done.2.refs_5_), channel_id=1, source_target_pairs={{0,1},{1,0},{2,3},{3,2},{4,5},{5,4},{6,7},{7,6},{8,9},{9,8},{10,11... | collective-permute-start | bytes 602120 | tf_op jit(solution)/shard_map/ppermute | solution.py:333
  30.3 3.6 %copy-start.9 = (bf16[784,128]{1,0:T(8,128)(2,1)}, bf16[784,128]{1,0:T(8,128)(2,1)S(1)}, u32[]{:S(2)}) copy-start(bf16[784,128]{1,0:T(8,128)(2,1)S(1)} %collective-permute-done.10.refs_9_) | copy-start | bytes 602116
  30.3 3.5 %collective-permute-start.14 = (bf16[784,128]{1,0:T(8,128)(2,1)S(1)}, bf16[784,128]{1,0:T(8,128)(2,1)S(1)}, u32[]{:S(2)}, u32[]{:S(2)}) collective-permute-start(bf16[784,128]{1,0:T(8,128)(2,1)S(1)} %collective-permute-done.5.refs_6_), channel_id=1, source_target_pairs={{0,1},{1,0},{2,3},{3,2},{4,5},{5,4},{6,7},{7,6},{8,9},{9,8},{10,11... | collective-permute-start | bytes 602120 | tf_op jit(solution)/shard_map/ppermute | solution.py:333
  31.1 2.8 %copy-start.10 = (bf16[784,128]{1,0:T(8,128)(2,1)}, bf16[784,128]{1,0:T(8,128)(2,1)S(1)}, u32[]{:S(2)}) copy-start(bf16[784,128]{1,0:T(8,128)(2,1)S(1)} %collective-permute-done.9.refs_8_) | copy-start | bytes 602116
  31.1 12.0 %collective-permute-start.6 = (bf16[400,128]{1,0:T(8,128)(2,1)}, bf16[400,128]{1,0:T(8,128)(2,1)}, u32[]{:S(2)}, u32[]{:S(2)}) collective-permute-start(bf16[400,128]{1,0:T(8,128)(2,1)} %slice.6), channel_id=1, source_target_pairs={{0,4},{1,5},{4,8},{5,9},{8,12},{9,13},{12,14},{13,15},{14,10},{15,... | collective-permute-start | bytes 307208 | tf_op jit(solution)/shard_map/ppermute | solution.py:330
  33.6 0.7 copy-start.11
  33.6 9.5 %collective-permute-start.7 = (bf16[384,128]{1,0:T(8,128)(2,1)}, bf16[384,128]{1,0:T(8,128)(2,1)}, u32[]{:S(2)}, u32[]{:S(2)}) collective-permute-start(bf16[384,128]{1,0:T(8,128)(2,1)} %slice.7), channel_id=1, source_target_pairs={{0,2},{1,3},{4,0},{5,1},{8,4},{9,5},{12,8},{13,9},{14,12},{15,13},... | collective-permute-start | bytes 294920 | tf_op jit(solution)/shard_map/ppermute | solution.py:330
  33.8 0.7 copy-start.12
  33.8 0.8 copy-start.13
  34.6 0.7 copy-start.14
  43.2 1.7 %collective-permute-start.15 = (bf16[400,128]{1,0:T(8,128)(2,1)}, bf16[400,128]{1,0:T(8,128)(2,1)S(1)}, u32[]{:S(2)}, u32[]{:S(2)}) collective-permute-start(bf16[400,128]{1,0:T(8,128)(2,1)} %collective-permute-done.6.refs_0_), channel_id=1, source_target_pairs={{0,1},{1,0},{2,3},{3,2},{4,5},{5,4},{6,7},{7,6},{8,9},{9,8},{10,11... | collective-permute-start | bytes 307208 | tf_op jit(solution)/shard_map/ppermute | solution.py:333
  43.3 1.7 %collective-permute-start.16 = (bf16[384,128]{1,0:T(8,128)(2,1)}, bf16[384,128]{1,0:T(8,128)(2,1)S(1)}, u32[]{:S(2)}, u32[]{:S(2)}) collective-permute-start(bf16[384,128]{1,0:T(8,128)(2,1)} %collective-permute-done.7.refs_1_), channel_id=1, source_target_pairs={{0,1},{1,0},{2,3},{3,2},{4,5},{5,4},{6,7},{7,6},{8,9},{9,8},{10,11... | collective-permute-start | bytes 294920 | tf_op jit(solution)/shard_map/ppermute | solution.py:333
  44.9 0.6 copy-start.16
  44.9 0.7 copy-start.15
  45.6 29.2 %copy-start = (s32[16,1]{0,1:T(1,128)S(1)}, s32[16,1]{0,1:T(1,128)}, u32[]{:S(2)}) copy-start(s32[16,1]{0,1:T(1,128)} %param.17) | copy-start | bytes 196

commit v4 on v3

--- a/solution.py
+++ b/solution.py
@@ -130,7 +130,9 @@
 
 def gather_kernel(whole, split, me_ref, mask_ref, pk_hbm, pv_hbm, *refs):
     sources = refs[:whole]
-    key_ref, value_hbm, bias_ref, value_ref, taken_ref, *blocks, sems = refs[whole:]
+    near_key, near_value, bias_ref, far_key_hbm, far_value_hbm = refs[whole : whole + 5]
+    far_key, far_value, taken_ref, *blocks, sems = refs[whole + 5 :]
+    near = near_key.shape[0]
     slabs, room, _ = taken_ref.shape
     kv_heads = slabs // 2
     prompt = pk_hbm.shape[1]
@@ -141,10 +143,12 @@
     start = starter(sems)
     moves = [start(source, target) for source, target in zip(sources, blocks)]
     wide = []
-    for g in range(kv_heads):
+    homes = [(near_key.at[g], near_value.at[g]) for g in range(near)]
+    homes += [(far_key.at[g], far_value.at[g]) for g in range(kv_heads - near)]
+    for g, (key_ref, value_ref) in enumerate(homes):
         lanes = pl.ds(g * HD, HD)
-        wide.append(start(pv_hbm.at[0, :, lanes], value_ref.at[g, pl.ds(0, prompt), :]))
-        wide.append(start(pk_hbm.at[0, :, lanes], key_ref.at[g, pl.ds(0, prompt), :]))
+        wide.append(start(pv_hbm.at[0, :, lanes], value_ref.at[pl.ds(0, prompt), :]))
+        wide.append(start(pk_hbm.at[0, :, lanes], key_ref.at[pl.ds(0, prompt), :]))
     column = lax.broadcasted_iota(jnp.int32, (1, room), 1)
     seen = jnp.zeros((1, room), jnp.bool_)
     taken_ref[...] = jnp.zeros(taken_ref.shape, jnp.float32)
@@ -164,9 +168,9 @@
                 taken_ref[j, pl.ds(at, rows), :] = rows_picked(block[base : base + live, :], pick)
 
         slot = slot + (pick >= 0).astype(jnp.int32)
-    for g in range(kv_heads):
-        key_ref[g, prompt : prompt + room, :] = taken_ref[g].astype(jnp.bfloat16)
-        value_ref[g, prompt : prompt + room, :] = taken_ref[kv_heads + g].astype(jnp.bfloat16)
+    for g, (key_ref, value_ref) in enumerate(homes):
+        key_ref[prompt : prompt + room, :] = taken_ref[g].astype(jnp.bfloat16)
+        value_ref[prompt : prompt + room, :] = taken_ref[kv_heads + g].astype(jnp.bfloat16)
     blocks_seen = mask_ref.shape[1]
     biases = [
         jnp.full((1, prompt // blocks_seen), jnp.where(mask_ref[0, j] > 0, 0.0, NONE))
@@ -176,16 +180,22 @@
     bias_ref[...] = bias
     for copy in wide:
         copy.wait()
-    leaving = start(value_ref, value_hbm)
-    leaving.wait()
-
-
-def attend_kernel(split, me_ref, key_ref, bias_ref, recv_ref, value_hbm, *refs):
-    out_ref, late_key_ref, late_value_ref, first_ref, second_ref, value_ref, *halves, sems = refs[2 * split :]
-    kv_heads, early, _ = key_ref.shape
+    leaving = [start(far_key, far_key_hbm), start(far_value, far_value_hbm)]
+    for copy in leaving:
+        copy.wait()
+
+
+def attend_kernel(split, me_ref, near_key, near_value, bias_ref, recv_ref, *refs):
+    halves = refs[: 2 * split]
+    far_key_hbm, far_value_hbm, out_ref, late_key_ref, late_value_ref, first_ref, second_ref, far_key, far_value, sems = (
+        refs[2 * split :]
+    )
+    near, early, _ = near_key.shape
+    kv_heads = near + far_key.shape[0]
+    early_of = [(near_key.at[g], near_value.at[g]) for g in range(near)]
+    early_of += [(far_key.at[g], far_value.at[g]) for g in range(kv_heads - near)]
     start = starter(sems)
-    half_moves = [start(source, target) for source, target in zip(refs[: 2 * split], halves)]
-    value_moves = [start(value_hbm.at[g], value_ref.at[g]) for g in range(kv_heads)]
+    far_moves = [start(far_key_hbm, far_key), start(far_value_hbm, far_value)]
     branches = recv_ref.shape[0]
     heads = kv_heads * GRP
     width = branches * CAP
@@ -199,12 +209,11 @@
 
     def score(g, base, target):
         queries = recv_ref[pl.ds(base, chunk), g * TILE : (g + 1) * TILE, :].reshape(count, HD)
-        target[:, 0:main] = dot_nt(queries, key_ref[g, 0:main, :]) + bias_ref[0:1, 0:main]
+        target[:, 0:main] = dot_nt(queries, early_of[g][0][0:main, :]) + bias_ref[0:1, 0:main]
 
     if branches == chunk:
         score(0, 0, first_ref)
-    for copy in half_moves:
-        copy.wait()
+        score(1, 0, second_ref)
     size = branches * TILE
     place = lax.broadcasted_iota(jnp.int32, (size, size), 1)
     wanted = lax.broadcasted_iota(jnp.int32, (size, size), 0)
@@ -214,15 +223,17 @@
         first = heads * CAP + which * TILE
         rows = recv_ref[:, first : first + TILE, :].reshape(size, HD)
         unique.append(jnp.dot(choose, rows, preferred_element_type=jnp.float32).reshape(kv_heads, width, HD))
-    for copy in value_moves:
-        copy.wait()
     choices = [picked(halves[2 * n][kv_heads * live :, :], me_ref[0], branches) for n in range(split)]
-    for which, source, target in ((0, key_ref, late_key_ref), (1, value_ref, late_value_ref)):
-        for g in range(kv_heads):
+
+    def fill(g):
+        for which, target in ((0, late_key_ref), (1, late_value_ref)):
             rows = [rows_picked(halves[2 * n + which][g * live : (g + 1) * live, :], choices[n][0]) for n in range(split)]
             if tail:
-                rows = [source[g, main:early, :].astype(jnp.float32)] + rows
+                rows = [early_of[g][which][main:early, :].astype(jnp.float32)] + rows
             target[g] = jnp.concatenate(rows + [unique[which][g]], axis=0).astype(jnp.bfloat16)
+
+    for g in range(near):
+        fill(g)
     one = jnp.where(lax.broadcasted_iota(jnp.int32, (TILE, HD), 1) == 0, 1.0, 0.0).astype(jnp.bfloat16)
     absent = dot_nt(one, late_key_ref[0])[0:1, :] > ABSENT / 2
     spot = lax.broadcasted_iota(jnp.int32, (1, far), 1)
@@ -233,6 +244,15 @@
     column = lax.broadcasted_iota(jnp.int32, (count, late), 1) - (late - width)
     own_slot = lax.broadcasted_iota(jnp.int32, (count, late), 0) // GRP
 
+    def far_part():
+        for copy in far_moves:
+            copy.wait()
+        for g in range(near, kv_heads):
+            fill(g)
+
+    if branches > chunk:
+        far_part()
+
     def run(base):
         late_hidden = jnp.where((column >= 0) & (absent | (column > own_slot + base * CAP)), NONE, late_bias)
 
@@ -246,7 +266,7 @@
             weights = jnp.exp2((scores - largest) * FACTOR)
             total = jnp.sum(weights, axis=1, keepdims=True)
             probs = weights.astype(jnp.bfloat16)
-            mixed = jnp.dot(probs[:, 0:main], value_ref[g, 0:main, :], preferred_element_type=jnp.float32)
+            mixed = jnp.dot(probs[:, 0:main], early_of[g][1][0:main, :], preferred_element_type=jnp.float32)
             mixed = mixed + jnp.dot(probs[:, main:], late_value_ref[g], preferred_element_type=jnp.float32)
             result = (mixed / total).astype(jnp.bfloat16)
             out_ref[pl.ds(base, chunk), g * TILE : (g + 1) * TILE, :] = result.reshape(chunk, TILE, HD)
@@ -254,12 +274,16 @@
         buffers = (first_ref, second_ref)
         if branches > chunk:
             score(0, base, buffers[0])
+            score(1, base, buffers[1])
         score_late(0, buffers[0])
+        score_late(1, buffers[1])
         for g in range(kv_heads):
-            if g + 1 < kv_heads:
-                score(g + 1, base, buffers[(g + 1) % 2])
-                score_late(g + 1, buffers[(g + 1) % 2])
             finish(g, buffers[g % 2])
+            if g + 2 == near and branches == chunk:
+                far_part()
+            if g + 2 < kv_heads:
+                score(g + 2, base, buffers[g % 2])
+                score_late(g + 2, buffers[g % 2])
 
     if branches == chunk:
         run(0)
@@ -373,41 +397,45 @@
     chunk_rows = min(branches, 16) * TILE
     rows = width * GRP
     arrays = [pltpu.with_memory_space_constraint(x, pltpu.HBM) for x in (prompt_k, prompt_v, *blocks)]
-    keys, values, bias = pl.pallas_call(
+    near = kv_heads // 2 - 1
+    keys, values, bias, *far_early = pl.pallas_call(
         functools.partial(gather_kernel, whole, split),
         out_shape=(
-            pltpu.VMEM((kv_heads, early, HD), jnp.bfloat16),
-            pltpu.HBM((kv_heads, early, HD), jnp.bfloat16),
+            pltpu.VMEM((near, early, HD), jnp.bfloat16),
+            pltpu.VMEM((near, early, HD), jnp.bfloat16),
             pltpu.VMEM((1, early), jnp.float32),
+            pltpu.HBM((kv_heads - near, early, HD), jnp.bfloat16),
+            pltpu.HBM((kv_heads - near, early, HD), jnp.bfloat16),
         ),
         in_specs=[SMEM, SMEM] + [ANY] * len(arrays),
-        out_specs=(VMEM, ANY, VMEM),
+        out_specs=(VMEM, VMEM, VMEM, ANY, ANY),
         scratch_shapes=[
-            pltpu.VMEM((kv_heads, early, HD), jnp.bfloat16),
+            pltpu.VMEM((kv_heads - near, early, HD), jnp.bfloat16),
+            pltpu.VMEM((kv_heads - near, early, HD), jnp.bfloat16),
             pltpu.VMEM((2 * kv_heads, room, HD), jnp.float32),
             *[pltpu.VMEM(x.shape, jnp.bfloat16) for x in arrays[2:]],
-            pltpu.SemaphoreType.DMA((len(arrays) - 2 + 2 * kv_heads + 1,)),
+            pltpu.SemaphoreType.DMA((len(arrays) - 2 + 2 * kv_heads + 2,)),
         ],
         compiler_params=grant(40 if branches > 16 else 20),
         cost_estimate=pl.CostEstimate(flops=0, bytes_accessed=8 * prompt_k.size, transcendentals=0),
         name="gather",
     )(me, prompt_mask, *arrays)
-    halves, keys = lax.optimization_barrier((halves, keys))
+    halves, keys, values = lax.optimization_barrier((halves, keys, values))
     halves = halves + [across(x) for x in halves]
     late = tail + split * result_rows + width
     outputs = pl.pallas_call(
         functools.partial(attend_kernel, split),
         out_shape=bf16(branches, CAP * heads, HD),
-        in_specs=[SMEM, VMEM, VMEM, VMEM] + [ANY] * (1 + 2 * split),
+        in_specs=[SMEM] + [VMEM] * (4 + 2 * split) + [ANY] * 2,
         out_specs=VMEM,
         scratch_shapes=[
             pltpu.VMEM((kv_heads, late, HD), jnp.bfloat16),
             pltpu.VMEM((kv_heads, late, HD), jnp.bfloat16),
             pltpu.VMEM((chunk_rows, early - tail + late), jnp.float32),
             pltpu.VMEM((chunk_rows, early - tail + late), jnp.float32),
-            pltpu.VMEM((kv_heads, early, HD), jnp.bfloat16),
-            *[pltpu.VMEM(x.shape, jnp.bfloat16) for x in halves],
-            pltpu.SemaphoreType.DMA((2 * split + kv_heads,)),
+            pltpu.VMEM((kv_heads - near, early, HD), jnp.bfloat16),
+            pltpu.VMEM((kv_heads - near, early, HD), jnp.bfloat16),
+            pltpu.SemaphoreType.DMA((2,)),
         ],
         compiler_params=grant(40),
         cost_estimate=pl.CostEstimate(
@@ -416,7 +444,7 @@
             transcendentals=kv_heads * rows * (early + width),
         ),
         name="attend",
-    )(me, keys, bias, recv, *[pltpu.with_memory_space_constraint(x, pltpu.HBM) for x in (values, *halves)])
+    )(me, keys, values, bias, recv, *halves, *[pltpu.with_memory_space_constraint(x, pltpu.HBM) for x in far_early])
     back = lax.all_to_all(outputs, "branch", split_axis=0, concat_axis=0, tiled=True)
     return pl.pallas_call(
         post_kernel,

time: 76.7 us -> 74.5 us (0.971)
  Pallas kernels: 20.6 us -> 19.7 us
    pallas_call x1, Pallas kernels: 6.65 us -> 5.53 us  [body(): pl.pallas_call(functools.partial(attend_kernel, split), out_shape=bf16(br...]
    unnamed x34 -> x32, local copies, waits for them, and re-layouts: 1.76 us -> 1.33 us
  transfers between devices with their start and end apart: 18 -> 18, of which waited for: 7 -> 7; matrix products, arithmetic and copies ran while one was open for 2% -> 2% of each run, Pallas kernels for 14% -> 15%
where the time goes in v4:
time: 74.5 us; the launch traced here: 74.2 us
  blocking collectives  21.9 us (29%)
  Pallas kernels  19.7 us (26%)
  starting transfers between devices  16.8 us (23%)
  waiting for transfers between devices  13 us (17%)
  local copies, waits for them, and re-layouts  2.62 us (4%)
    all_to_all x1, blocking collectives, body(): lax.all_to_all(outputs, 'branch', split_axis=0, concat_axis=0, tiled=True)  21.9 us
    ppermute x8, waiting for transfers between devices, along(): return lax.ppermute(x, 'branch', pairs)  11.7 us
    ppermute x8, starting transfers between devices, along(): return lax.ppermute(x, 'branch', pairs)  9.21 us
    pallas_call x1, Pallas kernels, body(): pl.pallas_call(functools.partial(gather_kernel, whole, split), out_shape=...  8.13 us
    pallas_call x1, Pallas kernels, body(): pl.pallas_call(functools.partial(attend_kernel, split), out_shape=bf16(br...  5.53 us
    all_to_all x1, starting transfers between devices, body(): lax.all_to_all(send, 'branch', split_axis=0, concat_axis=0, tiled=True)  4.93 us
    pallas_call x1, Pallas kernels, body(): pl.pallas_call(prep_kernel, out_shape=bf16(branches, slot_rows, HD), in_s...  2.78 us
    ppermute x9, starting transfers between devices, across(): return lax.ppermute(x, 'branch', [(i, i ^ 1) for i in range(branches)])  2.71 us
  transfers between devices with their start and end apart: 18, of which 7 were waited for; matrix products, arithmetic and copies ran while one was open for 2% of the time, Pallas kernels for 15%

profile of v4, /device:TPU:0, one launch (start us, length us, event | category | flops | bytes accessed | tf_op | source)
XLA Modules:
  0.0 74.2 jit_solution(4513390370693581775)
XLA Ops:
  0.0 1.7 %payload.1.after_hbm.refs_0_ = bf16[784,128]{1,0:T(8,128)(2,1)} custom-call(s32[1,16]{1,0:T(1,128)} %pick_hbm.1, s32[1,2]{1,0:T(1,128)} %bitcast.5, bf16[2,24,2048]{2,1,0:T(8,128)(2,1)} %shared_hbm.1), custom_call_target="tpu_custom_call" | custom-call | tf_op jit(solution)/shard_map/payload/pallas_call | solution.py:331
  1.7 0.0 copy-start.2
  1.7 3.1 %collective-permute-start = (bf16[784,128]{1,0:T(8,128)(2,1)}, bf16[784,128]{1,0:T(8,128)(2,1)S(1)}, u32[]{:S(2)}, u32[]{:S(2)}) collective-permute-start(bf16[784,128]{1,0:T(8,128)(2,1)} %payload.1.after_hbm.refs_0_), channel_id=1, source_target_pairs={{0,4},{1,5},{4,8},{5,9},{8,12},{9,13},{12,14},{13,15},{14,10},{15,... | collective-permute-start | bytes 602120 | tf_op jit(solution)/shard_map/ppermute | solution.py:354
  4.8 0.0 collective-permute-start.3
  4.8 2.8 %prep.1 = bf16[16,160,128]{2,1,0:T(8,128)(2,1)} custom-call(s32[16]{0:T(128)} %bitcast.3, bf16[16,8192]{1,0:T(8,128)(2,1)} %q_hbm.1, bf16[16,2048]{1,0:T(8,128)(2,1)} %kv_hbm.1, bf16[784,128]{1,0:T(8,128)(2,1)} %payload.1.after_hbm.refs_0_), custom_call_target="tpu_custom_call" | custom-call | bytes 1024 | tf_op jit(solution)/shard_map/prep/pallas_call | solution.py:359
  7.6 2.4 %collective-permute-done.refs_1_ = bf16[784,128]{1,0:T(8,128)(2,1)S(1)} collective-permute-done((bf16[784,128]{1,0:T(8,128)(2,1)}, bf16[784,128]{1,0:T(8,128)(2,1)S(1)}, u32[]{:S(2)}, u32[]{:S(2)}) %collective-permute-start) | collective-permute-done | bytes 200736 | tf_op jit(solution)/shard_map/ppermute | solution.py:354
  10.0 1.8 %collective-permute-start.1 = (bf16[784,128]{1,0:T(8,128)(2,1)S(1)}, bf16[784,128]{1,0:T(8,128)(2,1)S(1)}, u32[]{:S(2)}, u32[]{:S(2)}) collective-permute-start(bf16[784,128]{1,0:T(8,128)(2,1)S(1)} %collective-permute-done.refs_1_), channel_id=1, source_target_pairs={{0,4},{1,5},{4,8},{5,9},{8,12},{9,13},{12,14},{13,15},{14,10},{15,... | collective-permute-start | bytes 602120 | tf_op jit(solution)/shard_map/ppermute | solution.py:354
  11.7 0.0 collective-permute-done.3.refs_2_
  11.7 0.2 collective-permute-start.4
  12.0 4.1 %collective-permute-done.1.refs_3_ = bf16[784,128]{1,0:T(8,128)(2,1)S(1)} collective-permute-done((bf16[784,128]{1,0:T(8,128)(2,1)S(1)}, bf16[784,128]{1,0:T(8,128)(2,1)S(1)}, u32[]{:S(2)}, u32[]{:S(2)}) %collective-permute-start.1) | collective-permute-done | bytes 200736 | tf_op jit(solution)/shard_map/ppermute | solution.py:354
  16.1 1.5 %collective-permute-start.2 = (bf16[784,128]{1,0:T(8,128)(2,1)S(1)}, bf16[784,128]{1,0:T(8,128)(2,1)S(1)}, u32[]{:S(2)}, u32[]{:S(2)}) collective-permute-start(bf16[784,128]{1,0:T(8,128)(2,1)S(1)} %collective-permute-done.1.refs_3_), channel_id=1, source_target_pairs={{0,4},{1,5},{4,8},{5,9},{8,12},{9,13},{12,14},{13,15},{14,10},{15,... | collective-permute-start | bytes 602120 | tf_op jit(solution)/shard_map/ppermute | solution.py:354
  17.6 0.0 collective-permute-done.4.refs_4_
  17.6 0.6 collective-permute-start.5
  18.2 3.7 %collective-permute-done.2.refs_5_ = bf16[784,128]{1,0:T(8,128)(2,1)S(1)} collective-permute-done((bf16[784,128]{1,0:T(8,128)(2,1)S(1)}, bf16[784,128]{1,0:T(8,128)(2,1)S(1)}, u32[]{:S(2)}, u32[]{:S(2)}) %collective-permute-start.2) | collective-permute-done | bytes 200736 | tf_op jit(solution)/shard_map/ppermute | solution.py:354
  21.8 1.5 %collective-permute-done.5.refs_6_ = bf16[784,128]{1,0:T(8,128)(2,1)S(1)} collective-permute-done((bf16[784,128]{1,0:T(8,128)(2,1)S(1)}, bf16[784,128]{1,0:T(8,128)(2,1)S(1)}, u32[]{:S(2)}, u32[]{:S(2)}) %collective-permute-start.5) | collective-permute-done | bytes 200736 | tf_op jit(solution)/shard_map/ppermute | solution.py:354
  23.3 4.9 %all-to-all-start = ((bf16[16,160,128]{2,1,0:T(8,128)(2,1)}), bf16[16,160,128]{2,1,0:T(8,128)(2,1)S(1)}, u32[]{:S(2)}, u32[]{:S(2)}) async-start(bf16[16,160,128]{2,1,0:T(8,128)(2,1)} %prep.1), calls=%async_computation | async-start | bytes 1310720 | tf_op jit(solution)/shard_map/all_to_all | solution.py:386
  28.3 0.5 collective-permute-start.8
  28.7 0.1 collective-permute-start.10
  28.8 0.4 collective-permute-start.9
  29.2 0.1 collective-permute-start.11
  29.4 0.4 collective-permute-start.12
  29.8 0.1 collective-permute-done.8.refs_7_
  29.8 0.4 collective-permute-start.13
  30.2 0.0 collective-permute-done.10.refs_9_
  30.2 0.3 collective-permute-start.14
  30.5 0.6 slice.6
  31.1 0.0 collective-permute-done.9.refs_8_
  31.1 1.8 %collective-permute-start.6 = (bf16[400,128]{1,0:T(8,128)(2,1)}, bf16[400,128]{1,0:T(8,128)(2,1)S(1)}, u32[]{:S(2)}, u32[]{:S(2)}) collective-permute-start(bf16[400,128]{1,0:T(8,128)(2,1)} %slice.6), channel_id=1, source_target_pairs={{0,4},{1,5},{4,8},{5,9},{8,12},{9,13},{12,14},{13,15},{14,10},{15,... | collective-permute-start | bytes 307208 | tf_op jit(solution)/shard_map/ppermute | solution.py:354
  32.9 0.6 slice.7
  33.6 0.0 collective-permute-done.11.refs_10_
  33.6 0.3 collective-permute-start.7
  33.9 0.0 collective-permute-done.12.refs_11_
  33.9 0.0 collective-permute-done.13.refs_12_
  33.9 0.0 collective-permute-done.14.refs_13_
  33.9 0.3 copy-done.12
  34.2 0.3 copy-done.13
  34.5 0.7 copy-done.15
  35.2 8.1 %gather.1 = (bf16[3,1312,128]{2,1,0:T(8,128)(2,1)S(1)}, bf16[3,1312,128]{2,1,0:T(8,128)(2,1)S(1)}, f32[1,1312]{1,0:T(1,128)S(1)}, bf16[5,1312,128]{2,1,0:T(8,128)(2,1)}, bf16[5,1312,128]{2,1,0:T(8,128)(2,1)}) custom-call(s32[1]{0:T(128)} %bitcast.1.me_ref, s32[1,8]{1,0:T(1,128)S(1)} %copy-done.1, bf16[1,1024,1024]{2,1,0:T(8,128)(2,1)} %pk_hbm.1, ...), custom_call_target="tpu_custom_call" | custom-call | bytes 8388608 | tf_op jit(solution)/shard_map/gather/pallas_call | solution.py:401
  43.4 0.0 collective-permute-done.7.refs_1_
  43.4 0.0 collective-permute-done.6.refs_0_
  43.4 0.1 collective-permute-start.15
  43.5 0.5 collective-permute-start.16
  44.0 0.9 %collective-permute-done.16.refs_3_ = bf16[384,128]{1,0:T(8,128)(2,1)S(1)} collective-permute-done((bf16[384,128]{1,0:T(8,128)(2,1)S(1)}, bf16[384,128]{1,0:T(8,128)(2,1)S(1)}, u32[]{:S(2)}, u32[]{:S(2)}) %collective-permute-start.16) | collective-permute-done | bytes 98336 | tf_op jit(solution)/shard_map/ppermute | solution.py:357
  44.9 0.0 collective-permute-done.15.refs_2_
  44.9 0.3 all-to-all-done.recv_ref
  45.2 5.5 %attend.1 = bf16[16,128,128]{2,1,0:T(8,128)(2,1)S(1)} custom-call(s32[1]{0:T(128)} %bitcast.1.me_ref, bf16[3,1312,128]{2,1,0:T(8,128)(2,1)S(1)} %get-tuple-element.25.near_key, bf16[3,1312,128]{2,1,0:T(8,128)(2,1)S(1)} %get-tuple-element.26.near_value, f32[1,1312]{1,0:T(1,128)S(1)} %get-tuple-element.27.bias_ref, ...), custom_call_target="tpu_custom_call" | custom-call | flops 1409286144 | bytes 4194304 | tf_op jit(solution)/shard_map/attend/pallas_call | solution.py:426
  50.8 21.9 %all_to_all.10.back_ref = bf16[16,128,128]{2,1,0:T(8,128)(2,1)S(1)} all-to-all(bf16[16,128,128]{2,1,0:T(8,128)(2,1)S(1)} %attend.1), channel_id=1, replica_groups=mesh['groups'=2,'branch'=16] {'branch'}, dimensions={0} | all-to-all | bytes 1048576 | tf_op jit(solution)/shard_map/all_to_all | solution.py:448
  72.7 1.5 %post.1 = bf16[16,8192]{1,0:T(8,128)(2,1)} custom-call(s32[16]{0:T(128)S(1)} %bitcast.4, bf16[16,128,128]{2,1,0:T(8,128)(2,1)S(1)} %all_to_all.10.back_ref), custom_call_target="tpu_custom_call" | custom-call | tf_op jit(solution)/shard_map/post/pallas_call | solution.py:449
  (28 shorter events, 0.1 us)
Async XLA Ops:
  0.0 35.2 %copy-start.1 = (s32[1,8]{1,0:T(1,128)S(1)}, s32[1,8]{1,0:T(1,128)}, u32[]{:S(2)}) copy-start(s32[1,8]{1,0:T(1,128)} %mask_ref.1) | copy-start | bytes 100
  1.7 26.5 %copy-start.2 = (bf16[784,128]{1,0:T(8,128)(2,1)S(1)}, bf16[784,128]{1,0:T(8,128)(2,1)}, u32[]{:S(2)}) copy-start(bf16[784,128]{1,0:T(8,128)(2,1)} %payload.1.after_hbm.refs_0_) | copy-start | bytes 602116
  1.7 8.2 %collective-permute-start = (bf16[784,128]{1,0:T(8,128)(2,1)}, bf16[784,128]{1,0:T(8,128)(2,1)S(1)}, u32[]{:S(2)}, u32[]{:S(2)}) collective-permute-start(bf16[784,128]{1,0:T(8,128)(2,1)} %payload.1.after_hbm.refs_0_), channel_id=1, source_target_pairs={{0,4},{1,5},{4,8},{5,9},{8,12},{9,13},{12,14},{13,15},{14,10},{15,... | collective-permute-start | bytes 602120 | tf_op jit(solution)/shard_map/ppermute | solution.py:354
  4.8 6.9 %collective-permute-start.3 = (bf16[784,128]{1,0:T(8,128)(2,1)}, bf16[784,128]{1,0:T(8,128)(2,1)S(1)}, u32[]{:S(2)}, u32[]{:S(2)}) collective-permute-start(bf16[784,128]{1,0:T(8,128)(2,1)} %payload.1.after_hbm.refs_0_), channel_id=1, source_target_pairs={{0,2},{1,3},{4,0},{5,1},{8,4},{9,5},{12,8},{13,9},{14,12},{15,13},... | collective-permute-start | bytes 602120 | tf_op jit(solution)/shard_map/ppermute | solution.py:354
  9.9 21.2 %copy-start.5 = (bf16[784,128]{1,0:T(8,128)(2,1)}, bf16[784,128]{1,0:T(8,128)(2,1)S(1)}, u32[]{:S(2)}) copy-start(bf16[784,128]{1,0:T(8,128)(2,1)S(1)} %collective-permute-done.refs_1_) | copy-start | bytes 602116
  10.0 6.2 %collective-permute-start.1 = (bf16[784,128]{1,0:T(8,128)(2,1)S(1)}, bf16[784,128]{1,0:T(8,128)(2,1)S(1)}, u32[]{:S(2)}, u32[]{:S(2)}) collective-permute-start(bf16[784,128]{1,0:T(8,128)(2,1)S(1)} %collective-permute-done.refs_1_), channel_id=1, source_target_pairs={{0,4},{1,5},{4,8},{5,9},{8,12},{9,13},{12,14},{13,15},{14,10},{15,... | collective-permute-start | bytes 602120 | tf_op jit(solution)/shard_map/ppermute | solution.py:354
  11.7 22.1 %copy-start.6 = (bf16[784,128]{1,0:T(8,128)(2,1)}, bf16[784,128]{1,0:T(8,128)(2,1)S(1)}, u32[]{:S(2)}) copy-start(bf16[784,128]{1,0:T(8,128)(2,1)S(1)} %collective-permute-done.3.refs_2_) | copy-start | bytes 602116
  11.7 5.9 %collective-permute-start.4 = (bf16[784,128]{1,0:T(8,128)(2,1)S(1)}, bf16[784,128]{1,0:T(8,128)(2,1)S(1)}, u32[]{:S(2)}, u32[]{:S(2)}) collective-permute-start(bf16[784,128]{1,0:T(8,128)(2,1)S(1)} %collective-permute-done.3.refs_2_), channel_id=1, source_target_pairs={{0,2},{1,3},{4,0},{5,1},{8,4},{9,5},{12,8},{13,9},{14,12},{15,13},... | collective-permute-start | bytes 602120 | tf_op jit(solution)/shard_map/ppermute | solution.py:354
  16.1 17.8 %copy-start.7 = (bf16[784,128]{1,0:T(8,128)(2,1)}, bf16[784,128]{1,0:T(8,128)(2,1)S(1)}, u32[]{:S(2)}) copy-start(bf16[784,128]{1,0:T(8,128)(2,1)S(1)} %collective-permute-done.1.refs_3_) | copy-start | bytes 602116
  16.1 5.7 %collective-permute-start.2 = (bf16[784,128]{1,0:T(8,128)(2,1)S(1)}, bf16[784,128]{1,0:T(8,128)(2,1)S(1)}, u32[]{:S(2)}, u32[]{:S(2)}) collective-permute-start(bf16[784,128]{1,0:T(8,128)(2,1)S(1)} %collective-permute-done.1.refs_3_), channel_id=1, source_target_pairs={{0,4},{1,5},{4,8},{5,9},{8,12},{9,13},{12,14},{13,15},{14,10},{15,... | collective-permute-start | bytes 602120 | tf_op jit(solution)/shard_map/ppermute | solution.py:354
  17.6 16.3 %copy-start.8 = (bf16[784,128]{1,0:T(8,128)(2,1)}, bf16[784,128]{1,0:T(8,128)(2,1)S(1)}, u32[]{:S(2)}) copy-start(bf16[784,128]{1,0:T(8,128)(2,1)S(1)} %collective-permute-done.4.refs_4_) | copy-start | bytes 602116
  17.6 5.7 %collective-permute-start.5 = (bf16[784,128]{1,0:T(8,128)(2,1)S(1)}, bf16[784,128]{1,0:T(8,128)(2,1)S(1)}, u32[]{:S(2)}, u32[]{:S(2)}) collective-permute-start(bf16[784,128]{1,0:T(8,128)(2,1)S(1)} %collective-permute-done.4.refs_4_), channel_id=1, source_target_pairs={{0,2},{1,3},{4,0},{5,1},{8,4},{9,5},{12,8},{13,9},{14,12},{15,13},... | collective-permute-start | bytes 602120 | tf_op jit(solution)/shard_map/ppermute | solution.py:354
  21.8 13.4 %copy-start.3 = (bf16[784,128]{1,0:T(8,128)(2,1)}, bf16[784,128]{1,0:T(8,128)(2,1)S(1)}, u32[]{:S(2)}) copy-start(bf16[784,128]{1,0:T(8,128)(2,1)S(1)} %collective-permute-done.2.refs_5_) | copy-start | bytes 602116
  23.3 11.9 %copy-start.4 = (bf16[784,128]{1,0:T(8,128)(2,1)}, bf16[784,128]{1,0:T(8,128)(2,1)S(1)}, u32[]{:S(2)}) copy-start(bf16[784,128]{1,0:T(8,128)(2,1)S(1)} %collective-permute-done.5.refs_6_) | copy-start | bytes 602116
  23.3 21.9 %all-to-all-start = ((bf16[16,160,128]{2,1,0:T(8,128)(2,1)}), bf16[16,160,128]{2,1,0:T(8,128)(2,1)S(1)}, u32[]{:S(2)}, u32[]{:S(2)}) async-start(bf16[16,160,128]{2,1,0:T(8,128)(2,1)} %prep.1), calls=%async_computation | async-start | bytes 1310720 | tf_op jit(solution)/shard_map/all_to_all | solution.py:386
  28.3 1.5 %collective-permute-start.8 = (bf16[784,128]{1,0:T(8,128)(2,1)S(1)}, bf16[784,128]{1,0:T(8,128)(2,1)S(1)}, u32[]{:S(2)}, u32[]{:S(2)}) collective-permute-start(bf16[784,128]{1,0:T(8,128)(2,1)S(1)} %copy-done.2), channel_id=1, source_target_pairs={{0,1},{1,0},{2,3},{3,2},{4,5},{5,4},{6,7},{7,6},{8,9},{9,8},{10,11... | collective-permute-start | bytes 602120 | tf_op jit(solution)/shard_map/ppermute | solution.py:357
  28.7 1.5 %collective-permute-start.10 = (bf16[784,128]{1,0:T(8,128)(2,1)S(1)}, bf16[784,128]{1,0:T(8,128)(2,1)S(1)}, u32[]{:S(2)}, u32[]{:S(2)}) collective-permute-start(bf16[784,128]{1,0:T(8,128)(2,1)S(1)} %collective-permute-done.3.refs_2_), channel_id=1, source_target_pairs={{0,1},{1,0},{2,3},{3,2},{4,5},{5,4},{6,7},{7,6},{8,9},{9,8},{10,11... | collective-permute-start | bytes 602120 | tf_op jit(solution)/shard_map/ppermute | solution.py:357
  28.8 2.3 %collective-permute-start.9 = (bf16[784,128]{1,0:T(8,128)(2,1)S(1)}, bf16[784,128]{1,0:T(8,128)(2,1)S(1)}, u32[]{:S(2)}, u32[]{:S(2)}) collective-permute-start(bf16[784,128]{1,0:T(8,128)(2,1)S(1)} %collective-permute-done.refs_1_), channel_id=1, source_target_pairs={{0,1},{1,0},{2,3},{3,2},{4,5},{5,4},{6,7},{7,6},{8,9},{9,8},{10,11... | collective-permute-start | bytes 602120 | tf_op jit(solution)/shard_map/ppermute | solution.py:357
  29.2 4.3 %collective-permute-start.11 = (bf16[784,128]{1,0:T(8,128)(2,1)S(1)}, bf16[784,128]{1,0:T(8,128)(2,1)S(1)}, u32[]{:S(2)}, u32[]{:S(2)}) collective-permute-start(bf16[784,128]{1,0:T(8,128)(2,1)S(1)} %collective-permute-done.1.refs_3_), channel_id=1, source_target_pairs={{0,1},{1,0},{2,3},{3,2},{4,5},{5,4},{6,7},{7,6},{8,9},{9,8},{10,11... | collective-permute-start | bytes 602120 | tf_op jit(solution)/shard_map/ppermute | solution.py:357
  29.4 4.5 %collective-permute-start.12 = (bf16[784,128]{1,0:T(8,128)(2,1)S(1)}, bf16[784,128]{1,0:T(8,128)(2,1)S(1)}, u32[]{:S(2)}, u32[]{:S(2)}) collective-permute-start(bf16[784,128]{1,0:T(8,128)(2,1)S(1)} %collective-permute-done.4.refs_4_), channel_id=1, source_target_pairs={{0,1},{1,0},{2,3},{3,2},{4,5},{5,4},{6,7},{7,6},{8,9},{9,8},{10,11... | collective-permute-start | bytes 602120 | tf_op jit(solution)/shard_map/ppermute | solution.py:357
  29.8 4.1 %copy-start.9 = (bf16[784,128]{1,0:T(8,128)(2,1)}, bf16[784,128]{1,0:T(8,128)(2,1)S(1)}, u32[]{:S(2)}) copy-start(bf16[784,128]{1,0:T(8,128)(2,1)S(1)} %collective-permute-done.8.refs_7_) | copy-start | bytes 602116
  29.8 4.0 %collective-permute-start.13 = (bf16[784,128]{1,0:T(8,128)(2,1)S(1)}, bf16[784,128]{1,0:T(8,128)(2,1)S(1)}, u32[]{:S(2)}, u32[]{:S(2)}) collective-permute-start(bf16[784,128]{1,0:T(8,128)(2,1)S(1)} %collective-permute-done.2.refs_5_), channel_id=1, source_target_pairs={{0,1},{1,0},{2,3},{3,2},{4,5},{5,4},{6,7},{7,6},{8,9},{9,8},{10,11... | collective-permute-start | bytes 602120 | tf_op jit(solution)/shard_map/ppermute | solution.py:357
  30.2 3.7 %copy-start.10 = (bf16[784,128]{1,0:T(8,128)(2,1)}, bf16[784,128]{1,0:T(8,128)(2,1)S(1)}, u32[]{:S(2)}) copy-start(bf16[784,128]{1,0:T(8,128)(2,1)S(1)} %collective-permute-done.10.refs_9_) | copy-start | bytes 602116
  30.2 3.7 %collective-permute-start.14 = (bf16[784,128]{1,0:T(8,128)(2,1)S(1)}, bf16[784,128]{1,0:T(8,128)(2,1)S(1)}, u32[]{:S(2)}, u32[]{:S(2)}) collective-permute-start(bf16[784,128]{1,0:T(8,128)(2,1)S(1)} %collective-permute-done.5.refs_6_), channel_id=1, source_target_pairs={{0,1},{1,0},{2,3},{3,2},{4,5},{5,4},{6,7},{7,6},{8,9},{9,8},{10,11... | collective-permute-start | bytes 602120 | tf_op jit(solution)/shard_map/ppermute | solution.py:357
  31.1 2.8 %copy-start.11 = (bf16[784,128]{1,0:T(8,128)(2,1)}, bf16[784,128]{1,0:T(8,128)(2,1)S(1)}, u32[]{:S(2)}) copy-start(bf16[784,128]{1,0:T(8,128)(2,1)S(1)} %collective-permute-done.9.refs_8_) | copy-start | bytes 602116
  31.1 12.3 %collective-permute-start.6 = (bf16[400,128]{1,0:T(8,128)(2,1)}, bf16[400,128]{1,0:T(8,128)(2,1)S(1)}, u32[]{:S(2)}, u32[]{:S(2)}) collective-permute-start(bf16[400,128]{1,0:T(8,128)(2,1)} %slice.6), channel_id=1, source_target_pairs={{0,4},{1,5},{4,8},{5,9},{8,12},{9,13},{12,14},{13,15},{14,10},{15,... | collective-permute-start | bytes 307208 | tf_op jit(solution)/shard_map/ppermute | solution.py:354
  33.6 0.7 copy-start.12
  33.6 9.8 %collective-permute-start.7 = (bf16[384,128]{1,0:T(8,128)(2,1)}, bf16[384,128]{1,0:T(8,128)(2,1)S(1)}, u32[]{:S(2)}, u32[]{:S(2)}) collective-permute-start(bf16[384,128]{1,0:T(8,128)(2,1)} %slice.7), channel_id=1, source_target_pairs={{0,2},{1,3},{4,0},{5,1},{8,4},{9,5},{12,8},{13,9},{14,12},{15,13},... | collective-permute-start | bytes 294920 | tf_op jit(solution)/shard_map/ppermute | solution.py:354
  33.9 0.7 copy-start.13
  33.9 1.4 %copy-start.14 = (bf16[784,128]{1,0:T(8,128)(2,1)}, bf16[784,128]{1,0:T(8,128)(2,1)S(1)}, u32[]{:S(2)}) copy-start(bf16[784,128]{1,0:T(8,128)(2,1)S(1)} %collective-permute-done.13.refs_12_) | copy-start | bytes 602116
  34.5 0.7 copy-start.15
  43.4 1.5 %collective-permute-start.15 = (bf16[400,128]{1,0:T(8,128)(2,1)S(1)}, bf16[400,128]{1,0:T(8,128)(2,1)S(1)}, u32[]{:S(2)}, u32[]{:S(2)}) collective-permute-start(bf16[400,128]{1,0:T(8,128)(2,1)S(1)} %collective-permute-done.6.refs_0_), channel_id=1, source_target_pairs={{0,1},{1,0},{2,3},{3,2},{4,5},{5,4},{6,7},{7,6},{8,9},{9,8},{10,11... | collective-permute-start | bytes 307208 | tf_op jit(solution)/shard_map/ppermute | solution.py:357
  43.5 1.4 %collective-permute-start.16 = (bf16[384,128]{1,0:T(8,128)(2,1)S(1)}, bf16[384,128]{1,0:T(8,128)(2,1)S(1)}, u32[]{:S(2)}, u32[]{:S(2)}) collective-permute-start(bf16[384,128]{1,0:T(8,128)(2,1)S(1)} %collective-permute-done.7.refs_1_), channel_id=1, source_target_pairs={{0,1},{1,0},{2,3},{3,2},{4,5},{5,4},{6,7},{7,6},{8,9},{9,8},{10,11... | collective-permute-start | bytes 294920 | tf_op jit(solution)/shard_map/ppermute | solution.py:357
  45.2 27.5 %copy-start = (s32[16,1]{0,1:T(1,128)S(1)}, s32[16,1]{0,1:T(1,128)}, u32[]{:S(2)}) copy-start(s32[16,1]{0,1:T(1,128)} %param.17) | copy-start | bytes 196

commit v5 on v4

--- a/solution.py
+++ b/solution.py
@@ -64,6 +64,18 @@
         count_ref[b] = rank + 1
 
 
+def ring_place(me, chips):
+    chip = me // 2
+    return jnp.where(lax.rem(chip, 2) == 0, chip // 2, chips - 1 - chip // 2)
+
+
+def has_short_way(me, chips):
+    if chips != 8:
+        return jnp.bool_(False)
+    place = lax.rem(ring_place(me, chips), 4)
+    return (place == 1) | (place == 2)
+
+
 def prep_kernel(owner_ref, q_hbm, kv_hbm, after_hbm, out_ref, index_ref, count_ref, q_ref, kv_ref, q3_ref, kv3_ref, sems):
     del after_hbm
     rows, q_width = q_ref.shape
@@ -128,7 +140,7 @@
     return jnp.where(pick == 0, both[0:rows], both[rows:])
 
 
-def gather_kernel(whole, split, me_ref, mask_ref, pk_hbm, pv_hbm, *refs):
+def gather_kernel(whole, branches, short, me_ref, mask_ref, pk_hbm, pv_hbm, *refs):
     sources = refs[:whole]
     near_key, near_value, bias_ref, far_key_hbm, far_value_hbm = refs[whole : whole + 5]
     far_key, far_value, taken_ref, *blocks, sems = refs[whole + 5 :]
@@ -138,7 +150,6 @@
     prompt = pk_hbm.shape[1]
     live = (blocks[0].shape[0] - TILE) // slabs
     rows = live // 2
-    branches = whole + split
     middle = kv_heads * live
     start = starter(sems)
     moves = [start(source, target) for source, target in zip(sources, blocks)]
@@ -155,8 +166,11 @@
     for copy in moves:
         copy.wait()
     slot = jnp.int32(0)
-    for block in blocks:
+    straight = has_short_way(me_ref[0], branches // 2)
+    for n, block in enumerate(blocks):
         pick, length = picked(block[middle : middle + TILE, :], me_ref[0], branches)
+        if n >= whole - short:
+            pick, length = jnp.where(straight, pick, -1), jnp.where(straight, length, 0)
         at = pl.multiple_of(jnp.minimum(slot * rows, room - rows), 8)
         place = column - at
         seen = seen | ((place >= 0) & (place < length))
@@ -186,9 +200,9 @@
 
 
 def attend_kernel(split, me_ref, near_key, near_value, bias_ref, recv_ref, *refs):
-    halves = refs[: 2 * split]
+    halves = refs[:split]
     far_key_hbm, far_value_hbm, out_ref, late_key_ref, late_value_ref, first_ref, second_ref, far_key, far_value, sems = (
-        refs[2 * split :]
+        refs[split:]
     )
     near, early, _ = near_key.shape
     kv_heads = near + far_key.shape[0]
@@ -200,7 +214,8 @@
     heads = kv_heads * GRP
     width = branches * CAP
     late = late_key_ref.shape[1]
-    live = halves[1].shape[0] // kv_heads
+    live = (halves[0].shape[0] - TILE) // (2 * kv_heads)
+    middle = kv_heads * live
     far = live // 2
     tail = late - width - split * far
     main = early - tail
@@ -223,11 +238,14 @@
         first = heads * CAP + which * TILE
         rows = recv_ref[:, first : first + TILE, :].reshape(size, HD)
         unique.append(jnp.dot(choose, rows, preferred_element_type=jnp.float32).reshape(kv_heads, width, HD))
-    choices = [picked(halves[2 * n][kv_heads * live :, :], me_ref[0], branches) for n in range(split)]
+    choices = [picked(halves[n][middle : middle + TILE, :], me_ref[0], branches) for n in range(split)]
+    straight = has_short_way(me_ref[0], branches // 2)
+    choices = [(pick, jnp.where(straight, 0, length)) for pick, length in choices]
 
     def fill(g):
         for which, target in ((0, late_key_ref), (1, late_value_ref)):
-            rows = [rows_picked(halves[2 * n + which][g * live : (g + 1) * live, :], choices[n][0]) for n in range(split)]
+            at = which * (middle + TILE) + g * live
+            rows = [rows_picked(halves[n][at : at + live, :], choices[n][0]) for n in range(split)]
             if tail:
                 rows = [early_of[g][which][main:early, :].astype(jnp.float32)] + rows
             target[g] = jnp.concatenate(rows + [unique[which][g]], axis=0).astype(jnp.bfloat16)
@@ -345,13 +363,12 @@
 
     order = list(range(0, chips, 2)) + list(range(1, chips, 2))[::-1]
 
+    def hop(x, places):
+        pairs = [(order[p] * 2 + core, order[q] * 2 + core) for p, q in places for core in range(2)]
+        return lax.ppermute(x, "branch", pairs)
+
     def along(x, step):
-        pairs = [
-            (order[p] * 2 + core, order[(p + step) % chips] * 2 + core)
-            for p in range(chips)
-            for core in range(2)
-        ]
-        return lax.ppermute(x, "branch", pairs)
+        return hop(x, [(p, (p + step) % chips) for p in range(chips)])
 
     def across(x):
         return lax.ppermute(x, "branch", [(i, i ^ 1) for i in range(branches)])
@@ -375,19 +392,27 @@
         name="prep",
     )(owner_of, unique_q, unique_kv, block)
 
-    blocks = [block]
+    me = jnp.full((1,), lax.axis_index("branch"), jnp.int32)
+    blocks, shorts = [block], []
     ahead = behind = block
     for step in range(chips // 2 - 1):
         ahead, behind = along(ahead, 1), along(behind, -1)
         blocks += [ahead, behind]
         if step == 0:
             send, ahead = lax.optimization_barrier((send, ahead))
-    send, ahead, behind = lax.optimization_barrier((send, ahead, behind))
+        if step == 0 and chips == 8:
+            place = lax.rem(ring_place(me[0], chips), 4)
+            facing = jnp.where(place == 2, ahead, behind)
+            shorts = [hop(facing, [(1, 6), (6, 1), (2, 5), (5, 2)])]
+    send, ahead, behind, *shorts = lax.optimization_barrier((send, ahead, behind, *shorts))
     recv = lax.all_to_all(send, "branch", split_axis=0, concat_axis=0, tiled=True)
-    cut = kv_heads * live + TILE
-    halves = [along(ahead[:cut], 1), along(behind[cut:], -1)]
-    blocks = blocks + [across(x) for x in blocks]
-    me = jnp.full((1,), lax.axis_index("branch"), jnp.int32)
+    if shorts:
+        last = jnp.where(lax.rem(ring_place(me[0], chips), 4) == 0, behind, ahead)
+        halves = [hop(last, [(7, 0), (0, 7), (3, 4), (4, 3)])]
+    else:
+        halves = [along(ahead, 1)]
+    shorts = shorts + [across(x) for x in shorts]
+    blocks = blocks + [across(x) for x in blocks] + shorts
     prompt = prompt_k.shape[1]
     whole, split = len(blocks), 2
     room = branches * 3 // 4 * result_rows
@@ -399,7 +424,7 @@
     arrays = [pltpu.with_memory_space_constraint(x, pltpu.HBM) for x in (prompt_k, prompt_v, *blocks)]
     near = kv_heads // 2 - 1
     keys, values, bias, *far_early = pl.pallas_call(
-        functools.partial(gather_kernel, whole, split),
+        functools.partial(gather_kernel, whole, branches, len(shorts)),
         out_shape=(
             pltpu.VMEM((near, early, HD), jnp.bfloat16),
             pltpu.VMEM((near, early, HD), jnp.bfloat16),
@@ -426,7 +451,7 @@
     outputs = pl.pallas_call(
         functools.partial(attend_kernel, split),
         out_shape=bf16(branches, CAP * heads, HD),
-        in_specs=[SMEM] + [VMEM] * (4 + 2 * split) + [ANY] * 2,
+        in_specs=[SMEM] + [VMEM] * (4 + split) + [ANY] * 2,
         out_specs=VMEM,
         scratch_shapes=[
             pltpu.VMEM((kv_heads, late, HD), jnp.bfloat16),

time: 74.5 us -> 73.1 us (0.981)
  blocking collectives: 21.9 us -> 18.9 us
  starting transfers between devices: 16.8 us -> 18.9 us
  local copies, waits for them, and re-layouts: 2.62 us -> 0.8 us
  Pallas kernels: 19.7 us -> 21.4 us
    all_to_all x1, blocking collectives: 21.9 us -> 18.9 us  [body(): lax.all_to_all(outputs, 'branch', split_axis=0, concat_axis=0, tiled=True)]
    ppermute x8, starting transfers between devices: 9.21 us -> 11.5 us  [hop(): return lax.ppermute(x, 'branch', pairs)]
    slice x2 -> x0, local copies, waits for them, and re-layouts: 1.29 us -> none  [body(): halves = [along(ahead[:cut], 1), along(behind[cut:], -1)]]
    pallas_call x1, Pallas kernels: 5.53 us -> 6.6 us  [body(): pl.pallas_call(functools.partial(attend_kernel, split), out_shape=bf16(br...]
  transfers between devices with their start and end apart: 18 -> 18, of which waited for: 7 -> 6; matrix products, arithmetic and copies ran while one was open for 2% -> 0% of each run, Pallas kernels for 15% -> 16%
where the time goes in v5:
time: 73.1 us; the launch traced here: 72.7 us
  Pallas kernels  21.4 us (29%)
  starting transfers between devices  18.9 us (26%)
  blocking collectives  18.9 us (26%)
  waiting for transfers between devices  12.4 us (17%)
  local copies, waits for them, and re-layouts  0.8 us (1%)
    all_to_all x1, blocking collectives, body(): lax.all_to_all(outputs, 'branch', split_axis=0, concat_axis=0, tiled=True)  18.9 us
    ppermute x8, starting transfers between devices, hop(): return lax.ppermute(x, 'branch', pairs)  11.5 us
    ppermute x8, waiting for transfers between devices, hop(): return lax.ppermute(x, 'branch', pairs)  10.9 us
    pallas_call x1, Pallas kernels, body(): pl.pallas_call(functools.partial(gather_kernel, whole, branches, len(shor...  8.74 us
    pallas_call x1, Pallas kernels, body(): pl.pallas_call(functools.partial(attend_kernel, split), out_shape=bf16(br...  6.6 us
    all_to_all x1, starting transfers between devices, body(): lax.all_to_all(send, 'branch', split_axis=0, concat_axis=0, tiled=True)  4.93 us
    pallas_call x1, Pallas kernels, body(): pl.pallas_call(prep_kernel, out_shape=bf16(branches, slot_rows, HD), in_s...  2.79 us
    ppermute x9, starting transfers between devices, across(): return lax.ppermute(x, 'branch', [(i, i ^ 1) for i in range(branches)])  2.5 us
  transfers between devices with their start and end apart: 18, of which 6 were waited for; matrix products, arithmetic and copies ran while one was open for 0% of the time, Pallas kernels for 16%

profile of v5, /device:TPU:0, one launch (start us, length us, event | category | flops | bytes accessed | tf_op | source)
XLA Modules:
  0.0 72.7 jit_solution(1981169783120449862)
XLA Ops:
  0.0 1.7 %payload.1.after_hbm.refs_0_ = bf16[784,128]{1,0:T(8,128)(2,1)} custom-call(s32[1,16]{1,0:T(1,128)} %pick_hbm.1, s32[1,2]{1,0:T(1,128)} %bitcast.5, bf16[2,24,2048]{2,1,0:T(8,128)(2,1)} %shared_hbm.1), custom_call_target="tpu_custom_call" | custom-call | tf_op jit(solution)/shard_map/payload/pallas_call | solution.py:349
  1.7 0.0 copy-start.2
  1.7 3.1 %collective-permute-start = (bf16[784,128]{1,0:T(8,128)(2,1)}, bf16[784,128]{1,0:T(8,128)(2,1)S(1)}, u32[]{:S(2)}, u32[]{:S(2)}) collective-permute-start(bf16[784,128]{1,0:T(8,128)(2,1)} %payload.1.after_hbm.refs_0_), channel_id=1, source_target_pairs={{0,4},{1,5},{4,8},{5,9},{8,12},{9,13},{12,14},{13,15},{14,10},{15,... | collective-permute-start | bytes 602120 | tf_op jit(solution)/shard_map/ppermute | solution.py:368
  4.8 0.0 collective-permute-start.3
  4.8 2.8 %prep.1 = bf16[16,160,128]{2,1,0:T(8,128)(2,1)} custom-call(s32[16]{0:T(128)} %bitcast.3, bf16[16,8192]{1,0:T(8,128)(2,1)} %q_hbm.1, bf16[16,2048]{1,0:T(8,128)(2,1)} %kv_hbm.1, bf16[784,128]{1,0:T(8,128)(2,1)} %payload.1.after_hbm.refs_0_), custom_call_target="tpu_custom_call" | custom-call | bytes 1024 | tf_op jit(solution)/shard_map/prep/pallas_call | solution.py:376
  7.6 2.3 %collective-permute-done.refs_1_ = bf16[784,128]{1,0:T(8,128)(2,1)S(1)} collective-permute-done((bf16[784,128]{1,0:T(8,128)(2,1)}, bf16[784,128]{1,0:T(8,128)(2,1)S(1)}, u32[]{:S(2)}, u32[]{:S(2)}) %collective-permute-start) | collective-permute-done | bytes 200736 | tf_op jit(solution)/shard_map/ppermute | solution.py:368
  10.0 1.8 %collective-permute-start.1 = (bf16[784,128]{1,0:T(8,128)(2,1)S(1)}, bf16[784,128]{1,0:T(8,128)(2,1)S(1)}, u32[]{:S(2)}, u32[]{:S(2)}) collective-permute-start(bf16[784,128]{1,0:T(8,128)(2,1)S(1)} %collective-permute-done.refs_1_), channel_id=1, source_target_pairs={{0,4},{1,5},{4,8},{5,9},{8,12},{9,13},{12,14},{13,15},{14,10},{15,... | collective-permute-start | bytes 602120 | tf_op jit(solution)/shard_map/ppermute | solution.py:368
  11.7 0.0 collective-permute-done.3.refs_2_
  11.7 0.2 collective-permute-start.4
  12.0 0.7 collective-permute-start.6
  12.7 3.4 %collective-permute-done.1.refs_3_ = bf16[784,128]{1,0:T(8,128)(2,1)S(1)} collective-permute-done((bf16[784,128]{1,0:T(8,128)(2,1)S(1)}, bf16[784,128]{1,0:T(8,128)(2,1)S(1)}, u32[]{:S(2)}, u32[]{:S(2)}) %collective-permute-start.1) | collective-permute-done | bytes 200736 | tf_op jit(solution)/shard_map/ppermute | solution.py:368
  16.1 1.5 %collective-permute-start.2 = (bf16[784,128]{1,0:T(8,128)(2,1)S(1)}, bf16[784,128]{1,0:T(8,128)(2,1)S(1)}, u32[]{:S(2)}, u32[]{:S(2)}) collective-permute-start(bf16[784,128]{1,0:T(8,128)(2,1)S(1)} %collective-permute-done.1.refs_3_), channel_id=1, source_target_pairs={{0,4},{1,5},{4,8},{5,9},{8,12},{9,13},{12,14},{13,15},{14,10},{15,... | collective-permute-start | bytes 602120 | tf_op jit(solution)/shard_map/ppermute | solution.py:368
  17.6 0.0 collective-permute-done.4.refs_4_
  17.6 0.6 collective-permute-start.5
  18.2 0.0 collective-permute-done.6.refs_14_
  18.2 3.7 %collective-permute-done.2.refs_5_ = bf16[784,128]{1,0:T(8,128)(2,1)S(1)} collective-permute-done((bf16[784,128]{1,0:T(8,128)(2,1)S(1)}, bf16[784,128]{1,0:T(8,128)(2,1)S(1)}, u32[]{:S(2)}, u32[]{:S(2)}) %collective-permute-start.2) | collective-permute-done | bytes 200736 | tf_op jit(solution)/shard_map/ppermute | solution.py:368
  21.8 1.5 %collective-permute-done.5.refs_6_ = bf16[784,128]{1,0:T(8,128)(2,1)S(1)} collective-permute-done((bf16[784,128]{1,0:T(8,128)(2,1)S(1)}, bf16[784,128]{1,0:T(8,128)(2,1)S(1)}, u32[]{:S(2)}, u32[]{:S(2)}) %collective-permute-start.5) | collective-permute-done | bytes 200736 | tf_op jit(solution)/shard_map/ppermute | solution.py:368
  23.3 4.9 %all-to-all-start = ((bf16[16,160,128]{2,1,0:T(8,128)(2,1)}), bf16[16,160,128]{2,1,0:T(8,128)(2,1)S(1)}, u32[]{:S(2)}, u32[]{:S(2)}) async-start(bf16[16,160,128]{2,1,0:T(8,128)(2,1)} %prep.1), calls=%async_computation | async-start | bytes 1310720 | tf_op jit(solution)/shard_map/all_to_all | solution.py:408
  28.3 0.5 collective-permute-start.8
  28.7 0.1 collective-permute-start.10
  28.8 0.4 collective-permute-start.9
  29.2 0.1 collective-permute-start.11
  29.4 0.4 collective-permute-start.12
  29.8 0.1 collective-permute-done.8.refs_7_
  29.8 0.4 collective-permute-start.15
  30.2 0.0 collective-permute-done.10.refs_9_
  30.2 0.3 collective-permute-start.13
  30.5 0.0 collective-permute-done.9.refs_8_
  30.5 0.3 collective-permute-start.14
  30.8 0.0 collective-permute-done.11.refs_10_
  30.8 0.0 copy-start.13
  30.8 3.7 %collective-permute-start.7 = (bf16[784,128]{1,0:T(8,128)(2,1)S(1)}, bf16[784,128]{1,0:T(8,128)(2,1)S(1)}, u32[]{:S(2)}, u32[]{:S(2)}) collective-permute-start(bf16[784,128]{1,0:T(8,128)(2,1)S(1)} %broadcast_select_fusion.1), channel_id=1, source_target_pairs={{2,0},{3,1},{0,2},{1,3},{12,14},{13,15},{14,12},{15,13},{18,16},{1... | collective-permute-start | bytes 602120 | tf_op jit(solution)/shard_map/ppermute | solution.py:368
  34.5 0.0 collective-permute-done.12.refs_11_
  34.5 0.0 collective-permute-done.15.refs_15_
  34.5 0.0 collective-permute-done.13.refs_12_
  34.5 0.0 collective-permute-done.14.refs_13_
  34.7 0.5 copy-done.14
  35.2 0.1 copy-done.15
  35.2 0.1 copy-done.16
  35.3 0.1 copy-done.17
  35.4 8.7 %gather.1 = (bf16[3,1312,128]{2,1,0:T(8,128)(2,1)S(1)}, bf16[3,1312,128]{2,1,0:T(8,128)(2,1)S(1)}, f32[1,1312]{1,0:T(1,128)S(1)}, bf16[5,1312,128]{2,1,0:T(8,128)(2,1)}, bf16[5,1312,128]{2,1,0:T(8,128)(2,1)}) custom-call(s32[1]{0:T(128)} %bitcast.1.me_ref, s32[1,8]{1,0:T(1,128)S(1)} %copy-done.1, bf16[1,1024,1024]{2,1,0:T(8,128)(2,1)} %pk_hbm.1, ...), custom_call_target="tpu_custom_call" | custom-call | bytes 8388608 | tf_op jit(solution)/shard_map/gather/pallas_call | solution.py:426
  44.2 0.0 collective-permute-done.7.refs_0_
  44.2 0.1 collective-permute-start.16
  44.2 1.4 %collective-permute-done.16.refs_1_ = bf16[784,128]{1,0:T(8,128)(2,1)S(1)} collective-permute-done((bf16[784,128]{1,0:T(8,128)(2,1)S(1)}, bf16[784,128]{1,0:T(8,128)(2,1)S(1)}, u32[]{:S(2)}, u32[]{:S(2)}) %collective-permute-start.16) | collective-permute-done | bytes 200736 | tf_op jit(solution)/shard_map/ppermute | solution.py:374
  45.7 0.0 all-to-all-done.recv_ref
  45.7 6.6 %attend.1 = bf16[16,128,128]{2,1,0:T(8,128)(2,1)S(1)} custom-call(s32[1]{0:T(128)} %bitcast.1.me_ref, bf16[3,1312,128]{2,1,0:T(8,128)(2,1)S(1)} %get-tuple-element.26.near_key, bf16[3,1312,128]{2,1,0:T(8,128)(2,1)S(1)} %get-tuple-element.27.near_value, f32[1,1312]{1,0:T(1,128)S(1)} %get-tuple-element.28.bias_ref, ...), custom_call_target="tpu_custom_call" | custom-call | flops 1409286144 | bytes 4194304 | tf_op jit(solution)/shard_map/attend/pallas_call | solution.py:451
  52.3 18.9 %all_to_all.10.back_ref = bf16[16,128,128]{2,1,0:T(8,128)(2,1)S(1)} all-to-all(bf16[16,128,128]{2,1,0:T(8,128)(2,1)S(1)} %attend.1), channel_id=1, replica_groups=mesh['groups'=2,'branch'=16] {'branch'}, dimensions={0} | all-to-all | bytes 1048576 | tf_op jit(solution)/shard_map/all_to_all | solution.py:473
  71.2 1.5 %post.1 = bf16[16,8192]{1,0:T(8,128)(2,1)} custom-call(s32[16]{0:T(128)S(1)} %bitcast.4, bf16[16,128,128]{2,1,0:T(8,128)(2,1)S(1)} %all_to_all.10.back_ref), custom_call_target="tpu_custom_call" | custom-call | tf_op jit(solution)/shard_map/post/pallas_call | solution.py:474
  (32 shorter events, 0.1 us)
Async XLA Ops:
  0.0 35.4 %copy-start.1 = (s32[1,8]{1,0:T(1,128)S(1)}, s32[1,8]{1,0:T(1,128)}, u32[]{:S(2)}) copy-start(s32[1,8]{1,0:T(1,128)} %mask_ref.1) | copy-start | bytes 100
  1.7 26.5 %copy-start.2 = (bf16[784,128]{1,0:T(8,128)(2,1)S(1)}, bf16[784,128]{1,0:T(8,128)(2,1)}, u32[]{:S(2)}) copy-start(bf16[784,128]{1,0:T(8,128)(2,1)} %payload.1.after_hbm.refs_0_) | copy-start | bytes 602116
  1.7 8.2 %collective-permute-start = (bf16[784,128]{1,0:T(8,128)(2,1)}, bf16[784,128]{1,0:T(8,128)(2,1)S(1)}, u32[]{:S(2)}, u32[]{:S(2)}) collective-permute-start(bf16[784,128]{1,0:T(8,128)(2,1)} %payload.1.after_hbm.refs_0_), channel_id=1, source_target_pairs={{0,4},{1,5},{4,8},{5,9},{8,12},{9,13},{12,14},{13,15},{14,10},{15,... | collective-permute-start | bytes 602120 | tf_op jit(solution)/shard_map/ppermute | solution.py:368
  4.8 6.9 %collective-permute-start.3 = (bf16[784,128]{1,0:T(8,128)(2,1)}, bf16[784,128]{1,0:T(8,128)(2,1)S(1)}, u32[]{:S(2)}, u32[]{:S(2)}) collective-permute-start(bf16[784,128]{1,0:T(8,128)(2,1)} %payload.1.after_hbm.refs_0_), channel_id=1, source_target_pairs={{0,2},{1,3},{4,0},{5,1},{8,4},{9,5},{12,8},{13,9},{14,12},{15,13},... | collective-permute-start | bytes 602120 | tf_op jit(solution)/shard_map/ppermute | solution.py:368
  9.9 24.7 %copy-start.3 = (bf16[784,128]{1,0:T(8,128)(2,1)}, bf16[784,128]{1,0:T(8,128)(2,1)S(1)}, u32[]{:S(2)}) copy-start(bf16[784,128]{1,0:T(8,128)(2,1)S(1)} %collective-permute-done.refs_1_) | copy-start | bytes 602116
  10.0 6.2 %collective-permute-start.1 = (bf16[784,128]{1,0:T(8,128)(2,1)S(1)}, bf16[784,128]{1,0:T(8,128)(2,1)S(1)}, u32[]{:S(2)}, u32[]{:S(2)}) collective-permute-start(bf16[784,128]{1,0:T(8,128)(2,1)S(1)} %collective-permute-done.refs_1_), channel_id=1, source_target_pairs={{0,4},{1,5},{4,8},{5,9},{8,12},{9,13},{12,14},{13,15},{14,10},{15,... | collective-permute-start | bytes 602120 | tf_op jit(solution)/shard_map/ppermute | solution.py:368
  11.7 22.9 %copy-start.4 = (bf16[784,128]{1,0:T(8,128)(2,1)}, bf16[784,128]{1,0:T(8,128)(2,1)S(1)}, u32[]{:S(2)}) copy-start(bf16[784,128]{1,0:T(8,128)(2,1)S(1)} %collective-permute-done.3.refs_2_) | copy-start | bytes 602116
  11.7 5.9 %collective-permute-start.4 = (bf16[784,128]{1,0:T(8,128)(2,1)S(1)}, bf16[784,128]{1,0:T(8,128)(2,1)S(1)}, u32[]{:S(2)}, u32[]{:S(2)}) collective-permute-start(bf16[784,128]{1,0:T(8,128)(2,1)S(1)} %collective-permute-done.3.refs_2_), channel_id=1, source_target_pairs={{0,2},{1,3},{4,0},{5,1},{8,4},{9,5},{12,8},{13,9},{14,12},{15,13},... | collective-permute-start | bytes 602120 | tf_op jit(solution)/shard_map/ppermute | solution.py:368
  12.0 6.1 %collective-permute-start.6 = (bf16[784,128]{1,0:T(8,128)(2,1)S(1)}, bf16[784,128]{1,0:T(8,128)(2,1)S(1)}, u32[]{:S(2)}, u32[]{:S(2)}) collective-permute-start(bf16[784,128]{1,0:T(8,128)(2,1)S(1)} %broadcast_select_fusion), channel_id=1, source_target_pairs={{4,6},{5,7},{6,4},{7,5},{8,10},{9,11},{10,8},{11,9},{20,22},{21,23... | collective-permute-start | bytes 602120 | tf_op jit(solution)/shard_map/ppermute | solution.py:368
  16.1 14.7 %copy-start.7 = (bf16[784,128]{1,0:T(8,128)(2,1)}, bf16[784,128]{1,0:T(8,128)(2,1)S(1)}, u32[]{:S(2)}) copy-start(bf16[784,128]{1,0:T(8,128)(2,1)S(1)} %collective-permute-done.1.refs_3_) | copy-start | bytes 602116
  16.1 5.7 %collective-permute-start.2 = (bf16[784,128]{1,0:T(8,128)(2,1)S(1)}, bf16[784,128]{1,0:T(8,128)(2,1)S(1)}, u32[]{:S(2)}, u32[]{:S(2)}) collective-permute-start(bf16[784,128]{1,0:T(8,128)(2,1)S(1)} %collective-permute-done.1.refs_3_), channel_id=1, source_target_pairs={{0,4},{1,5},{4,8},{5,9},{8,12},{9,13},{12,14},{13,15},{14,10},{15,... | collective-permute-start | bytes 602120 | tf_op jit(solution)/shard_map/ppermute | solution.py:368
  17.6 17.0 %copy-start.8 = (bf16[784,128]{1,0:T(8,128)(2,1)}, bf16[784,128]{1,0:T(8,128)(2,1)S(1)}, u32[]{:S(2)}) copy-start(bf16[784,128]{1,0:T(8,128)(2,1)S(1)} %collective-permute-done.4.refs_4_) | copy-start | bytes 602116
  17.6 5.7 %collective-permute-start.5 = (bf16[784,128]{1,0:T(8,128)(2,1)S(1)}, bf16[784,128]{1,0:T(8,128)(2,1)S(1)}, u32[]{:S(2)}, u32[]{:S(2)}) collective-permute-start(bf16[784,128]{1,0:T(8,128)(2,1)S(1)} %collective-permute-done.4.refs_4_), channel_id=1, source_target_pairs={{0,2},{1,3},{4,0},{5,1},{8,4},{9,5},{12,8},{13,9},{14,12},{15,13},... | collective-permute-start | bytes 602120 | tf_op jit(solution)/shard_map/ppermute | solution.py:368
  18.2 16.4 %copy-start.9 = (bf16[784,128]{1,0:T(8,128)(2,1)}, bf16[784,128]{1,0:T(8,128)(2,1)S(1)}, u32[]{:S(2)}) copy-start(bf16[784,128]{1,0:T(8,128)(2,1)S(1)} %collective-permute-done.6.refs_14_) | copy-start | bytes 602116
  21.8 12.7 %copy-start.5 = (bf16[784,128]{1,0:T(8,128)(2,1)}, bf16[784,128]{1,0:T(8,128)(2,1)S(1)}, u32[]{:S(2)}) copy-start(bf16[784,128]{1,0:T(8,128)(2,1)S(1)} %collective-permute-done.2.refs_5_) | copy-start | bytes 602116
  23.3 11.3 %copy-start.6 = (bf16[784,128]{1,0:T(8,128)(2,1)}, bf16[784,128]{1,0:T(8,128)(2,1)S(1)}, u32[]{:S(2)}) copy-start(bf16[784,128]{1,0:T(8,128)(2,1)S(1)} %collective-permute-done.5.refs_6_) | copy-start | bytes 602116
  23.3 22.4 %all-to-all-start = ((bf16[16,160,128]{2,1,0:T(8,128)(2,1)}), bf16[16,160,128]{2,1,0:T(8,128)(2,1)S(1)}, u32[]{:S(2)}, u32[]{:S(2)}) async-start(bf16[16,160,128]{2,1,0:T(8,128)(2,1)} %prep.1), calls=%async_computation | async-start | bytes 1310720 | tf_op jit(solution)/shard_map/all_to_all | solution.py:408
  28.3 1.5 %collective-permute-start.8 = (bf16[784,128]{1,0:T(8,128)(2,1)S(1)}, bf16[784,128]{1,0:T(8,128)(2,1)S(1)}, u32[]{:S(2)}, u32[]{:S(2)}) collective-permute-start(bf16[784,128]{1,0:T(8,128)(2,1)S(1)} %copy-done.2), channel_id=1, source_target_pairs={{0,1},{1,0},{2,3},{3,2},{4,5},{5,4},{6,7},{7,6},{8,9},{9,8},{10,11... | collective-permute-start | bytes 602120 | tf_op jit(solution)/shard_map/ppermute | solution.py:374
  28.7 1.5 %collective-permute-start.10 = (bf16[784,128]{1,0:T(8,128)(2,1)S(1)}, bf16[784,128]{1,0:T(8,128)(2,1)S(1)}, u32[]{:S(2)}, u32[]{:S(2)}) collective-permute-start(bf16[784,128]{1,0:T(8,128)(2,1)S(1)} %collective-permute-done.3.refs_2_), channel_id=1, source_target_pairs={{0,1},{1,0},{2,3},{3,2},{4,5},{5,4},{6,7},{7,6},{8,9},{9,8},{10,11... | collective-permute-start | bytes 602120 | tf_op jit(solution)/shard_map/ppermute | solution.py:374
  28.8 1.6 %collective-permute-start.9 = (bf16[784,128]{1,0:T(8,128)(2,1)S(1)}, bf16[784,128]{1,0:T(8,128)(2,1)S(1)}, u32[]{:S(2)}, u32[]{:S(2)}) collective-permute-start(bf16[784,128]{1,0:T(8,128)(2,1)S(1)} %collective-permute-done.refs_1_), channel_id=1, source_target_pairs={{0,1},{1,0},{2,3},{3,2},{4,5},{5,4},{6,7},{7,6},{8,9},{9,8},{10,11... | collective-permute-start | bytes 602120 | tf_op jit(solution)/shard_map/ppermute | solution.py:374
  29.2 1.6 %collective-permute-start.11 = (bf16[784,128]{1,0:T(8,128)(2,1)S(1)}, bf16[784,128]{1,0:T(8,128)(2,1)S(1)}, u32[]{:S(2)}, u32[]{:S(2)}) collective-permute-start(bf16[784,128]{1,0:T(8,128)(2,1)S(1)} %collective-permute-done.1.refs_3_), channel_id=1, source_target_pairs={{0,1},{1,0},{2,3},{3,2},{4,5},{5,4},{6,7},{7,6},{8,9},{9,8},{10,11... | collective-permute-start | bytes 602120 | tf_op jit(solution)/shard_map/ppermute | solution.py:374
  29.4 5.1 %collective-permute-start.12 = (bf16[784,128]{1,0:T(8,128)(2,1)S(1)}, bf16[784,128]{1,0:T(8,128)(2,1)S(1)}, u32[]{:S(2)}, u32[]{:S(2)}) collective-permute-start(bf16[784,128]{1,0:T(8,128)(2,1)S(1)} %collective-permute-done.4.refs_4_), channel_id=1, source_target_pairs={{0,1},{1,0},{2,3},{3,2},{4,5},{5,4},{6,7},{7,6},{8,9},{9,8},{10,11... | collective-permute-start | bytes 602120 | tf_op jit(solution)/shard_map/ppermute | solution.py:374
  29.8 4.8 %copy-start.10 = (bf16[784,128]{1,0:T(8,128)(2,1)}, bf16[784,128]{1,0:T(8,128)(2,1)S(1)}, u32[]{:S(2)}) copy-start(bf16[784,128]{1,0:T(8,128)(2,1)S(1)} %collective-permute-done.8.refs_7_) | copy-start | bytes 602116
  29.8 4.7 %collective-permute-start.15 = (bf16[784,128]{1,0:T(8,128)(2,1)S(1)}, bf16[784,128]{1,0:T(8,128)(2,1)S(1)}, u32[]{:S(2)}, u32[]{:S(2)}) collective-permute-start(bf16[784,128]{1,0:T(8,128)(2,1)S(1)} %collective-permute-done.6.refs_14_), channel_id=1, source_target_pairs={{0,1},{1,0},{2,3},{3,2},{4,5},{5,4},{6,7},{7,6},{8,9},{9,8},{10,11... | collective-permute-start | bytes 602120 | tf_op jit(solution)/shard_map/ppermute | solution.py:374
  30.2 4.4 %copy-start.11 = (bf16[784,128]{1,0:T(8,128)(2,1)}, bf16[784,128]{1,0:T(8,128)(2,1)S(1)}, u32[]{:S(2)}) copy-start(bf16[784,128]{1,0:T(8,128)(2,1)S(1)} %collective-permute-done.10.refs_9_) | copy-start | bytes 602116
  30.2 4.3 %collective-permute-start.13 = (bf16[784,128]{1,0:T(8,128)(2,1)S(1)}, bf16[784,128]{1,0:T(8,128)(2,1)S(1)}, u32[]{:S(2)}, u32[]{:S(2)}) collective-permute-start(bf16[784,128]{1,0:T(8,128)(2,1)S(1)} %collective-permute-done.2.refs_5_), channel_id=1, source_target_pairs={{0,1},{1,0},{2,3},{3,2},{4,5},{5,4},{6,7},{7,6},{8,9},{9,8},{10,11... | collective-permute-start | bytes 602120 | tf_op jit(solution)/shard_map/ppermute | solution.py:374
  30.5 4.1 %copy-start.12 = (bf16[784,128]{1,0:T(8,128)(2,1)}, bf16[784,128]{1,0:T(8,128)(2,1)S(1)}, u32[]{:S(2)}) copy-start(bf16[784,128]{1,0:T(8,128)(2,1)S(1)} %collective-permute-done.9.refs_8_) | copy-start | bytes 602116
  30.5 4.1 %collective-permute-start.14 = (bf16[784,128]{1,0:T(8,128)(2,1)S(1)}, bf16[784,128]{1,0:T(8,128)(2,1)S(1)}, u32[]{:S(2)}, u32[]{:S(2)}) collective-permute-start(bf16[784,128]{1,0:T(8,128)(2,1)S(1)} %collective-permute-done.5.refs_6_), channel_id=1, source_target_pairs={{0,1},{1,0},{2,3},{3,2},{4,5},{5,4},{6,7},{7,6},{8,9},{9,8},{10,11... | collective-permute-start | bytes 602120 | tf_op jit(solution)/shard_map/ppermute | solution.py:374
  30.8 3.8 %copy-start.13 = (bf16[784,128]{1,0:T(8,128)(2,1)}, bf16[784,128]{1,0:T(8,128)(2,1)S(1)}, u32[]{:S(2)}) copy-start(bf16[784,128]{1,0:T(8,128)(2,1)S(1)} %collective-permute-done.11.refs_10_) | copy-start | bytes 602116
  30.8 13.3 %collective-permute-start.7 = (bf16[784,128]{1,0:T(8,128)(2,1)S(1)}, bf16[784,128]{1,0:T(8,128)(2,1)S(1)}, u32[]{:S(2)}, u32[]{:S(2)}) collective-permute-start(bf16[784,128]{1,0:T(8,128)(2,1)S(1)} %broadcast_select_fusion.1), channel_id=1, source_target_pairs={{2,0},{3,1},{0,2},{1,3},{12,14},{13,15},{14,12},{15,13},{18,16},{1... | collective-permute-start | bytes 602120 | tf_op jit(solution)/shard_map/ppermute | solution.py:368
  34.5 0.7 copy-start.14
  34.5 0.7 copy-start.15
  34.5 0.8 %copy-start.16 = (bf16[784,128]{1,0:T(8,128)(2,1)}, bf16[784,128]{1,0:T(8,128)(2,1)S(1)}, u32[]{:S(2)}) copy-start(bf16[784,128]{1,0:T(8,128)(2,1)S(1)} %collective-permute-done.13.refs_12_) | copy-start | bytes 602116
  34.6 0.8 %copy-start.17 = (bf16[784,128]{1,0:T(8,128)(2,1)}, bf16[784,128]{1,0:T(8,128)(2,1)S(1)}, u32[]{:S(2)}) copy-start(bf16[784,128]{1,0:T(8,128)(2,1)S(1)} %collective-permute-done.14.refs_13_) | copy-start | bytes 602116
  44.2 1.5 %collective-permute-start.16 = (bf16[784,128]{1,0:T(8,128)(2,1)S(1)}, bf16[784,128]{1,0:T(8,128)(2,1)S(1)}, u32[]{:S(2)}, u32[]{:S(2)}) collective-permute-start(bf16[784,128]{1,0:T(8,128)(2,1)S(1)} %collective-permute-done.7.refs_0_), channel_id=1, source_target_pairs={{0,1},{1,0},{2,3},{3,2},{4,5},{5,4},{6,7},{7,6},{8,9},{9,8},{10,11... | collective-permute-start | bytes 602120 | tf_op jit(solution)/shard_map/ppermute | solution.py:374
  45.7 25.5 %copy-start = (s32[16,1]{0,1:T(1,128)S(1)}, s32[16,1]{0,1:T(1,128)}, u32[]{:S(2)}) copy-start(s32[16,1]{0,1:T(1,128)} %param.17) | copy-start | bytes 196

commit v6 on v5

--- a/solution.py
+++ b/solution.py
@@ -167,7 +167,17 @@
         copy.wait()
     slot = jnp.int32(0)
     straight = has_short_way(me_ref[0], branches // 2)
+    early = pl.ds(0, prompt)
+    late = pl.ds(prompt, room)
+    leaving = []
     for n, block in enumerate(blocks):
+        if n == len(blocks) // 2:
+            for copy in wide:
+                copy.wait()
+            leaving += [
+                start(far_key.at[:, early, :], far_key_hbm.at[:, early, :]),
+                start(far_value.at[:, early, :], far_value_hbm.at[:, early, :]),
+            ]
         pick, length = picked(block[middle : middle + TILE, :], me_ref[0], branches)
         if n >= whole - short:
             pick, length = jnp.where(straight, pick, -1), jnp.where(straight, length, 0)
@@ -185,6 +195,10 @@
     for g, (key_ref, value_ref) in enumerate(homes):
         key_ref[prompt : prompt + room, :] = taken_ref[g].astype(jnp.bfloat16)
         value_ref[prompt : prompt + room, :] = taken_ref[kv_heads + g].astype(jnp.bfloat16)
+    leaving += [
+        start(far_key.at[:, late, :], far_key_hbm.at[:, late, :]),
+        start(far_value.at[:, late, :], far_value_hbm.at[:, late, :]),
+    ]
     blocks_seen = mask_ref.shape[1]
     biases = [
         jnp.full((1, prompt // blocks_seen), jnp.where(mask_ref[0, j] > 0, 0.0, NONE))
@@ -192,17 +206,14 @@
     ]
     bias = jnp.concatenate(biases + [jnp.where(seen, 0.0, NONE)], axis=1)
     bias_ref[...] = bias
-    for copy in wide:
-        copy.wait()
-    leaving = [start(far_key, far_key_hbm), start(far_value, far_value_hbm)]
     for copy in leaving:
         copy.wait()
 
 
 def attend_kernel(split, me_ref, near_key, near_value, bias_ref, recv_ref, *refs):
-    halves = refs[:split]
+    halves = refs[: 2 * split]
     far_key_hbm, far_value_hbm, out_ref, late_key_ref, late_value_ref, first_ref, second_ref, far_key, far_value, sems = (
-        refs[split:]
+        refs[2 * split :]
     )
     near, early, _ = near_key.shape
     kv_heads = near + far_key.shape[0]
@@ -214,8 +225,7 @@
     heads = kv_heads * GRP
     width = branches * CAP
     late = late_key_ref.shape[1]
-    live = (halves[0].shape[0] - TILE) // (2 * kv_heads)
-    middle = kv_heads * live
+    live = halves[1].shape[0] // kv_heads
     far = live // 2
     tail = late - width - split * far
     main = early - tail
@@ -238,14 +248,13 @@
         first = heads * CAP + which * TILE
         rows = recv_ref[:, first : first + TILE, :].reshape(size, HD)
         unique.append(jnp.dot(choose, rows, preferred_element_type=jnp.float32).reshape(kv_heads, width, HD))
-    choices = [picked(halves[n][middle : middle + TILE, :], me_ref[0], branches) for n in range(split)]
+    choices = [picked(halves[2 * n][kv_heads * live :, :], me_ref[0], branches) for n in range(split)]
     straight = has_short_way(me_ref[0], branches // 2)
     choices = [(pick, jnp.where(straight, 0, length)) for pick, length in choices]
 
     def fill(g):
         for which, target in ((0, late_key_ref), (1, late_value_ref)):
-            at = which * (middle + TILE) + g * live
-            rows = [rows_picked(halves[n][at : at + live, :], choices[n][0]) for n in range(split)]
+            rows = [rows_picked(halves[2 * n + which][g * live : (g + 1) * live, :], choices[n][0]) for n in range(split)]
             if tail:
                 rows = [early_of[g][which][main:early, :].astype(jnp.float32)] + rows
             target[g] = jnp.concatenate(rows + [unique[which][g]], axis=0).astype(jnp.bfloat16)
@@ -439,7 +448,7 @@
             pltpu.VMEM((kv_heads - near, early, HD), jnp.bfloat16),
             pltpu.VMEM((2 * kv_heads, room, HD), jnp.float32),
             *[pltpu.VMEM(x.shape, jnp.bfloat16) for x in arrays[2:]],
-            pltpu.SemaphoreType.DMA((len(arrays) - 2 + 2 * kv_heads + 2,)),
+            pltpu.SemaphoreType.DMA((len(arrays) - 2 + 2 * kv_heads + 4,)),
         ],
         compiler_params=grant(40 if branches > 16 else 20),
         cost_estimate=pl.CostEstimate(flops=0, bytes_accessed=8 * prompt_k.size, transcendentals=0),
@@ -447,11 +456,13 @@
     )(me, prompt_mask, *arrays)
     halves, keys, values = lax.optimization_barrier((halves, keys, values))
     halves = halves + [across(x) for x in halves]
+    cut = kv_heads * live + TILE
+    halves = [part for x in halves for part in (x[:cut], x[cut:])]
     late = tail + split * result_rows + width
     outputs = pl.pallas_call(
         functools.partial(attend_kernel, split),
         out_shape=bf16(branches, CAP * heads, HD),
-        in_specs=[SMEM] + [VMEM] * (4 + split) + [ANY] * 2,
+        in_specs=[SMEM] + [VMEM] * (4 + 2 * split) + [ANY] * 2,
         out_specs=VMEM,
         scratch_shapes=[
             pltpu.VMEM((kv_heads, late, HD), jnp.bfloat16),

time: 73.1 us -> 71.3 us (0.975)
  Pallas kernels: 21.4 us -> 19.4 us
    pallas_call x1, Pallas kernels: 6.6 us -> 5.54 us  [body(): pl.pallas_call(functools.partial(attend_kernel, split), out_shape=bf16(br...]
    pallas_call x1, Pallas kernels: 8.74 us -> 7.87 us  [body(): pl.pallas_call(functools.partial(gather_kernel, whole, branches, len(shor...]
  transfers between devices with their start and end apart: 18 -> 18, of which waited for: 6 -> 6; matrix products, arithmetic and copies ran while one was open for 0% -> 0% of each run, Pallas kernels for 16% -> 15%
where the time goes in v6:
time: 71.3 us; the launch traced here: 71 us
  Pallas kernels  19.4 us (27%)
  blocking collectives  19 us (27%)
  starting transfers between devices  18.9 us (27%)
  waiting for transfers between devices  12.4 us (17%)
  local copies, waits for them, and re-layouts  0.82 us (1%)
    all_to_all x1, blocking collectives, body(): lax.all_to_all(outputs, 'branch', split_axis=0, concat_axis=0, tiled=True)  19 us
    ppermute x8, starting transfers between devices, hop(): return lax.ppermute(x, 'branch', pairs)  11.5 us
    ppermute x8, waiting for transfers between devices, hop(): return lax.ppermute(x, 'branch', pairs)  10.9 us
    pallas_call x1, Pallas kernels, body(): pl.pallas_call(functools.partial(gather_kernel, whole, branches, len(shor...  7.87 us
    pallas_call x1, Pallas kernels, body(): pl.pallas_call(functools.partial(attend_kernel, split), out_shape=bf16(br...  5.54 us
    all_to_all x1, starting transfers between devices, body(): lax.all_to_all(send, 'branch', split_axis=0, concat_axis=0, tiled=True)  4.93 us
    pallas_call x1, Pallas kernels, body(): pl.pallas_call(prep_kernel, out_shape=bf16(branches, slot_rows, HD), in_s...  2.79 us
    ppermute x9, starting transfers between devices, across(): return lax.ppermute(x, 'branch', [(i, i ^ 1) for i in range(branches)])  2.5 us
  transfers between devices with their start and end apart: 18, of which 6 were waited for; matrix products, arithmetic and copies ran while one was open for 0% of the time, Pallas kernels for 15%

profile of v6, /device:TPU:0, one launch (start us, length us, event | category | flops | bytes accessed | tf_op | source)
XLA Modules:
  0.0 71.0 jit_solution(3569584389576179625)
XLA Ops:
  0.0 1.7 %payload.1.after_hbm.refs_0_ = bf16[784,128]{1,0:T(8,128)(2,1)} custom-call(s32[1,16]{1,0:T(1,128)} %pick_hbm.1, s32[1,2]{1,0:T(1,128)} %bitcast.5, bf16[2,24,2048]{2,1,0:T(8,128)(2,1)} %shared_hbm.1), custom_call_target="tpu_custom_call" | custom-call | tf_op jit(solution)/shard_map/payload/pallas_call | solution.py:358
  1.7 0.0 copy-start.2
  1.7 3.1 %collective-permute-start = (bf16[784,128]{1,0:T(8,128)(2,1)}, bf16[784,128]{1,0:T(8,128)(2,1)S(1)}, u32[]{:S(2)}, u32[]{:S(2)}) collective-permute-start(bf16[784,128]{1,0:T(8,128)(2,1)} %payload.1.after_hbm.refs_0_), channel_id=1, source_target_pairs={{0,4},{1,5},{4,8},{5,9},{8,12},{9,13},{12,14},{13,15},{14,10},{15,... | collective-permute-start | bytes 602120 | tf_op jit(solution)/shard_map/ppermute | solution.py:377
  4.8 0.0 collective-permute-start.3
  4.8 2.8 %prep.1 = bf16[16,160,128]{2,1,0:T(8,128)(2,1)} custom-call(s32[16]{0:T(128)} %bitcast.3, bf16[16,8192]{1,0:T(8,128)(2,1)} %q_hbm.1, bf16[16,2048]{1,0:T(8,128)(2,1)} %kv_hbm.1, bf16[784,128]{1,0:T(8,128)(2,1)} %payload.1.after_hbm.refs_0_), custom_call_target="tpu_custom_call" | custom-call | bytes 1024 | tf_op jit(solution)/shard_map/prep/pallas_call | solution.py:385
  7.6 2.3 %collective-permute-done.refs_1_ = bf16[784,128]{1,0:T(8,128)(2,1)S(1)} collective-permute-done((bf16[784,128]{1,0:T(8,128)(2,1)}, bf16[784,128]{1,0:T(8,128)(2,1)S(1)}, u32[]{:S(2)}, u32[]{:S(2)}) %collective-permute-start) | collective-permute-done | bytes 200736 | tf_op jit(solution)/shard_map/ppermute | solution.py:377
  10.0 1.8 %collective-permute-start.1 = (bf16[784,128]{1,0:T(8,128)(2,1)S(1)}, bf16[784,128]{1,0:T(8,128)(2,1)S(1)}, u32[]{:S(2)}, u32[]{:S(2)}) collective-permute-start(bf16[784,128]{1,0:T(8,128)(2,1)S(1)} %collective-permute-done.refs_1_), channel_id=1, source_target_pairs={{0,4},{1,5},{4,8},{5,9},{8,12},{9,13},{12,14},{13,15},{14,10},{15,... | collective-permute-start | bytes 602120 | tf_op jit(solution)/shard_map/ppermute | solution.py:377
  11.7 0.0 collective-permute-done.3.refs_2_
  11.7 0.2 collective-permute-start.4
  12.0 0.7 collective-permute-start.6
  12.7 3.4 %collective-permute-done.1.refs_3_ = bf16[784,128]{1,0:T(8,128)(2,1)S(1)} collective-permute-done((bf16[784,128]{1,0:T(8,128)(2,1)S(1)}, bf16[784,128]{1,0:T(8,128)(2,1)S(1)}, u32[]{:S(2)}, u32[]{:S(2)}) %collective-permute-start.1) | collective-permute-done | bytes 200736 | tf_op jit(solution)/shard_map/ppermute | solution.py:377
  16.1 1.5 %collective-permute-start.2 = (bf16[784,128]{1,0:T(8,128)(2,1)S(1)}, bf16[784,128]{1,0:T(8,128)(2,1)S(1)}, u32[]{:S(2)}, u32[]{:S(2)}) collective-permute-start(bf16[784,128]{1,0:T(8,128)(2,1)S(1)} %collective-permute-done.1.refs_3_), channel_id=1, source_target_pairs={{0,4},{1,5},{4,8},{5,9},{8,12},{9,13},{12,14},{13,15},{14,10},{15,... | collective-permute-start | bytes 602120 | tf_op jit(solution)/shard_map/ppermute | solution.py:377
  17.6 0.0 collective-permute-done.4.refs_4_
  17.6 0.6 collective-permute-start.5
  18.2 0.0 collective-permute-done.6.refs_14_
  18.2 3.7 %collective-permute-done.2.refs_5_ = bf16[784,128]{1,0:T(8,128)(2,1)S(1)} collective-permute-done((bf16[784,128]{1,0:T(8,128)(2,1)S(1)}, bf16[784,128]{1,0:T(8,128)(2,1)S(1)}, u32[]{:S(2)}, u32[]{:S(2)}) %collective-permute-start.2) | collective-permute-done | bytes 200736 | tf_op jit(solution)/shard_map/ppermute | solution.py:377
  21.8 1.5 %collective-permute-done.5.refs_6_ = bf16[784,128]{1,0:T(8,128)(2,1)S(1)} collective-permute-done((bf16[784,128]{1,0:T(8,128)(2,1)S(1)}, bf16[784,128]{1,0:T(8,128)(2,1)S(1)}, u32[]{:S(2)}, u32[]{:S(2)}) %collective-permute-start.5) | collective-permute-done | bytes 200736 | tf_op jit(solution)/shard_map/ppermute | solution.py:377
  23.3 4.9 %all-to-all-start = ((bf16[16,160,128]{2,1,0:T(8,128)(2,1)}), bf16[16,160,128]{2,1,0:T(8,128)(2,1)S(1)}, u32[]{:S(2)}, u32[]{:S(2)}) async-start(bf16[16,160,128]{2,1,0:T(8,128)(2,1)} %prep.1), calls=%async_computation | async-start | bytes 1310720 | tf_op jit(solution)/shard_map/all_to_all | solution.py:417
  28.3 0.5 collective-permute-start.8
  28.7 0.1 collective-permute-start.10
  28.8 0.4 collective-permute-start.9
  29.2 0.1 collective-permute-start.11
  29.4 0.4 collective-permute-start.12
  29.8 0.1 collective-permute-done.8.refs_7_
  29.8 0.4 collective-permute-start.15
  30.2 0.0 collective-permute-done.10.refs_9_
  30.2 0.3 collective-permute-start.13
  30.5 0.0 collective-permute-done.9.refs_8_
  30.5 0.3 collective-permute-start.14
  30.8 0.0 collective-permute-done.11.refs_10_
  30.8 0.0 copy-start.13
  30.8 3.7 %collective-permute-start.7 = (bf16[784,128]{1,0:T(8,128)(2,1)S(1)}, bf16[784,128]{1,0:T(8,128)(2,1)S(1)}, u32[]{:S(2)}, u32[]{:S(2)}) collective-permute-start(bf16[784,128]{1,0:T(8,128)(2,1)S(1)} %broadcast_select_fusion.1), channel_id=1, source_target_pairs={{2,0},{3,1},{0,2},{1,3},{12,14},{13,15},{14,12},{15,13},{18,16},{1... | collective-permute-start | bytes 602120 | tf_op jit(solution)/shard_map/ppermute | solution.py:377
  34.5 0.0 collective-permute-done.12.refs_11_
  34.5 0.0 collective-permute-done.15.refs_15_
  34.5 0.0 collective-permute-done.13.refs_12_
  34.5 0.0 collective-permute-done.14.refs_13_
  34.7 0.5 copy-done.14
  35.2 0.1 copy-done.15
  35.2 0.1 copy-done.16
  35.3 0.1 copy-done.17
  35.4 7.9 %gather.1 = (bf16[3,1312,128]{2,1,0:T(8,128)(2,1)S(1)}, bf16[3,1312,128]{2,1,0:T(8,128)(2,1)S(1)}, f32[1,1312]{1,0:T(1,128)S(1)}, bf16[5,1312,128]{2,1,0:T(8,128)(2,1)}, bf16[5,1312,128]{2,1,0:T(8,128)(2,1)}) custom-call(s32[1]{0:T(128)} %bitcast.1.me_ref, s32[1,8]{1,0:T(1,128)S(1)} %copy-done.1, bf16[1,1024,1024]{2,1,0:T(8,128)(2,1)} %pk_hbm.1, ...), custom_call_target="tpu_custom_call" | custom-call | bytes 8388608 | tf_op jit(solution)/shard_map/gather/pallas_call | solution.py:435
  43.3 0.0 collective-permute-done.7
  43.3 0.1 collective-permute-start.16
  43.4 1.4 %collective-permute-done.16 = bf16[784,128]{1,0:T(8,128)(2,1)S(1)} collective-permute-done((bf16[784,128]{1,0:T(8,128)(2,1)S(1)}, bf16[784,128]{1,0:T(8,128)(2,1)S(1)}, u32[]{:S(2)}, u32[]{:S(2)}) %collective-permute-start.16) | collective-permute-done | bytes 200736 | tf_op jit(solution)/shard_map/ppermute | solution.py:383
  44.8 0.0 all-to-all-done.recv_ref
  44.9 5.5 %attend.1 = bf16[16,128,128]{2,1,0:T(8,128)(2,1)S(1)} custom-call(s32[1]{0:T(128)} %bitcast.1.me_ref, bf16[3,1312,128]{2,1,0:T(8,128)(2,1)S(1)} %get-tuple-element.26.near_key, bf16[3,1312,128]{2,1,0:T(8,128)(2,1)S(1)} %get-tuple-element.27.near_value, f32[1,1312]{1,0:T(1,128)S(1)} %get-tuple-element.28.bias_ref, ...), custom_call_target="tpu_custom_call" | custom-call | flops 1409286144 | bytes 4194304 | tf_op jit(solution)/shard_map/attend/pallas_call | solution.py:462
  50.4 19.0 %all_to_all.10.back_ref = bf16[16,128,128]{2,1,0:T(8,128)(2,1)S(1)} all-to-all(bf16[16,128,128]{2,1,0:T(8,128)(2,1)S(1)} %attend.1), channel_id=1, replica_groups=mesh['groups'=2,'branch'=16] {'branch'}, dimensions={0} | all-to-all | bytes 1048576 | tf_op jit(solution)/shard_map/all_to_all | solution.py:484
  69.5 1.5 %post.1 = bf16[16,8192]{1,0:T(8,128)(2,1)} custom-call(s32[16]{0:T(128)S(1)} %bitcast.4, bf16[16,128,128]{2,1,0:T(8,128)(2,1)S(1)} %all_to_all.10.back_ref), custom_call_target="tpu_custom_call" | custom-call | tf_op jit(solution)/shard_map/post/pallas_call | solution.py:485
  (36 shorter events, 0.2 us)
Async XLA Ops:
  0.0 35.4 %copy-start.1 = (s32[1,8]{1,0:T(1,128)S(1)}, s32[1,8]{1,0:T(1,128)}, u32[]{:S(2)}) copy-start(s32[1,8]{1,0:T(1,128)} %mask_ref.1) | copy-start | bytes 100
  1.7 26.5 %copy-start.2 = (bf16[784,128]{1,0:T(8,128)(2,1)S(1)}, bf16[784,128]{1,0:T(8,128)(2,1)}, u32[]{:S(2)}) copy-start(bf16[784,128]{1,0:T(8,128)(2,1)} %payload.1.after_hbm.refs_0_) | copy-start | bytes 602116
  1.7 8.2 %collective-permute-start = (bf16[784,128]{1,0:T(8,128)(2,1)}, bf16[784,128]{1,0:T(8,128)(2,1)S(1)}, u32[]{:S(2)}, u32[]{:S(2)}) collective-permute-start(bf16[784,128]{1,0:T(8,128)(2,1)} %payload.1.after_hbm.refs_0_), channel_id=1, source_target_pairs={{0,4},{1,5},{4,8},{5,9},{8,12},{9,13},{12,14},{13,15},{14,10},{15,... | collective-permute-start | bytes 602120 | tf_op jit(solution)/shard_map/ppermute | solution.py:377
  4.8 6.9 %collective-permute-start.3 = (bf16[784,128]{1,0:T(8,128)(2,1)}, bf16[784,128]{1,0:T(8,128)(2,1)S(1)}, u32[]{:S(2)}, u32[]{:S(2)}) collective-permute-start(bf16[784,128]{1,0:T(8,128)(2,1)} %payload.1.after_hbm.refs_0_), channel_id=1, source_target_pairs={{0,2},{1,3},{4,0},{5,1},{8,4},{9,5},{12,8},{13,9},{14,12},{15,13},... | collective-permute-start | bytes 602120 | tf_op jit(solution)/shard_map/ppermute | solution.py:377
  9.9 24.7 %copy-start.3 = (bf16[784,128]{1,0:T(8,128)(2,1)}, bf16[784,128]{1,0:T(8,128)(2,1)S(1)}, u32[]{:S(2)}) copy-start(bf16[784,128]{1,0:T(8,128)(2,1)S(1)} %collective-permute-done.refs_1_) | copy-start | bytes 602116
  10.0 6.2 %collective-permute-start.1 = (bf16[784,128]{1,0:T(8,128)(2,1)S(1)}, bf16[784,128]{1,0:T(8,128)(2,1)S(1)}, u32[]{:S(2)}, u32[]{:S(2)}) collective-permute-start(bf16[784,128]{1,0:T(8,128)(2,1)S(1)} %collective-permute-done.refs_1_), channel_id=1, source_target_pairs={{0,4},{1,5},{4,8},{5,9},{8,12},{9,13},{12,14},{13,15},{14,10},{15,... | collective-permute-start | bytes 602120 | tf_op jit(solution)/shard_map/ppermute | solution.py:377
  11.7 22.9 %copy-start.4 = (bf16[784,128]{1,0:T(8,128)(2,1)}, bf16[784,128]{1,0:T(8,128)(2,1)S(1)}, u32[]{:S(2)}) copy-start(bf16[784,128]{1,0:T(8,128)(2,1)S(1)} %collective-permute-done.3.refs_2_) | copy-start | bytes 602116
  11.7 5.9 %collective-permute-start.4 = (bf16[784,128]{1,0:T(8,128)(2,1)S(1)}, bf16[784,128]{1,0:T(8,128)(2,1)S(1)}, u32[]{:S(2)}, u32[]{:S(2)}) collective-permute-start(bf16[784,128]{1,0:T(8,128)(2,1)S(1)} %collective-permute-done.3.refs_2_), channel_id=1, source_target_pairs={{0,2},{1,3},{4,0},{5,1},{8,4},{9,5},{12,8},{13,9},{14,12},{15,13},... | collective-permute-start | bytes 602120 | tf_op jit(solution)/shard_map/ppermute | solution.py:377
  12.0 6.1 %collective-permute-start.6 = (bf16[784,128]{1,0:T(8,128)(2,1)S(1)}, bf16[784,128]{1,0:T(8,128)(2,1)S(1)}, u32[]{:S(2)}, u32[]{:S(2)}) collective-permute-start(bf16[784,128]{1,0:T(8,128)(2,1)S(1)} %broadcast_select_fusion), channel_id=1, source_target_pairs={{4,6},{5,7},{6,4},{7,5},{8,10},{9,11},{10,8},{11,9},{20,22},{21,23... | collective-permute-start | bytes 602120 | tf_op jit(solution)/shard_map/ppermute | solution.py:377
  16.1 18.4 %copy-start.7 = (bf16[784,128]{1,0:T(8,128)(2,1)}, bf16[784,128]{1,0:T(8,128)(2,1)S(1)}, u32[]{:S(2)}) copy-start(bf16[784,128]{1,0:T(8,128)(2,1)S(1)} %collective-permute-done.1.refs_3_) | copy-start | bytes 602116
  16.1 5.7 %collective-permute-start.2 = (bf16[784,128]{1,0:T(8,128)(2,1)S(1)}, bf16[784,128]{1,0:T(8,128)(2,1)S(1)}, u32[]{:S(2)}, u32[]{:S(2)}) collective-permute-start(bf16[784,128]{1,0:T(8,128)(2,1)S(1)} %collective-permute-done.1.refs_3_), channel_id=1, source_target_pairs={{0,4},{1,5},{4,8},{5,9},{8,12},{9,13},{12,14},{13,15},{14,10},{15,... | collective-permute-start | bytes 602120 | tf_op jit(solution)/shard_map/ppermute | solution.py:377
  17.6 17.0 %copy-start.8 = (bf16[784,128]{1,0:T(8,128)(2,1)}, bf16[784,128]{1,0:T(8,128)(2,1)S(1)}, u32[]{:S(2)}) copy-start(bf16[784,128]{1,0:T(8,128)(2,1)S(1)} %collective-permute-done.4.refs_4_) | copy-start | bytes 602116
  17.6 5.7 %collective-permute-start.5 = (bf16[784,128]{1,0:T(8,128)(2,1)S(1)}, bf16[784,128]{1,0:T(8,128)(2,1)S(1)}, u32[]{:S(2)}, u32[]{:S(2)}) collective-permute-start(bf16[784,128]{1,0:T(8,128)(2,1)S(1)} %collective-permute-done.4.refs_4_), channel_id=1, source_target_pairs={{0,2},{1,3},{4,0},{5,1},{8,4},{9,5},{12,8},{13,9},{14,12},{15,13},... | collective-permute-start | bytes 602120 | tf_op jit(solution)/shard_map/ppermute | solution.py:377
  18.2 16.4 %copy-start.9 = (bf16[784,128]{1,0:T(8,128)(2,1)}, bf16[784,128]{1,0:T(8,128)(2,1)S(1)}, u32[]{:S(2)}) copy-start(bf16[784,128]{1,0:T(8,128)(2,1)S(1)} %collective-permute-done.6.refs_14_) | copy-start | bytes 602116
  21.8 12.8 %copy-start.5 = (bf16[784,128]{1,0:T(8,128)(2,1)}, bf16[784,128]{1,0:T(8,128)(2,1)S(1)}, u32[]{:S(2)}) copy-start(bf16[784,128]{1,0:T(8,128)(2,1)S(1)} %collective-permute-done.2.refs_5_) | copy-start | bytes 602116
  23.3 11.3 %copy-start.6 = (bf16[784,128]{1,0:T(8,128)(2,1)}, bf16[784,128]{1,0:T(8,128)(2,1)S(1)}, u32[]{:S(2)}) copy-start(bf16[784,128]{1,0:T(8,128)(2,1)S(1)} %collective-permute-done.5.refs_6_) | copy-start | bytes 602116
  23.3 21.5 %all-to-all-start = ((bf16[16,160,128]{2,1,0:T(8,128)(2,1)}), bf16[16,160,128]{2,1,0:T(8,128)(2,1)S(1)}, u32[]{:S(2)}, u32[]{:S(2)}) async-start(bf16[16,160,128]{2,1,0:T(8,128)(2,1)} %prep.1), calls=%async_computation | async-start | bytes 1310720 | tf_op jit(solution)/shard_map/all_to_all | solution.py:417
  28.3 1.5 %collective-permute-start.8 = (bf16[784,128]{1,0:T(8,128)(2,1)S(1)}, bf16[784,128]{1,0:T(8,128)(2,1)S(1)}, u32[]{:S(2)}, u32[]{:S(2)}) collective-permute-start(bf16[784,128]{1,0:T(8,128)(2,1)S(1)} %copy-done.2), channel_id=1, source_target_pairs={{0,1},{1,0},{2,3},{3,2},{4,5},{5,4},{6,7},{7,6},{8,9},{9,8},{10,11... | collective-permute-start | bytes 602120 | tf_op jit(solution)/shard_map/ppermute | solution.py:383
  28.7 1.5 %collective-permute-start.10 = (bf16[784,128]{1,0:T(8,128)(2,1)S(1)}, bf16[784,128]{1,0:T(8,128)(2,1)S(1)}, u32[]{:S(2)}, u32[]{:S(2)}) collective-permute-start(bf16[784,128]{1,0:T(8,128)(2,1)S(1)} %collective-permute-done.3.refs_2_), channel_id=1, source_target_pairs={{0,1},{1,0},{2,3},{3,2},{4,5},{5,4},{6,7},{7,6},{8,9},{9,8},{10,11... | collective-permute-start | bytes 602120 | tf_op jit(solution)/shard_map/ppermute | solution.py:383
  28.8 1.6 %collective-permute-start.9 = (bf16[784,128]{1,0:T(8,128)(2,1)S(1)}, bf16[784,128]{1,0:T(8,128)(2,1)S(1)}, u32[]{:S(2)}, u32[]{:S(2)}) collective-permute-start(bf16[784,128]{1,0:T(8,128)(2,1)S(1)} %collective-permute-done.refs_1_), channel_id=1, source_target_pairs={{0,1},{1,0},{2,3},{3,2},{4,5},{5,4},{6,7},{7,6},{8,9},{9,8},{10,11... | collective-permute-start | bytes 602120 | tf_op jit(solution)/shard_map/ppermute | solution.py:383
  29.2 1.5 %collective-permute-start.11 = (bf16[784,128]{1,0:T(8,128)(2,1)S(1)}, bf16[784,128]{1,0:T(8,128)(2,1)S(1)}, u32[]{:S(2)}, u32[]{:S(2)}) collective-permute-start(bf16[784,128]{1,0:T(8,128)(2,1)S(1)} %collective-permute-done.1.refs_3_), channel_id=1, source_target_pairs={{0,1},{1,0},{2,3},{3,2},{4,5},{5,4},{6,7},{7,6},{8,9},{9,8},{10,11... | collective-permute-start | bytes 602120 | tf_op jit(solution)/shard_map/ppermute | solution.py:383
  29.4 5.1 %collective-permute-start.12 = (bf16[784,128]{1,0:T(8,128)(2,1)S(1)}, bf16[784,128]{1,0:T(8,128)(2,1)S(1)}, u32[]{:S(2)}, u32[]{:S(2)}) collective-permute-start(bf16[784,128]{1,0:T(8,128)(2,1)S(1)} %collective-permute-done.4.refs_4_), channel_id=1, source_target_pairs={{0,1},{1,0},{2,3},{3,2},{4,5},{5,4},{6,7},{7,6},{8,9},{9,8},{10,11... | collective-permute-start | bytes 602120 | tf_op jit(solution)/shard_map/ppermute | solution.py:383
  29.8 4.8 %copy-start.10 = (bf16[784,128]{1,0:T(8,128)(2,1)}, bf16[784,128]{1,0:T(8,128)(2,1)S(1)}, u32[]{:S(2)}) copy-start(bf16[784,128]{1,0:T(8,128)(2,1)S(1)} %collective-permute-done.8.refs_7_) | copy-start | bytes 602116
  29.8 4.7 %collective-permute-start.15 = (bf16[784,128]{1,0:T(8,128)(2,1)S(1)}, bf16[784,128]{1,0:T(8,128)(2,1)S(1)}, u32[]{:S(2)}, u32[]{:S(2)}) collective-permute-start(bf16[784,128]{1,0:T(8,128)(2,1)S(1)} %collective-permute-done.6.refs_14_), channel_id=1, source_target_pairs={{0,1},{1,0},{2,3},{3,2},{4,5},{5,4},{6,7},{7,6},{8,9},{9,8},{10,11... | collective-permute-start | bytes 602120 | tf_op jit(solution)/shard_map/ppermute | solution.py:383
  30.2 4.4 %copy-start.11 = (bf16[784,128]{1,0:T(8,128)(2,1)}, bf16[784,128]{1,0:T(8,128)(2,1)S(1)}, u32[]{:S(2)}) copy-start(bf16[784,128]{1,0:T(8,128)(2,1)S(1)} %collective-permute-done.10.refs_9_) | copy-start | bytes 602116
  30.2 4.3 %collective-permute-start.13 = (bf16[784,128]{1,0:T(8,128)(2,1)S(1)}, bf16[784,128]{1,0:T(8,128)(2,1)S(1)}, u32[]{:S(2)}, u32[]{:S(2)}) collective-permute-start(bf16[784,128]{1,0:T(8,128)(2,1)S(1)} %collective-permute-done.2.refs_5_), channel_id=1, source_target_pairs={{0,1},{1,0},{2,3},{3,2},{4,5},{5,4},{6,7},{7,6},{8,9},{9,8},{10,11... | collective-permute-start | bytes 602120 | tf_op jit(solution)/shard_map/ppermute | solution.py:383
  30.5 4.1 %copy-start.12 = (bf16[784,128]{1,0:T(8,128)(2,1)}, bf16[784,128]{1,0:T(8,128)(2,1)S(1)}, u32[]{:S(2)}) copy-start(bf16[784,128]{1,0:T(8,128)(2,1)S(1)} %collective-permute-done.9.refs_8_) | copy-start | bytes 602116
  30.5 4.1 %collective-permute-start.14 = (bf16[784,128]{1,0:T(8,128)(2,1)S(1)}, bf16[784,128]{1,0:T(8,128)(2,1)S(1)}, u32[]{:S(2)}, u32[]{:S(2)}) collective-permute-start(bf16[784,128]{1,0:T(8,128)(2,1)S(1)} %collective-permute-done.5.refs_6_), channel_id=1, source_target_pairs={{0,1},{1,0},{2,3},{3,2},{4,5},{5,4},{6,7},{7,6},{8,9},{9,8},{10,11... | collective-permute-start | bytes 602120 | tf_op jit(solution)/shard_map/ppermute | solution.py:383
  30.8 3.9 %copy-start.13 = (bf16[784,128]{1,0:T(8,128)(2,1)}, bf16[784,128]{1,0:T(8,128)(2,1)S(1)}, u32[]{:S(2)}) copy-start(bf16[784,128]{1,0:T(8,128)(2,1)S(1)} %collective-permute-done.11.refs_10_) | copy-start | bytes 602116
  30.8 12.5 %collective-permute-start.7 = (bf16[784,128]{1,0:T(8,128)(2,1)S(1)}, bf16[784,128]{1,0:T(8,128)(2,1)S(1)}, u32[]{:S(2)}, u32[]{:S(2)}) collective-permute-start(bf16[784,128]{1,0:T(8,128)(2,1)S(1)} %broadcast_select_fusion.1), channel_id=1, source_target_pairs={{2,0},{3,1},{0,2},{1,3},{12,14},{13,15},{14,12},{15,13},{18,16},{1... | collective-permute-start | bytes 602120 | tf_op jit(solution)/shard_map/ppermute | solution.py:377
  34.5 0.7 copy-start.14
  34.5 0.7 %copy-start.15 = (bf16[784,128]{1,0:T(8,128)(2,1)}, bf16[784,128]{1,0:T(8,128)(2,1)S(1)}, u32[]{:S(2)}) copy-start(bf16[784,128]{1,0:T(8,128)(2,1)S(1)} %collective-permute-done.15.refs_15_) | copy-start | bytes 602116
  34.5 0.8 %copy-start.16 = (bf16[784,128]{1,0:T(8,128)(2,1)}, bf16[784,128]{1,0:T(8,128)(2,1)S(1)}, u32[]{:S(2)}) copy-start(bf16[784,128]{1,0:T(8,128)(2,1)S(1)} %collective-permute-done.13.refs_12_) | copy-start | bytes 602116
  34.6 0.8 %copy-start.17 = (bf16[784,128]{1,0:T(8,128)(2,1)}, bf16[784,128]{1,0:T(8,128)(2,1)S(1)}, u32[]{:S(2)}) copy-start(bf16[784,128]{1,0:T(8,128)(2,1)S(1)} %collective-permute-done.14.refs_13_) | copy-start | bytes 602116
  43.3 1.5 %collective-permute-start.16 = (bf16[784,128]{1,0:T(8,128)(2,1)S(1)}, bf16[784,128]{1,0:T(8,128)(2,1)S(1)}, u32[]{:S(2)}, u32[]{:S(2)}) collective-permute-start(bf16[784,128]{1,0:T(8,128)(2,1)S(1)} %collective-permute-done.7), channel_id=1, source_target_pairs={{0,1},{1,0},{2,3},{3,2},{4,5},{5,4},{6,7},{7,6},{8,9},{9,8},{10,11... | collective-permute-start | bytes 602120 | tf_op jit(solution)/shard_map/ppermute | solution.py:383
  44.9 24.6 %copy-start = (s32[16,1]{0,1:T(1,128)S(1)}, s32[16,1]{0,1:T(1,128)}, u32[]{:S(2)}) copy-start(s32[16,1]{0,1:T(1,128)} %param.17) | copy-start | bytes 196

commit v7 on v6

--- a/solution.py
+++ b/solution.py
@@ -162,7 +162,7 @@
         wide.append(start(pk_hbm.at[0, :, lanes], key_ref.at[pl.ds(0, prompt), :]))
     column = lax.broadcasted_iota(jnp.int32, (1, room), 1)
     seen = jnp.zeros((1, room), jnp.bool_)
-    taken_ref[...] = jnp.zeros(taken_ref.shape, jnp.float32)
+    taken_ref[:, room - 2 * rows : room, :] = jnp.zeros((slabs, 2 * rows, HD), jnp.float32)
     for copy in moves:
         copy.wait()
     slot = jnp.int32(0)

time: 71.3 us -> 71.3 us (level)
  no operation moved by 1% of the time
where the time goes in v7:
time: 71.3 us; the launch traced here: 71 us
  Pallas kernels  19.5 us (27%)
  blocking collectives  19 us (27%)
  starting transfers between devices  18.9 us (27%)
  waiting for transfers between devices  12.4 us (17%)
  local copies, waits for them, and re-layouts  0.82 us (1%)
    all_to_all x1, blocking collectives, body(): lax.all_to_all(outputs, 'branch', split_axis=0, concat_axis=0, tiled=True)  19 us
    ppermute x8, starting transfers between devices, hop(): return lax.ppermute(x, 'branch', pairs)  11.5 us
    ppermute x8, waiting for transfers between devices, hop(): return lax.ppermute(x, 'branch', pairs)  10.9 us
    pallas_call x1, Pallas kernels, body(): pl.pallas_call(functools.partial(gather_kernel, whole, branches, len(shor...  7.89 us
    pallas_call x1, Pallas kernels, body(): pl.pallas_call(functools.partial(attend_kernel, split), out_shape=bf16(br...  5.54 us
    all_to_all x1, starting transfers between devices, body(): lax.all_to_all(send, 'branch', split_axis=0, concat_axis=0, tiled=True)  4.93 us
    pallas_call x1, Pallas kernels, body(): pl.pallas_call(prep_kernel, out_shape=bf16(branches, slot_rows, HD), in_s...  2.79 us
    ppermute x9, starting transfers between devices, across(): return lax.ppermute(x, 'branch', [(i, i ^ 1) for i in range(branches)])  2.5 us
  transfers between devices with their start and end apart: 18, of which 6 were waited for; matrix products, arithmetic and copies ran while one was open for 0% of the time, Pallas kernels for 15%

profile of v7, /device:TPU:0, one launch (start us, length us, event | category | flops | bytes accessed | tf_op | source)
XLA Modules:
  0.0 71.0 jit_solution(16659512727366333685)
XLA Ops:
  0.0 1.7 %payload.1.after_hbm.refs_0_ = bf16[784,128]{1,0:T(8,128)(2,1)} custom-call(s32[1,16]{1,0:T(1,128)} %pick_hbm.1, s32[1,2]{1,0:T(1,128)} %bitcast.5, bf16[2,24,2048]{2,1,0:T(8,128)(2,1)} %shared_hbm.1), custom_call_target="tpu_custom_call" | custom-call | tf_op jit(solution)/shard_map/payload/pallas_call | solution.py:358
  1.7 0.0 copy-start.2
  1.7 3.1 %collective-permute-start = (bf16[784,128]{1,0:T(8,128)(2,1)}, bf16[784,128]{1,0:T(8,128)(2,1)S(1)}, u32[]{:S(2)}, u32[]{:S(2)}) collective-permute-start(bf16[784,128]{1,0:T(8,128)(2,1)} %payload.1.after_hbm.refs_0_), channel_id=1, source_target_pairs={{0,4},{1,5},{4,8},{5,9},{8,12},{9,13},{12,14},{13,15},{14,10},{15,... | collective-permute-start | bytes 602120 | tf_op jit(solution)/shard_map/ppermute | solution.py:377
  4.8 0.0 collective-permute-start.3
  4.8 2.8 %prep.1 = bf16[16,160,128]{2,1,0:T(8,128)(2,1)} custom-call(s32[16]{0:T(128)} %bitcast.3, bf16[16,8192]{1,0:T(8,128)(2,1)} %q_hbm.1, bf16[16,2048]{1,0:T(8,128)(2,1)} %kv_hbm.1, bf16[784,128]{1,0:T(8,128)(2,1)} %payload.1.after_hbm.refs_0_), custom_call_target="tpu_custom_call" | custom-call | bytes 1024 | tf_op jit(solution)/shard_map/prep/pallas_call | solution.py:385
  7.6 2.3 %collective-permute-done.refs_1_ = bf16[784,128]{1,0:T(8,128)(2,1)S(1)} collective-permute-done((bf16[784,128]{1,0:T(8,128)(2,1)}, bf16[784,128]{1,0:T(8,128)(2,1)S(1)}, u32[]{:S(2)}, u32[]{:S(2)}) %collective-permute-start) | collective-permute-done | bytes 200736 | tf_op jit(solution)/shard_map/ppermute | solution.py:377
  10.0 1.8 %collective-permute-start.1 = (bf16[784,128]{1,0:T(8,128)(2,1)S(1)}, bf16[784,128]{1,0:T(8,128)(2,1)S(1)}, u32[]{:S(2)}, u32[]{:S(2)}) collective-permute-start(bf16[784,128]{1,0:T(8,128)(2,1)S(1)} %collective-permute-done.refs_1_), channel_id=1, source_target_pairs={{0,4},{1,5},{4,8},{5,9},{8,12},{9,13},{12,14},{13,15},{14,10},{15,... | collective-permute-start | bytes 602120 | tf_op jit(solution)/shard_map/ppermute | solution.py:377
  11.7 0.0 collective-permute-done.3.refs_2_
  11.7 0.2 collective-permute-start.4
  12.0 0.7 collective-permute-start.6
  12.7 3.4 %collective-permute-done.1.refs_3_ = bf16[784,128]{1,0:T(8,128)(2,1)S(1)} collective-permute-done((bf16[784,128]{1,0:T(8,128)(2,1)S(1)}, bf16[784,128]{1,0:T(8,128)(2,1)S(1)}, u32[]{:S(2)}, u32[]{:S(2)}) %collective-permute-start.1) | collective-permute-done | bytes 200736 | tf_op jit(solution)/shard_map/ppermute | solution.py:377
  16.1 1.5 %collective-permute-start.2 = (bf16[784,128]{1,0:T(8,128)(2,1)S(1)}, bf16[784,128]{1,0:T(8,128)(2,1)S(1)}, u32[]{:S(2)}, u32[]{:S(2)}) collective-permute-start(bf16[784,128]{1,0:T(8,128)(2,1)S(1)} %collective-permute-done.1.refs_3_), channel_id=1, source_target_pairs={{0,4},{1,5},{4,8},{5,9},{8,12},{9,13},{12,14},{13,15},{14,10},{15,... | collective-permute-start | bytes 602120 | tf_op jit(solution)/shard_map/ppermute | solution.py:377
  17.6 0.0 collective-permute-done.4.refs_4_
  17.6 0.6 collective-permute-start.5
  18.2 0.0 collective-permute-done.6.refs_14_
  18.2 3.7 %collective-permute-done.2.refs_5_ = bf16[784,128]{1,0:T(8,128)(2,1)S(1)} collective-permute-done((bf16[784,128]{1,0:T(8,128)(2,1)S(1)}, bf16[784,128]{1,0:T(8,128)(2,1)S(1)}, u32[]{:S(2)}, u32[]{:S(2)}) %collective-permute-start.2) | collective-permute-done | bytes 200736 | tf_op jit(solution)/shard_map/ppermute | solution.py:377
  21.8 1.5 %collective-permute-done.5.refs_6_ = bf16[784,128]{1,0:T(8,128)(2,1)S(1)} collective-permute-done((bf16[784,128]{1,0:T(8,128)(2,1)S(1)}, bf16[784,128]{1,0:T(8,128)(2,1)S(1)}, u32[]{:S(2)}, u32[]{:S(2)}) %collective-permute-start.5) | collective-permute-done | bytes 200736 | tf_op jit(solution)/shard_map/ppermute | solution.py:377
  23.3 4.9 %all-to-all-start = ((bf16[16,160,128]{2,1,0:T(8,128)(2,1)}), bf16[16,160,128]{2,1,0:T(8,128)(2,1)S(1)}, u32[]{:S(2)}, u32[]{:S(2)}) async-start(bf16[16,160,128]{2,1,0:T(8,128)(2,1)} %prep.1), calls=%async_computation | async-start | bytes 1310720 | tf_op jit(solution)/shard_map/all_to_all | solution.py:417
  28.3 0.5 collective-permute-start.8
  28.7 0.1 collective-permute-start.10
  28.8 0.4 collective-permute-start.9
  29.2 0.1 collective-permute-start.11
  29.4 0.4 collective-permute-start.12
  29.8 0.1 collective-permute-done.8.refs_7_
  29.8 0.4 collective-permute-start.15
  30.2 0.0 collective-permute-done.10.refs_9_
  30.2 0.3 collective-permute-start.13
  30.5 0.0 collective-permute-done.9.refs_8_
  30.5 0.3 collective-permute-start.14
  30.8 0.0 collective-permute-done.11.refs_10_
  30.8 3.7 %collective-permute-start.7 = (bf16[784,128]{1,0:T(8,128)(2,1)S(1)}, bf16[784,128]{1,0:T(8,128)(2,1)S(1)}, u32[]{:S(2)}, u32[]{:S(2)}) collective-permute-start(bf16[784,128]{1,0:T(8,128)(2,1)S(1)} %broadcast_select_fusion.1), channel_id=1, source_target_pairs={{2,0},{3,1},{0,2},{1,3},{12,14},{13,15},{14,12},{15,13},{18,16},{1... | collective-permute-start | bytes 602120 | tf_op jit(solution)/shard_map/ppermute | solution.py:377
  34.5 0.0 collective-permute-done.12.refs_11_
  34.5 0.0 collective-permute-done.15.refs_15_
  34.5 0.0 collective-permute-done.13.refs_12_
  34.5 0.0 collective-permute-done.14.refs_13_
  34.7 0.5 copy-done.14
  35.2 0.1 copy-done.15
  35.2 0.1 copy-done.16
  35.3 0.1 copy-done.17
  35.4 7.9 %gather.1 = (bf16[3,1312,128]{2,1,0:T(8,128)(2,1)S(1)}, bf16[3,1312,128]{2,1,0:T(8,128)(2,1)S(1)}, f32[1,1312]{1,0:T(1,128)S(1)}, bf16[5,1312,128]{2,1,0:T(8,128)(2,1)}, bf16[5,1312,128]{2,1,0:T(8,128)(2,1)}) custom-call(s32[1]{0:T(128)} %bitcast.1.me_ref, s32[1,8]{1,0:T(1,128)S(1)} %copy-done.1, bf16[1,1024,1024]{2,1,0:T(8,128)(2,1)} %pk_hbm.1, ...), custom_call_target="tpu_custom_call" | custom-call | bytes 8388608 | tf_op jit(solution)/shard_map/gather/pallas_call | solution.py:435
  43.3 0.0 collective-permute-done.7
  43.3 0.1 collective-permute-start.16
  43.4 1.4 %collective-permute-done.16 = bf16[784,128]{1,0:T(8,128)(2,1)S(1)} collective-permute-done((bf16[784,128]{1,0:T(8,128)(2,1)S(1)}, bf16[784,128]{1,0:T(8,128)(2,1)S(1)}, u32[]{:S(2)}, u32[]{:S(2)}) %collective-permute-start.16) | collective-permute-done | bytes 200736 | tf_op jit(solution)/shard_map/ppermute | solution.py:383
  44.8 0.0 all-to-all-done.recv_ref
  44.9 0.0 copy-start
  44.9 5.5 %attend.1 = bf16[16,128,128]{2,1,0:T(8,128)(2,1)S(1)} custom-call(s32[1]{0:T(128)} %bitcast.1.me_ref, bf16[3,1312,128]{2,1,0:T(8,128)(2,1)S(1)} %get-tuple-element.26.near_key, bf16[3,1312,128]{2,1,0:T(8,128)(2,1)S(1)} %get-tuple-element.27.near_value, f32[1,1312]{1,0:T(1,128)S(1)} %get-tuple-element.28.bias_ref, ...), custom_call_target="tpu_custom_call" | custom-call | flops 1409286144 | bytes 4194304 | tf_op jit(solution)/shard_map/attend/pallas_call | solution.py:462
  50.4 19.0 %all_to_all.10.back_ref = bf16[16,128,128]{2,1,0:T(8,128)(2,1)S(1)} all-to-all(bf16[16,128,128]{2,1,0:T(8,128)(2,1)S(1)} %attend.1), channel_id=1, replica_groups=mesh['groups'=2,'branch'=16] {'branch'}, dimensions={0} | all-to-all | bytes 1048576 | tf_op jit(solution)/shard_map/all_to_all | solution.py:484
  69.5 1.5 %post.1 = bf16[16,8192]{1,0:T(8,128)(2,1)} custom-call(s32[16]{0:T(128)S(1)} %bitcast.4, bf16[16,128,128]{2,1,0:T(8,128)(2,1)S(1)} %all_to_all.10.back_ref), custom_call_target="tpu_custom_call" | custom-call | tf_op jit(solution)/shard_map/post/pallas_call | solution.py:485
  (36 shorter events, 0.2 us)
Async XLA Ops:
  0.0 35.4 %copy-start.1 = (s32[1,8]{1,0:T(1,128)S(1)}, s32[1,8]{1,0:T(1,128)}, u32[]{:S(2)}) copy-start(s32[1,8]{1,0:T(1,128)} %mask_ref.1) | copy-start | bytes 100
  1.7 26.5 %copy-start.2 = (bf16[784,128]{1,0:T(8,128)(2,1)S(1)}, bf16[784,128]{1,0:T(8,128)(2,1)}, u32[]{:S(2)}) copy-start(bf16[784,128]{1,0:T(8,128)(2,1)} %payload.1.after_hbm.refs_0_) | copy-start | bytes 602116
  1.7 8.2 %collective-permute-start = (bf16[784,128]{1,0:T(8,128)(2,1)}, bf16[784,128]{1,0:T(8,128)(2,1)S(1)}, u32[]{:S(2)}, u32[]{:S(2)}) collective-permute-start(bf16[784,128]{1,0:T(8,128)(2,1)} %payload.1.after_hbm.refs_0_), channel_id=1, source_target_pairs={{0,4},{1,5},{4,8},{5,9},{8,12},{9,13},{12,14},{13,15},{14,10},{15,... | collective-permute-start | bytes 602120 | tf_op jit(solution)/shard_map/ppermute | solution.py:377
  4.8 6.9 %collective-permute-start.3 = (bf16[784,128]{1,0:T(8,128)(2,1)}, bf16[784,128]{1,0:T(8,128)(2,1)S(1)}, u32[]{:S(2)}, u32[]{:S(2)}) collective-permute-start(bf16[784,128]{1,0:T(8,128)(2,1)} %payload.1.after_hbm.refs_0_), channel_id=1, source_target_pairs={{0,2},{1,3},{4,0},{5,1},{8,4},{9,5},{12,8},{13,9},{14,12},{15,13},... | collective-permute-start | bytes 602120 | tf_op jit(solution)/shard_map/ppermute | solution.py:377
  9.9 24.7 %copy-start.3 = (bf16[784,128]{1,0:T(8,128)(2,1)}, bf16[784,128]{1,0:T(8,128)(2,1)S(1)}, u32[]{:S(2)}) copy-start(bf16[784,128]{1,0:T(8,128)(2,1)S(1)} %collective-permute-done.refs_1_) | copy-start | bytes 602116
  10.0 6.2 %collective-permute-start.1 = (bf16[784,128]{1,0:T(8,128)(2,1)S(1)}, bf16[784,128]{1,0:T(8,128)(2,1)S(1)}, u32[]{:S(2)}, u32[]{:S(2)}) collective-permute-start(bf16[784,128]{1,0:T(8,128)(2,1)S(1)} %collective-permute-done.refs_1_), channel_id=1, source_target_pairs={{0,4},{1,5},{4,8},{5,9},{8,12},{9,13},{12,14},{13,15},{14,10},{15,... | collective-permute-start | bytes 602120 | tf_op jit(solution)/shard_map/ppermute | solution.py:377
  11.7 22.9 %copy-start.4 = (bf16[784,128]{1,0:T(8,128)(2,1)}, bf16[784,128]{1,0:T(8,128)(2,1)S(1)}, u32[]{:S(2)}) copy-start(bf16[784,128]{1,0:T(8,128)(2,1)S(1)} %collective-permute-done.3.refs_2_) | copy-start | bytes 602116
  11.7 5.9 %collective-permute-start.4 = (bf16[784,128]{1,0:T(8,128)(2,1)S(1)}, bf16[784,128]{1,0:T(8,128)(2,1)S(1)}, u32[]{:S(2)}, u32[]{:S(2)}) collective-permute-start(bf16[784,128]{1,0:T(8,128)(2,1)S(1)} %collective-permute-done.3.refs_2_), channel_id=1, source_target_pairs={{0,2},{1,3},{4,0},{5,1},{8,4},{9,5},{12,8},{13,9},{14,12},{15,13},... | collective-permute-start | bytes 602120 | tf_op jit(solution)/shard_map/ppermute | solution.py:377
  12.0 6.1 %collective-permute-start.6 = (bf16[784,128]{1,0:T(8,128)(2,1)S(1)}, bf16[784,128]{1,0:T(8,128)(2,1)S(1)}, u32[]{:S(2)}, u32[]{:S(2)}) collective-permute-start(bf16[784,128]{1,0:T(8,128)(2,1)S(1)} %broadcast_select_fusion), channel_id=1, source_target_pairs={{4,6},{5,7},{6,4},{7,5},{8,10},{9,11},{10,8},{11,9},{20,22},{21,23... | collective-permute-start | bytes 602120 | tf_op jit(solution)/shard_map/ppermute | solution.py:377
  16.1 18.4 %copy-start.7 = (bf16[784,128]{1,0:T(8,128)(2,1)}, bf16[784,128]{1,0:T(8,128)(2,1)S(1)}, u32[]{:S(2)}) copy-start(bf16[784,128]{1,0:T(8,128)(2,1)S(1)} %collective-permute-done.1.refs_3_) | copy-start | bytes 602116
  16.1 5.7 %collective-permute-start.2 = (bf16[784,128]{1,0:T(8,128)(2,1)S(1)}, bf16[784,128]{1,0:T(8,128)(2,1)S(1)}, u32[]{:S(2)}, u32[]{:S(2)}) collective-permute-start(bf16[784,128]{1,0:T(8,128)(2,1)S(1)} %collective-permute-done.1.refs_3_), channel_id=1, source_target_pairs={{0,4},{1,5},{4,8},{5,9},{8,12},{9,13},{12,14},{13,15},{14,10},{15,... | collective-permute-start | bytes 602120 | tf_op jit(solution)/shard_map/ppermute | solution.py:377
  17.6 17.0 %copy-start.8 = (bf16[784,128]{1,0:T(8,128)(2,1)}, bf16[784,128]{1,0:T(8,128)(2,1)S(1)}, u32[]{:S(2)}) copy-start(bf16[784,128]{1,0:T(8,128)(2,1)S(1)} %collective-permute-done.4.refs_4_) | copy-start | bytes 602116
  17.6 5.7 %collective-permute-start.5 = (bf16[784,128]{1,0:T(8,128)(2,1)S(1)}, bf16[784,128]{1,0:T(8,128)(2,1)S(1)}, u32[]{:S(2)}, u32[]{:S(2)}) collective-permute-start(bf16[784,128]{1,0:T(8,128)(2,1)S(1)} %collective-permute-done.4.refs_4_), channel_id=1, source_target_pairs={{0,2},{1,3},{4,0},{5,1},{8,4},{9,5},{12,8},{13,9},{14,12},{15,13},... | collective-permute-start | bytes 602120 | tf_op jit(solution)/shard_map/ppermute | solution.py:377
  18.2 16.4 %copy-start.9 = (bf16[784,128]{1,0:T(8,128)(2,1)}, bf16[784,128]{1,0:T(8,128)(2,1)S(1)}, u32[]{:S(2)}) copy-start(bf16[784,128]{1,0:T(8,128)(2,1)S(1)} %collective-permute-done.6.refs_14_) | copy-start | bytes 602116
  21.8 12.8 %copy-start.5 = (bf16[784,128]{1,0:T(8,128)(2,1)}, bf16[784,128]{1,0:T(8,128)(2,1)S(1)}, u32[]{:S(2)}) copy-start(bf16[784,128]{1,0:T(8,128)(2,1)S(1)} %collective-permute-done.2.refs_5_) | copy-start | bytes 602116
  23.3 11.3 %copy-start.6 = (bf16[784,128]{1,0:T(8,128)(2,1)}, bf16[784,128]{1,0:T(8,128)(2,1)S(1)}, u32[]{:S(2)}) copy-start(bf16[784,128]{1,0:T(8,128)(2,1)S(1)} %collective-permute-done.5.refs_6_) | copy-start | bytes 602116
  23.3 21.5 %all-to-all-start = ((bf16[16,160,128]{2,1,0:T(8,128)(2,1)}), bf16[16,160,128]{2,1,0:T(8,128)(2,1)S(1)}, u32[]{:S(2)}, u32[]{:S(2)}) async-start(bf16[16,160,128]{2,1,0:T(8,128)(2,1)} %prep.1), calls=%async_computation | async-start | bytes 1310720 | tf_op jit(solution)/shard_map/all_to_all | solution.py:417
  28.3 1.5 %collective-permute-start.8 = (bf16[784,128]{1,0:T(8,128)(2,1)S(1)}, bf16[784,128]{1,0:T(8,128)(2,1)S(1)}, u32[]{:S(2)}, u32[]{:S(2)}) collective-permute-start(bf16[784,128]{1,0:T(8,128)(2,1)S(1)} %copy-done.2), channel_id=1, source_target_pairs={{0,1},{1,0},{2,3},{3,2},{4,5},{5,4},{6,7},{7,6},{8,9},{9,8},{10,11... | collective-permute-start | bytes 602120 | tf_op jit(solution)/shard_map/ppermute | solution.py:383
  28.7 1.5 %collective-permute-start.10 = (bf16[784,128]{1,0:T(8,128)(2,1)S(1)}, bf16[784,128]{1,0:T(8,128)(2,1)S(1)}, u32[]{:S(2)}, u32[]{:S(2)}) collective-permute-start(bf16[784,128]{1,0:T(8,128)(2,1)S(1)} %collective-permute-done.3.refs_2_), channel_id=1, source_target_pairs={{0,1},{1,0},{2,3},{3,2},{4,5},{5,4},{6,7},{7,6},{8,9},{9,8},{10,11... | collective-permute-start | bytes 602120 | tf_op jit(solution)/shard_map/ppermute | solution.py:383
  28.8 1.6 %collective-permute-start.9 = (bf16[784,128]{1,0:T(8,128)(2,1)S(1)}, bf16[784,128]{1,0:T(8,128)(2,1)S(1)}, u32[]{:S(2)}, u32[]{:S(2)}) collective-permute-start(bf16[784,128]{1,0:T(8,128)(2,1)S(1)} %collective-permute-done.refs_1_), channel_id=1, source_target_pairs={{0,1},{1,0},{2,3},{3,2},{4,5},{5,4},{6,7},{7,6},{8,9},{9,8},{10,11... | collective-permute-start | bytes 602120 | tf_op jit(solution)/shard_map/ppermute | solution.py:383
  29.2 1.5 %collective-permute-start.11 = (bf16[784,128]{1,0:T(8,128)(2,1)S(1)}, bf16[784,128]{1,0:T(8,128)(2,1)S(1)}, u32[]{:S(2)}, u32[]{:S(2)}) collective-permute-start(bf16[784,128]{1,0:T(8,128)(2,1)S(1)} %collective-permute-done.1.refs_3_), channel_id=1, source_target_pairs={{0,1},{1,0},{2,3},{3,2},{4,5},{5,4},{6,7},{7,6},{8,9},{9,8},{10,11... | collective-permute-start | bytes 602120 | tf_op jit(solution)/shard_map/ppermute | solution.py:383
  29.4 5.1 %collective-permute-start.12 = (bf16[784,128]{1,0:T(8,128)(2,1)S(1)}, bf16[784,128]{1,0:T(8,128)(2,1)S(1)}, u32[]{:S(2)}, u32[]{:S(2)}) collective-permute-start(bf16[784,128]{1,0:T(8,128)(2,1)S(1)} %collective-permute-done.4.refs_4_), channel_id=1, source_target_pairs={{0,1},{1,0},{2,3},{3,2},{4,5},{5,4},{6,7},{7,6},{8,9},{9,8},{10,11... | collective-permute-start | bytes 602120 | tf_op jit(solution)/shard_map/ppermute | solution.py:383
  29.8 4.8 %copy-start.10 = (bf16[784,128]{1,0:T(8,128)(2,1)}, bf16[784,128]{1,0:T(8,128)(2,1)S(1)}, u32[]{:S(2)}) copy-start(bf16[784,128]{1,0:T(8,128)(2,1)S(1)} %collective-permute-done.8.refs_7_) | copy-start | bytes 602116
  29.8 4.7 %collective-permute-start.15 = (bf16[784,128]{1,0:T(8,128)(2,1)S(1)}, bf16[784,128]{1,0:T(8,128)(2,1)S(1)}, u32[]{:S(2)}, u32[]{:S(2)}) collective-permute-start(bf16[784,128]{1,0:T(8,128)(2,1)S(1)} %collective-permute-done.6.refs_14_), channel_id=1, source_target_pairs={{0,1},{1,0},{2,3},{3,2},{4,5},{5,4},{6,7},{7,6},{8,9},{9,8},{10,11... | collective-permute-start | bytes 602120 | tf_op jit(solution)/shard_map/ppermute | solution.py:383
  30.2 4.4 %copy-start.11 = (bf16[784,128]{1,0:T(8,128)(2,1)}, bf16[784,128]{1,0:T(8,128)(2,1)S(1)}, u32[]{:S(2)}) copy-start(bf16[784,128]{1,0:T(8,128)(2,1)S(1)} %collective-permute-done.10.refs_9_) | copy-start | bytes 602116
  30.2 4.3 %collective-permute-start.13 = (bf16[784,128]{1,0:T(8,128)(2,1)S(1)}, bf16[784,128]{1,0:T(8,128)(2,1)S(1)}, u32[]{:S(2)}, u32[]{:S(2)}) collective-permute-start(bf16[784,128]{1,0:T(8,128)(2,1)S(1)} %collective-permute-done.2.refs_5_), channel_id=1, source_target_pairs={{0,1},{1,0},{2,3},{3,2},{4,5},{5,4},{6,7},{7,6},{8,9},{9,8},{10,11... | collective-permute-start | bytes 602120 | tf_op jit(solution)/shard_map/ppermute | solution.py:383
  30.5 4.1 %copy-start.12 = (bf16[784,128]{1,0:T(8,128)(2,1)}, bf16[784,128]{1,0:T(8,128)(2,1)S(1)}, u32[]{:S(2)}) copy-start(bf16[784,128]{1,0:T(8,128)(2,1)S(1)} %collective-permute-done.9.refs_8_) | copy-start | bytes 602116
  30.5 4.1 %collective-permute-start.14 = (bf16[784,128]{1,0:T(8,128)(2,1)S(1)}, bf16[784,128]{1,0:T(8,128)(2,1)S(1)}, u32[]{:S(2)}, u32[]{:S(2)}) collective-permute-start(bf16[784,128]{1,0:T(8,128)(2,1)S(1)} %collective-permute-done.5.refs_6_), channel_id=1, source_target_pairs={{0,1},{1,0},{2,3},{3,2},{4,5},{5,4},{6,7},{7,6},{8,9},{9,8},{10,11... | collective-permute-start | bytes 602120 | tf_op jit(solution)/shard_map/ppermute | solution.py:383
  30.8 3.9 %copy-start.13 = (bf16[784,128]{1,0:T(8,128)(2,1)}, bf16[784,128]{1,0:T(8,128)(2,1)S(1)}, u32[]{:S(2)}) copy-start(bf16[784,128]{1,0:T(8,128)(2,1)S(1)} %collective-permute-done.11.refs_10_) | copy-start | bytes 602116
  30.8 12.5 %collective-permute-start.7 = (bf16[784,128]{1,0:T(8,128)(2,1)S(1)}, bf16[784,128]{1,0:T(8,128)(2,1)S(1)}, u32[]{:S(2)}, u32[]{:S(2)}) collective-permute-start(bf16[784,128]{1,0:T(8,128)(2,1)S(1)} %broadcast_select_fusion.1), channel_id=1, source_target_pairs={{2,0},{3,1},{0,2},{1,3},{12,14},{13,15},{14,12},{15,13},{18,16},{1... | collective-permute-start | bytes 602120 | tf_op jit(solution)/shard_map/ppermute | solution.py:377
  34.5 0.7 copy-start.14
  34.5 0.7 %copy-start.15 = (bf16[784,128]{1,0:T(8,128)(2,1)}, bf16[784,128]{1,0:T(8,128)(2,1)S(1)}, u32[]{:S(2)}) copy-start(bf16[784,128]{1,0:T(8,128)(2,1)S(1)} %collective-permute-done.15.refs_15_) | copy-start | bytes 602116
  34.5 0.8 %copy-start.16 = (bf16[784,128]{1,0:T(8,128)(2,1)}, bf16[784,128]{1,0:T(8,128)(2,1)S(1)}, u32[]{:S(2)}) copy-start(bf16[784,128]{1,0:T(8,128)(2,1)S(1)} %collective-permute-done.13.refs_12_) | copy-start | bytes 602116
  34.6 0.8 %copy-start.17 = (bf16[784,128]{1,0:T(8,128)(2,1)}, bf16[784,128]{1,0:T(8,128)(2,1)S(1)}, u32[]{:S(2)}) copy-start(bf16[784,128]{1,0:T(8,128)(2,1)S(1)} %collective-permute-done.14.refs_13_) | copy-start | bytes 602116
  43.3 1.5 %collective-permute-start.16 = (bf16[784,128]{1,0:T(8,128)(2,1)S(1)}, bf16[784,128]{1,0:T(8,128)(2,1)S(1)}, u32[]{:S(2)}, u32[]{:S(2)}) collective-permute-start(bf16[784,128]{1,0:T(8,128)(2,1)S(1)} %collective-permute-done.7), channel_id=1, source_target_pairs={{0,1},{1,0},{2,3},{3,2},{4,5},{5,4},{6,7},{7,6},{8,9},{9,8},{10,11... | collective-permute-start | bytes 602120 | tf_op jit(solution)/shard_map/ppermute | solution.py:383
  44.9 24.6 %copy-start = (s32[16,1]{0,1:T(1,128)S(1)}, s32[16,1]{0,1:T(1,128)}, u32[]{:S(2)}) copy-start(s32[16,1]{0,1:T(1,128)} %param.17) | copy-start | bytes 196

commit v8 on v7

--- a/solution.py
+++ b/solution.py
@@ -171,7 +171,7 @@
     late = pl.ds(prompt, room)
     leaving = []
     for n, block in enumerate(blocks):
-        if n == len(blocks) // 2:
+        if n == len(blocks) * 3 // 4:
             for copy in wide:
                 copy.wait()
             leaving += [

time: 71.3 us -> 71.3 us (level)
  no operation moved by 1% of the time
where the time goes in v8:
time: 71.3 us; the launch traced here: 71 us
  Pallas kernels  19.4 us (27%)
  blocking collectives  19 us (27%)
  starting transfers between devices  18.9 us (27%)
  waiting for transfers between devices  12.5 us (18%)
  local copies, waits for them, and re-layouts  0.82 us (1%)
    all_to_all x1, blocking collectives, body(): lax.all_to_all(outputs, 'branch', split_axis=0, concat_axis=0, tiled=True)  19 us
    ppermute x8, starting transfers between devices, hop(): return lax.ppermute(x, 'branch', pairs)  11.5 us
    ppermute x8, waiting for transfers between devices, hop(): return lax.ppermute(x, 'branch', pairs)  10.9 us
    pallas_call x1, Pallas kernels, body(): pl.pallas_call(functools.partial(gather_kernel, whole, branches, len(shor...  7.85 us
    pallas_call x1, Pallas kernels, body(): pl.pallas_call(functools.partial(attend_kernel, split), out_shape=bf16(br...  5.54 us
    all_to_all x1, starting transfers between devices, body(): lax.all_to_all(send, 'branch', split_axis=0, concat_axis=0, tiled=True)  4.93 us
    pallas_call x1, Pallas kernels, body(): pl.pallas_call(prep_kernel, out_shape=bf16(branches, slot_rows, HD), in_s...  2.79 us
    ppermute x9, starting transfers between devices, across(): return lax.ppermute(x, 'branch', [(i, i ^ 1) for i in range(branches)])  2.5 us
  transfers between devices with their start and end apart: 18, of which 6 were waited for; matrix products, arithmetic and copies ran while one was open for 0% of the time, Pallas kernels for 15%

profile of v8, /device:TPU:0, one launch (start us, length us, event | category | flops | bytes accessed | tf_op | source)
XLA Modules:
  0.0 71.0 jit_solution(11583308500650184290)
XLA Ops:
  0.0 1.7 %payload.1.after_hbm.refs_0_ = bf16[784,128]{1,0:T(8,128)(2,1)} custom-call(s32[1,16]{1,0:T(1,128)} %pick_hbm.1, s32[1,2]{1,0:T(1,128)} %bitcast.5, bf16[2,24,2048]{2,1,0:T(8,128)(2,1)} %shared_hbm.1), custom_call_target="tpu_custom_call" | custom-call | tf_op jit(solution)/shard_map/payload/pallas_call | solution.py:358
  1.7 0.0 copy-start.2
  1.7 3.1 %collective-permute-start = (bf16[784,128]{1,0:T(8,128)(2,1)}, bf16[784,128]{1,0:T(8,128)(2,1)S(1)}, u32[]{:S(2)}, u32[]{:S(2)}) collective-permute-start(bf16[784,128]{1,0:T(8,128)(2,1)} %payload.1.after_hbm.refs_0_), channel_id=1, source_target_pairs={{0,4},{1,5},{4,8},{5,9},{8,12},{9,13},{12,14},{13,15},{14,10},{15,... | collective-permute-start | bytes 602120 | tf_op jit(solution)/shard_map/ppermute | solution.py:377
  4.8 0.0 collective-permute-start.3
  4.8 2.8 %prep.1 = bf16[16,160,128]{2,1,0:T(8,128)(2,1)} custom-call(s32[16]{0:T(128)} %bitcast.3, bf16[16,8192]{1,0:T(8,128)(2,1)} %q_hbm.1, bf16[16,2048]{1,0:T(8,128)(2,1)} %kv_hbm.1, bf16[784,128]{1,0:T(8,128)(2,1)} %payload.1.after_hbm.refs_0_), custom_call_target="tpu_custom_call" | custom-call | bytes 1024 | tf_op jit(solution)/shard_map/prep/pallas_call | solution.py:385
  7.6 2.3 %collective-permute-done.refs_1_ = bf16[784,128]{1,0:T(8,128)(2,1)S(1)} collective-permute-done((bf16[784,128]{1,0:T(8,128)(2,1)}, bf16[784,128]{1,0:T(8,128)(2,1)S(1)}, u32[]{:S(2)}, u32[]{:S(2)}) %collective-permute-start) | collective-permute-done | bytes 200736 | tf_op jit(solution)/shard_map/ppermute | solution.py:377
  10.0 1.8 %collective-permute-start.1 = (bf16[784,128]{1,0:T(8,128)(2,1)S(1)}, bf16[784,128]{1,0:T(8,128)(2,1)S(1)}, u32[]{:S(2)}, u32[]{:S(2)}) collective-permute-start(bf16[784,128]{1,0:T(8,128)(2,1)S(1)} %collective-permute-done.refs_1_), channel_id=1, source_target_pairs={{0,4},{1,5},{4,8},{5,9},{8,12},{9,13},{12,14},{13,15},{14,10},{15,... | collective-permute-start | bytes 602120 | tf_op jit(solution)/shard_map/ppermute | solution.py:377
  11.7 0.0 collective-permute-done.3.refs_2_
  11.7 0.2 collective-permute-start.4
  12.0 0.7 collective-permute-start.6
  12.7 3.4 %collective-permute-done.1.refs_3_ = bf16[784,128]{1,0:T(8,128)(2,1)S(1)} collective-permute-done((bf16[784,128]{1,0:T(8,128)(2,1)S(1)}, bf16[784,128]{1,0:T(8,128)(2,1)S(1)}, u32[]{:S(2)}, u32[]{:S(2)}) %collective-permute-start.1) | collective-permute-done | bytes 200736 | tf_op jit(solution)/shard_map/ppermute | solution.py:377
  16.1 1.5 %collective-permute-start.2 = (bf16[784,128]{1,0:T(8,128)(2,1)S(1)}, bf16[784,128]{1,0:T(8,128)(2,1)S(1)}, u32[]{:S(2)}, u32[]{:S(2)}) collective-permute-start(bf16[784,128]{1,0:T(8,128)(2,1)S(1)} %collective-permute-done.1.refs_3_), channel_id=1, source_target_pairs={{0,4},{1,5},{4,8},{5,9},{8,12},{9,13},{12,14},{13,15},{14,10},{15,... | collective-permute-start | bytes 602120 | tf_op jit(solution)/shard_map/ppermute | solution.py:377
  17.6 0.0 collective-permute-done.4.refs_4_
  17.6 0.6 collective-permute-start.5
  18.2 0.0 collective-permute-done.6.refs_14_
  18.2 3.7 %collective-permute-done.2.refs_5_ = bf16[784,128]{1,0:T(8,128)(2,1)S(1)} collective-permute-done((bf16[784,128]{1,0:T(8,128)(2,1)S(1)}, bf16[784,128]{1,0:T(8,128)(2,1)S(1)}, u32[]{:S(2)}, u32[]{:S(2)}) %collective-permute-start.2) | collective-permute-done | bytes 200736 | tf_op jit(solution)/shard_map/ppermute | solution.py:377
  21.8 1.5 %collective-permute-done.5.refs_6_ = bf16[784,128]{1,0:T(8,128)(2,1)S(1)} collective-permute-done((bf16[784,128]{1,0:T(8,128)(2,1)S(1)}, bf16[784,128]{1,0:T(8,128)(2,1)S(1)}, u32[]{:S(2)}, u32[]{:S(2)}) %collective-permute-start.5) | collective-permute-done | bytes 200736 | tf_op jit(solution)/shard_map/ppermute | solution.py:377
  23.3 4.9 %all-to-all-start = ((bf16[16,160,128]{2,1,0:T(8,128)(2,1)}), bf16[16,160,128]{2,1,0:T(8,128)(2,1)S(1)}, u32[]{:S(2)}, u32[]{:S(2)}) async-start(bf16[16,160,128]{2,1,0:T(8,128)(2,1)} %prep.1), calls=%async_computation | async-start | bytes 1310720 | tf_op jit(solution)/shard_map/all_to_all | solution.py:417
  28.3 0.5 collective-permute-start.8
  28.7 0.1 collective-permute-start.10
  28.8 0.4 collective-permute-start.9
  29.2 0.1 collective-permute-start.11
  29.4 0.4 collective-permute-start.12
  29.8 0.1 collective-permute-done.8.refs_7_
  29.8 0.4 collective-permute-start.15
  30.2 0.0 collective-permute-done.10.refs_9_
  30.2 0.3 collective-permute-start.13
  30.5 0.0 collective-permute-done.9.refs_8_
  30.5 0.3 collective-permute-start.14
  30.8 0.0 collective-permute-done.11.refs_10_
  30.8 0.0 copy-start.13
  30.8 3.7 %collective-permute-start.7 = (bf16[784,128]{1,0:T(8,128)(2,1)S(1)}, bf16[784,128]{1,0:T(8,128)(2,1)S(1)}, u32[]{:S(2)}, u32[]{:S(2)}) collective-permute-start(bf16[784,128]{1,0:T(8,128)(2,1)S(1)} %broadcast_select_fusion.1), channel_id=1, source_target_pairs={{2,0},{3,1},{0,2},{1,3},{12,14},{13,15},{14,12},{15,13},{18,16},{1... | collective-permute-start | bytes 602120 | tf_op jit(solution)/shard_map/ppermute | solution.py:377
  34.5 0.0 collective-permute-done.12.refs_11_
  34.5 0.0 collective-permute-done.15.refs_15_
  34.5 0.0 collective-permute-done.13.refs_12_
  34.5 0.0 collective-permute-done.14.refs_13_
  34.7 0.5 copy-done.14
  35.2 0.1 copy-done.15
  35.2 0.1 copy-done.16
  35.3 0.1 copy-done.17
  35.4 7.9 %gather.1 = (bf16[3,1312,128]{2,1,0:T(8,128)(2,1)S(1)}, bf16[3,1312,128]{2,1,0:T(8,128)(2,1)S(1)}, f32[1,1312]{1,0:T(1,128)S(1)}, bf16[5,1312,128]{2,1,0:T(8,128)(2,1)}, bf16[5,1312,128]{2,1,0:T(8,128)(2,1)}) custom-call(s32[1]{0:T(128)} %bitcast.1.me_ref, s32[1,8]{1,0:T(1,128)S(1)} %copy-done.1, bf16[1,1024,1024]{2,1,0:T(8,128)(2,1)} %pk_hbm.1, ...), custom_call_target="tpu_custom_call" | custom-call | bytes 8388608 | tf_op jit(solution)/shard_map/gather/pallas_call | solution.py:435
  43.3 0.0 collective-permute-done.7
  43.3 0.1 collective-permute-start.16
  43.4 1.4 %collective-permute-done.16 = bf16[784,128]{1,0:T(8,128)(2,1)S(1)} collective-permute-done((bf16[784,128]{1,0:T(8,128)(2,1)S(1)}, bf16[784,128]{1,0:T(8,128)(2,1)S(1)}, u32[]{:S(2)}, u32[]{:S(2)}) %collective-permute-start.16) | collective-permute-done | bytes 200736 | tf_op jit(solution)/shard_map/ppermute | solution.py:383
  44.8 0.0 all-to-all-done.recv_ref
  44.9 5.5 %attend.1 = bf16[16,128,128]{2,1,0:T(8,128)(2,1)S(1)} custom-call(s32[1]{0:T(128)} %bitcast.1.me_ref, bf16[3,1312,128]{2,1,0:T(8,128)(2,1)S(1)} %get-tuple-element.26.near_key, bf16[3,1312,128]{2,1,0:T(8,128)(2,1)S(1)} %get-tuple-element.27.near_value, f32[1,1312]{1,0:T(1,128)S(1)} %get-tuple-element.28.bias_ref, ...), custom_call_target="tpu_custom_call" | custom-call | flops 1409286144 | bytes 4194304 | tf_op jit(solution)/shard_map/attend/pallas_call | solution.py:462
  50.4 19.0 %all_to_all.10.back_ref = bf16[16,128,128]{2,1,0:T(8,128)(2,1)S(1)} all-to-all(bf16[16,128,128]{2,1,0:T(8,128)(2,1)S(1)} %attend.1), channel_id=1, replica_groups=mesh['groups'=2,'branch'=16] {'branch'}, dimensions={0} | all-to-all | bytes 1048576 | tf_op jit(solution)/shard_map/all_to_all | solution.py:484
  69.5 1.5 %post.1 = bf16[16,8192]{1,0:T(8,128)(2,1)} custom-call(s32[16]{0:T(128)S(1)} %bitcast.4, bf16[16,128,128]{2,1,0:T(8,128)(2,1)S(1)} %all_to_all.10.back_ref), custom_call_target="tpu_custom_call" | custom-call | tf_op jit(solution)/shard_map/post/pallas_call | solution.py:485
  (36 shorter events, 0.2 us)
Async XLA Ops:
  0.0 35.4 %copy-start.1 = (s32[1,8]{1,0:T(1,128)S(1)}, s32[1,8]{1,0:T(1,128)}, u32[]{:S(2)}) copy-start(s32[1,8]{1,0:T(1,128)} %mask_ref.1) | copy-start | bytes 100
  1.7 26.5 %copy-start.2 = (bf16[784,128]{1,0:T(8,128)(2,1)S(1)}, bf16[784,128]{1,0:T(8,128)(2,1)}, u32[]{:S(2)}) copy-start(bf16[784,128]{1,0:T(8,128)(2,1)} %payload.1.after_hbm.refs_0_) | copy-start | bytes 602116
  1.7 8.2 %collective-permute-start = (bf16[784,128]{1,0:T(8,128)(2,1)}, bf16[784,128]{1,0:T(8,128)(2,1)S(1)}, u32[]{:S(2)}, u32[]{:S(2)}) collective-permute-start(bf16[784,128]{1,0:T(8,128)(2,1)} %payload.1.after_hbm.refs_0_), channel_id=1, source_target_pairs={{0,4},{1,5},{4,8},{5,9},{8,12},{9,13},{12,14},{13,15},{14,10},{15,... | collective-permute-start | bytes 602120 | tf_op jit(solution)/shard_map/ppermute | solution.py:377
  4.8 6.9 %collective-permute-start.3 = (bf16[784,128]{1,0:T(8,128)(2,1)}, bf16[784,128]{1,0:T(8,128)(2,1)S(1)}, u32[]{:S(2)}, u32[]{:S(2)}) collective-permute-start(bf16[784,128]{1,0:T(8,128)(2,1)} %payload.1.after_hbm.refs_0_), channel_id=1, source_target_pairs={{0,2},{1,3},{4,0},{5,1},{8,4},{9,5},{12,8},{13,9},{14,12},{15,13},... | collective-permute-start | bytes 602120 | tf_op jit(solution)/shard_map/ppermute | solution.py:377
  9.9 24.7 %copy-start.3 = (bf16[784,128]{1,0:T(8,128)(2,1)}, bf16[784,128]{1,0:T(8,128)(2,1)S(1)}, u32[]{:S(2)}) copy-start(bf16[784,128]{1,0:T(8,128)(2,1)S(1)} %collective-permute-done.refs_1_) | copy-start | bytes 602116
  10.0 6.2 %collective-permute-start.1 = (bf16[784,128]{1,0:T(8,128)(2,1)S(1)}, bf16[784,128]{1,0:T(8,128)(2,1)S(1)}, u32[]{:S(2)}, u32[]{:S(2)}) collective-permute-start(bf16[784,128]{1,0:T(8,128)(2,1)S(1)} %collective-permute-done.refs_1_), channel_id=1, source_target_pairs={{0,4},{1,5},{4,8},{5,9},{8,12},{9,13},{12,14},{13,15},{14,10},{15,... | collective-permute-start | bytes 602120 | tf_op jit(solution)/shard_map/ppermute | solution.py:377
  11.7 22.9 %copy-start.4 = (bf16[784,128]{1,0:T(8,128)(2,1)}, bf16[784,128]{1,0:T(8,128)(2,1)S(1)}, u32[]{:S(2)}) copy-start(bf16[784,128]{1,0:T(8,128)(2,1)S(1)} %collective-permute-done.3.refs_2_) | copy-start | bytes 602116
  11.7 5.9 %collective-permute-start.4 = (bf16[784,128]{1,0:T(8,128)(2,1)S(1)}, bf16[784,128]{1,0:T(8,128)(2,1)S(1)}, u32[]{:S(2)}, u32[]{:S(2)}) collective-permute-start(bf16[784,128]{1,0:T(8,128)(2,1)S(1)} %collective-permute-done.3.refs_2_), channel_id=1, source_target_pairs={{0,2},{1,3},{4,0},{5,1},{8,4},{9,5},{12,8},{13,9},{14,12},{15,13},... | collective-permute-start | bytes 602120 | tf_op jit(solution)/shard_map/ppermute | solution.py:377
  12.0 6.1 %collective-permute-start.6 = (bf16[784,128]{1,0:T(8,128)(2,1)S(1)}, bf16[784,128]{1,0:T(8,128)(2,1)S(1)}, u32[]{:S(2)}, u32[]{:S(2)}) collective-permute-start(bf16[784,128]{1,0:T(8,128)(2,1)S(1)} %broadcast_select_fusion), channel_id=1, source_target_pairs={{4,6},{5,7},{6,4},{7,5},{8,10},{9,11},{10,8},{11,9},{20,22},{21,23... | collective-permute-start | bytes 602120 | tf_op jit(solution)/shard_map/ppermute | solution.py:377
  16.1 18.4 %copy-start.7 = (bf16[784,128]{1,0:T(8,128)(2,1)}, bf16[784,128]{1,0:T(8,128)(2,1)S(1)}, u32[]{:S(2)}) copy-start(bf16[784,128]{1,0:T(8,128)(2,1)S(1)} %collective-permute-done.1.refs_3_) | copy-start | bytes 602116
  16.1 5.7 %collective-permute-start.2 = (bf16[784,128]{1,0:T(8,128)(2,1)S(1)}, bf16[784,128]{1,0:T(8,128)(2,1)S(1)}, u32[]{:S(2)}, u32[]{:S(2)}) collective-permute-start(bf16[784,128]{1,0:T(8,128)(2,1)S(1)} %collective-permute-done.1.refs_3_), channel_id=1, source_target_pairs={{0,4},{1,5},{4,8},{5,9},{8,12},{9,13},{12,14},{13,15},{14,10},{15,... | collective-permute-start | bytes 602120 | tf_op jit(solution)/shard_map/ppermute | solution.py:377
  17.6 17.0 %copy-start.8 = (bf16[784,128]{1,0:T(8,128)(2,1)}, bf16[784,128]{1,0:T(8,128)(2,1)S(1)}, u32[]{:S(2)}) copy-start(bf16[784,128]{1,0:T(8,128)(2,1)S(1)} %collective-permute-done.4.refs_4_) | copy-start | bytes 602116
  17.6 5.7 %collective-permute-start.5 = (bf16[784,128]{1,0:T(8,128)(2,1)S(1)}, bf16[784,128]{1,0:T(8,128)(2,1)S(1)}, u32[]{:S(2)}, u32[]{:S(2)}) collective-permute-start(bf16[784,128]{1,0:T(8,128)(2,1)S(1)} %collective-permute-done.4.refs_4_), channel_id=1, source_target_pairs={{0,2},{1,3},{4,0},{5,1},{8,4},{9,5},{12,8},{13,9},{14,12},{15,13},... | collective-permute-start | bytes 602120 | tf_op jit(solution)/shard_map/ppermute | solution.py:377
  18.2 16.4 %copy-start.9 = (bf16[784,128]{1,0:T(8,128)(2,1)}, bf16[784,128]{1,0:T(8,128)(2,1)S(1)}, u32[]{:S(2)}) copy-start(bf16[784,128]{1,0:T(8,128)(2,1)S(1)} %collective-permute-done.6.refs_14_) | copy-start | bytes 602116
  21.8 12.8 %copy-start.5 = (bf16[784,128]{1,0:T(8,128)(2,1)}, bf16[784,128]{1,0:T(8,128)(2,1)S(1)}, u32[]{:S(2)}) copy-start(bf16[784,128]{1,0:T(8,128)(2,1)S(1)} %collective-permute-done.2.refs_5_) | copy-start | bytes 602116
  23.3 11.3 %copy-start.6 = (bf16[784,128]{1,0:T(8,128)(2,1)}, bf16[784,128]{1,0:T(8,128)(2,1)S(1)}, u32[]{:S(2)}) copy-start(bf16[784,128]{1,0:T(8,128)(2,1)S(1)} %collective-permute-done.5.refs_6_) | copy-start | bytes 602116
  23.3 21.5 %all-to-all-start = ((bf16[16,160,128]{2,1,0:T(8,128)(2,1)}), bf16[16,160,128]{2,1,0:T(8,128)(2,1)S(1)}, u32[]{:S(2)}, u32[]{:S(2)}) async-start(bf16[16,160,128]{2,1,0:T(8,128)(2,1)} %prep.1), calls=%async_computation | async-start | bytes 1310720 | tf_op jit(solution)/shard_map/all_to_all | solution.py:417
  28.3 1.5 %collective-permute-start.8 = (bf16[784,128]{1,0:T(8,128)(2,1)S(1)}, bf16[784,128]{1,0:T(8,128)(2,1)S(1)}, u32[]{:S(2)}, u32[]{:S(2)}) collective-permute-start(bf16[784,128]{1,0:T(8,128)(2,1)S(1)} %copy-done.2), channel_id=1, source_target_pairs={{0,1},{1,0},{2,3},{3,2},{4,5},{5,4},{6,7},{7,6},{8,9},{9,8},{10,11... | collective-permute-start | bytes 602120 | tf_op jit(solution)/shard_map/ppermute | solution.py:383
  28.7 1.5 %collective-permute-start.10 = (bf16[784,128]{1,0:T(8,128)(2,1)S(1)}, bf16[784,128]{1,0:T(8,128)(2,1)S(1)}, u32[]{:S(2)}, u32[]{:S(2)}) collective-permute-start(bf16[784,128]{1,0:T(8,128)(2,1)S(1)} %collective-permute-done.3.refs_2_), channel_id=1, source_target_pairs={{0,1},{1,0},{2,3},{3,2},{4,5},{5,4},{6,7},{7,6},{8,9},{9,8},{10,11... | collective-permute-start | bytes 602120 | tf_op jit(solution)/shard_map/ppermute | solution.py:383
  28.8 1.6 %collective-permute-start.9 = (bf16[784,128]{1,0:T(8,128)(2,1)S(1)}, bf16[784,128]{1,0:T(8,128)(2,1)S(1)}, u32[]{:S(2)}, u32[]{:S(2)}) collective-permute-start(bf16[784,128]{1,0:T(8,128)(2,1)S(1)} %collective-permute-done.refs_1_), channel_id=1, source_target_pairs={{0,1},{1,0},{2,3},{3,2},{4,5},{5,4},{6,7},{7,6},{8,9},{9,8},{10,11... | collective-permute-start | bytes 602120 | tf_op jit(solution)/shard_map/ppermute | solution.py:383
  29.2 1.5 %collective-permute-start.11 = (bf16[784,128]{1,0:T(8,128)(2,1)S(1)}, bf16[784,128]{1,0:T(8,128)(2,1)S(1)}, u32[]{:S(2)}, u32[]{:S(2)}) collective-permute-start(bf16[784,128]{1,0:T(8,128)(2,1)S(1)} %collective-permute-done.1.refs_3_), channel_id=1, source_target_pairs={{0,1},{1,0},{2,3},{3,2},{4,5},{5,4},{6,7},{7,6},{8,9},{9,8},{10,11... | collective-permute-start | bytes 602120 | tf_op jit(solution)/shard_map/ppermute | solution.py:383
  29.4 5.1 %collective-permute-start.12 = (bf16[784,128]{1,0:T(8,128)(2,1)S(1)}, bf16[784,128]{1,0:T(8,128)(2,1)S(1)}, u32[]{:S(2)}, u32[]{:S(2)}) collective-permute-start(bf16[784,128]{1,0:T(8,128)(2,1)S(1)} %collective-permute-done.4.refs_4_), channel_id=1, source_target_pairs={{0,1},{1,0},{2,3},{3,2},{4,5},{5,4},{6,7},{7,6},{8,9},{9,8},{10,11... | collective-permute-start | bytes 602120 | tf_op jit(solution)/shard_map/ppermute | solution.py:383
  29.8 4.8 %copy-start.10 = (bf16[784,128]{1,0:T(8,128)(2,1)}, bf16[784,128]{1,0:T(8,128)(2,1)S(1)}, u32[]{:S(2)}) copy-start(bf16[784,128]{1,0:T(8,128)(2,1)S(1)} %collective-permute-done.8.refs_7_) | copy-start | bytes 602116
  29.8 4.7 %collective-permute-start.15 = (bf16[784,128]{1,0:T(8,128)(2,1)S(1)}, bf16[784,128]{1,0:T(8,128)(2,1)S(1)}, u32[]{:S(2)}, u32[]{:S(2)}) collective-permute-start(bf16[784,128]{1,0:T(8,128)(2,1)S(1)} %collective-permute-done.6.refs_14_), channel_id=1, source_target_pairs={{0,1},{1,0},{2,3},{3,2},{4,5},{5,4},{6,7},{7,6},{8,9},{9,8},{10,11... | collective-permute-start | bytes 602120 | tf_op jit(solution)/shard_map/ppermute | solution.py:383
  30.2 4.4 %copy-start.11 = (bf16[784,128]{1,0:T(8,128)(2,1)}, bf16[784,128]{1,0:T(8,128)(2,1)S(1)}, u32[]{:S(2)}) copy-start(bf16[784,128]{1,0:T(8,128)(2,1)S(1)} %collective-permute-done.10.refs_9_) | copy-start | bytes 602116
  30.2 4.3 %collective-permute-start.13 = (bf16[784,128]{1,0:T(8,128)(2,1)S(1)}, bf16[784,128]{1,0:T(8,128)(2,1)S(1)}, u32[]{:S(2)}, u32[]{:S(2)}) collective-permute-start(bf16[784,128]{1,0:T(8,128)(2,1)S(1)} %collective-permute-done.2.refs_5_), channel_id=1, source_target_pairs={{0,1},{1,0},{2,3},{3,2},{4,5},{5,4},{6,7},{7,6},{8,9},{9,8},{10,11... | collective-permute-start | bytes 602120 | tf_op jit(solution)/shard_map/ppermute | solution.py:383
  30.5 4.1 %copy-start.12 = (bf16[784,128]{1,0:T(8,128)(2,1)}, bf16[784,128]{1,0:T(8,128)(2,1)S(1)}, u32[]{:S(2)}) copy-start(bf16[784,128]{1,0:T(8,128)(2,1)S(1)} %collective-permute-done.9.refs_8_) | copy-start | bytes 602116
  30.5 4.1 %collective-permute-start.14 = (bf16[784,128]{1,0:T(8,128)(2,1)S(1)}, bf16[784,128]{1,0:T(8,128)(2,1)S(1)}, u32[]{:S(2)}, u32[]{:S(2)}) collective-permute-start(bf16[784,128]{1,0:T(8,128)(2,1)S(1)} %collective-permute-done.5.refs_6_), channel_id=1, source_target_pairs={{0,1},{1,0},{2,3},{3,2},{4,5},{5,4},{6,7},{7,6},{8,9},{9,8},{10,11... | collective-permute-start | bytes 602120 | tf_op jit(solution)/shard_map/ppermute | solution.py:383
  30.8 3.9 %copy-start.13 = (bf16[784,128]{1,0:T(8,128)(2,1)}, bf16[784,128]{1,0:T(8,128)(2,1)S(1)}, u32[]{:S(2)}) copy-start(bf16[784,128]{1,0:T(8,128)(2,1)S(1)} %collective-permute-done.11.refs_10_) | copy-start | bytes 602116
  30.8 12.4 %collective-permute-start.7 = (bf16[784,128]{1,0:T(8,128)(2,1)S(1)}, bf16[784,128]{1,0:T(8,128)(2,1)S(1)}, u32[]{:S(2)}, u32[]{:S(2)}) collective-permute-start(bf16[784,128]{1,0:T(8,128)(2,1)S(1)} %broadcast_select_fusion.1), channel_id=1, source_target_pairs={{2,0},{3,1},{0,2},{1,3},{12,14},{13,15},{14,12},{15,13},{18,16},{1... | collective-permute-start | bytes 602120 | tf_op jit(solution)/shard_map/ppermute | solution.py:377
  34.5 0.7 copy-start.14
  34.5 0.7 %copy-start.15 = (bf16[784,128]{1,0:T(8,128)(2,1)}, bf16[784,128]{1,0:T(8,128)(2,1)S(1)}, u32[]{:S(2)}) copy-start(bf16[784,128]{1,0:T(8,128)(2,1)S(1)} %collective-permute-done.15.refs_15_) | copy-start | bytes 602116
  34.5 0.8 %copy-start.16 = (bf16[784,128]{1,0:T(8,128)(2,1)}, bf16[784,128]{1,0:T(8,128)(2,1)S(1)}, u32[]{:S(2)}) copy-start(bf16[784,128]{1,0:T(8,128)(2,1)S(1)} %collective-permute-done.13.refs_12_) | copy-start | bytes 602116
  34.6 0.8 %copy-start.17 = (bf16[784,128]{1,0:T(8,128)(2,1)}, bf16[784,128]{1,0:T(8,128)(2,1)S(1)}, u32[]{:S(2)}) copy-start(bf16[784,128]{1,0:T(8,128)(2,1)S(1)} %collective-permute-done.14.refs_13_) | copy-start | bytes 602116
  43.3 1.5 %collective-permute-start.16 = (bf16[784,128]{1,0:T(8,128)(2,1)S(1)}, bf16[784,128]{1,0:T(8,128)(2,1)S(1)}, u32[]{:S(2)}, u32[]{:S(2)}) collective-permute-start(bf16[784,128]{1,0:T(8,128)(2,1)S(1)} %collective-permute-done.7), channel_id=1, source_target_pairs={{0,1},{1,0},{2,3},{3,2},{4,5},{5,4},{6,7},{7,6},{8,9},{9,8},{10,11... | collective-permute-start | bytes 602120 | tf_op jit(solution)/shard_map/ppermute | solution.py:383
  44.9 24.6 %copy-start = (s32[16,1]{0,1:T(1,128)S(1)}, s32[16,1]{0,1:T(1,128)}, u32[]{:S(2)}) copy-start(s32[16,1]{0,1:T(1,128)} %param.17) | copy-start | bytes 196
